TPU v7x, 256 devices: a whole 4x4x8 slice. The times are simulated.
256 devices in a mesh: wide: 64 (over x_lo, z, y), narrow: 4 (over x_hi, core).
Axes of the slice: x: 4 (x_hi: 2, x_lo: 2; x = x_hi * 2 + x_lo), y: 4, z: 8, core: 2. Of those that a mesh axis runs over, the one named last changes fastest.
Arguments:
- samples: bfloat16 [1024, 396288], P(('narrow', 'wide')), may hold values from -6 to 6
- pfb_taps: float32 [4, 1024], replicated, may hold values from -3 to 3
Outputs:
- self_vis: float32 [2, 512, 1024, 256], P(None, 'wide', 'narrow')
- prior_vis: float32 [2, 512, 1024, 256], P(None, 'wide', 'narrow')
- far_vis: float32 [2, 512, 1024, 128], P(None, 'wide', 'narrow')
All inputs are finite; a program needn't handle non-finite values.
Results may differ from a plain program's by a relative error of at most 0.0065.
Values may be sent and summed in bfloat16 or wider, within the bound.
No kernel may reach another device: no remote copies, remote signals or barrier semaphores. Data moves between devices by JAX's collectives and lax.ppermute only.
A program may use at most 128 MiB of HBM per device.

v0:
```python
import math

import jax
import jax.numpy as jnp
from jax import lax
from jax.sharding import PartitionSpec as P


def dft_table(channels):
    positions = jnp.arange(2 * channels, dtype=jnp.int32)
    bins = jnp.arange(channels, dtype=jnp.int32)
    phases = bins[:, None] * positions[None, :] % (2 * channels)
    angles = phases.astype(jnp.float32) * (math.pi / channels)
    norming = (2.0 * channels) ** (-0.5)
    return jnp.stack([jnp.cos(angles) * norming, -jnp.sin(angles) * norming]).astype(jnp.bfloat16)


def polyphase(shaped, pfb_taps, spectra):
    total = jnp.zeros((shaped.shape[0], spectra, shaped.shape[2]), jnp.float32)
    for tap_index in range(pfb_taps.shape[0]):
        total = (
            total
            + shaped[:, tap_index : tap_index + spectra, :].astype(jnp.float32)
            * pfb_taps[tap_index]
        )
    return total.astype(jnp.bfloat16)


def cross_tile(row_block, col_block, spectra):
    turned = jnp.concatenate([row_block[..., spectra:], -row_block[..., :spectra]], axis=-1)
    stacked = jnp.concatenate([row_block, turned], axis=1)
    product = (
        jnp.einsum("cik,cjk->cij", stacked, col_block, preferred_element_type=jnp.float32) / spectra
    )
    width = row_block.shape[1]
    return jnp.stack([product[:, :width], product[:, width:]])


def on_device(samples, pfb_taps):
    channels = pfb_taps.shape[1] // 2
    tap_count = pfb_taps.shape[0]
    inputs_dev = samples.shape[0]
    frames = samples.shape[1] // (2 * channels)
    spectra = frames - tap_count + 1
    shaped = samples.reshape(inputs_dev, frames, 2 * channels)
    filtered = polyphase(shaped, pfb_taps, spectra)
    table = dft_table(channels)
    spectrum = jnp.einsum("pcn,isn->cips", table, filtered, preferred_element_type=jnp.float32)
    spectrum = spectrum.astype(jnp.bfloat16).reshape(channels, inputs_dev, 2 * spectra)
    local = lax.all_to_all(spectrum, "wide", split_axis=0, concat_axis=1, tiled=True)
    block_len = local.shape[1]
    halfway = block_len // 2
    position = lax.axis_index("narrow")
    group_size = lax.axis_size("narrow")
    whole = lax.all_gather(local, "narrow", axis=1, tiled=True)
    previous = lax.dynamic_slice_in_dim(
        whole, (position + group_size - 1) % group_size * block_len, block_len, 1
    )
    far_cols = lax.dynamic_slice_in_dim(
        whole, (position + 2) % group_size * block_len + position // 2 * halfway, halfway, 1
    )
    self_vis = cross_tile(local, local, spectra)
    prior_vis = cross_tile(local, previous, spectra)
    far_vis = cross_tile(local, far_cols, spectra)
    return (self_vis, prior_vis, far_vis)


def solution(mesh):
    return jax.shard_map(
        on_device,
        mesh=mesh,
        in_specs=(P(("narrow", "wide"), None), P()),
        out_specs=(
            P(None, "wide", "narrow", None),
            P(None, "wide", "narrow", None),
            P(None, "wide", "narrow", None),
        ),
        check_vma=False,
    )
```

profile of v0, /device:TPU:24, one launch (start us, length us, event | category | flops | bytes accessed | tf_op | source)
XLA Modules:
  0.0 231.9 jit_solution(10637659805752586051)
XLA Ops:
  7.2 0.0 all-gather.2.cloned.1.call-start
  7.2 9.3 %multiply_convert_fusion = (bf16[1,512,1024]{2,1,0:T(8,128)(2,1)}, bf16[1,512,1024]{2,1,0:T(8,128)(2,1)}) fusion(), kind=kLoop, calls=%fused_computation.34 | loop fusion | flops 9961472 | bytes 2097152 | tf_op jit(solution)/shard_map/convert.1
  16.5 0.9 fusion.35
  17.4 3.8 %reshape.93 = bf16[4,387,1024]{2,1,0:T(8,128)(2,1)S(1)} reshape(bf16[4,396288]{1,0:T(4,128)(2,1)} %param.2) | data formatting | bytes 6340608 | tf_op jit(solution)/shard_map/reshape | solution.py:45
  21.2 7.8 %fusion.13 = bf16[4,384,2,512]{3,1,2,0:T(8,128)(2,1)} fusion(bf16[4,387,1024]{2,1,0:T(8,128)(2,1)S(1)} %reshape.93, f32[1024]{0:T(1024)S(1)} %bitcast.39, f32[1024]{0:T(1024)S(1)} %bitcast.40, f32[1024]{0:T(1024)S(1)} %bitcast.38, f32[1024]{0:T(1024)S(1)} %bitcast.37, bf16[1,512,1024]{2,1,0:T(8,128)(2,1)} %get-tuple-element.15, ...), kind=kOutput, calls=%fused_computation.20 | convolution fusion | flops 3245867008 | bytes 17842176 | tf_op jit(solution)/shard_map/pcn,isn->cips/dot_general | solution.py:48
  29.0 4.7 %copy.8 = bf16[512,4,768]{2,1,0:T(4,128)(2,1)S(1)} copy(bf16[512,4,768]{0,2,1:T(8,128)(2,1)} %bitcast.36) | data formatting | bytes 6291456 | tf_op jit(solution)/shard_map/reshape | solution.py:49
  33.8 86.5 %all_to_all.18 = bf16[512,4,768]{2,1,0:T(4,128)(2,1)S(1)} all-to-all(bf16[512,4,768]{2,1,0:T(4,128)(2,1)S(1)} %copy.8), channel_id=1, replica_groups=mesh['wide'=64,'narrow'=4] {'wide'}, dimensions={0} | all-to-all | bytes 6291456 | tf_op jit(solution)/shard_map/all_to_all | solution.py:50
  120.2 0.4 copy.13
  120.6 2.4 %copy.10 = bf16[8,64,4,768]{3,2,1,0:T(4,128)(2,1)S(1)} copy(bf16[8,64,4,768]{3,0,1,2:T(8,128)(2,1)S(1)} %bitcast.35) | data formatting | bytes 6291456 | tf_op jit(solution)/shard_map/all_to_all | solution.py:50
  123.0 2.4 %all_to_all.16 = bf16[8,256,768]{2,1,0:T(8,128)(2,1)} reshape(bf16[8,64,4,768]{3,2,1,0:T(4,128)(2,1)S(1)} %copy.10) | data formatting | bytes 6291456 | tf_op jit(solution)/shard_map/all_to_all | solution.py:50
  125.5 1.8 copy-done
  127.3 0.3 fusion.34
  127.6 2.5 %convolution_multiply_fusion = f32[8,512,256]{2,1,0:T(8,128)S(1)} fusion(bf16[8,256,768]{2,1,0:T(8,128)(2,1)S(1)} %copy-done, bf16[8,256,384]{2,1,0:T(8,128)(2,1)S(1)} %get-tuple-element.8, bf16[8,256,384]{2,1,0:T(8,128)(2,1)S(1)} %get-tuple-element.7), kind=kOutput, calls=%fused_computation.21 | convolution fusion | flops 1630535680 | bytes 10485760 | tf_op jit(solution)/shard_map/cik,cjk->cij/dot_general | solution.py:33
  130.2 0.3 slice_bitcast_fusion.3
  130.5 2.4 %pad_maximum_fusion = f32[2,8,256,256]{3,2,1,0:T(8,128)} fusion(f32[1,8,256,256]{3,2,1,0:T(8,128)S(1)} %get-tuple-element.6, f32[1,8,256,256]{3,2,1,0:T(8,128)S(1)} %get-tuple-element.5), kind=kLoop, calls=%fused_computation.2 | loop fusion | flops 1048576 | bytes 8388608 | tf_op jit(solution)/shard_map/stack | solution.py:36
  132.9 77.8 %all-gather.2.cloned.1.call-done = bf16[8,1024,768]{2,1,0:T(8,128)(2,1)} async-done(((bf16[8,256,768]{2,1,0:T(8,128)(2,1)}), bf16[8,1024,768]{2,1,0:T(8,128)(2,1)}) %all-gather.2.cloned.1.call-update) | async-done | bytes 12582928 | tf_op jit(solution)/shard_map/all_gather | solution.py:55
  210.7 5.5 %fusion.16 = f32[8,512,256]{2,1,0:T(8,128)S(1)} fusion(bf16[8,1024,768]{2,1,0:T(8,128)(2,1)} %all-gather.2.cloned.1.call-done, s32[]{:T(128)S(6)} %select_n.42, bf16[8,256,384]{2,1,0:T(8,128)(2,1)} %copy-done.3, bf16[8,256,384]{2,1,0:T(8,128)(2,1)} %copy-done.1, bf16[8,256,768]{2,1,0:T(8,128)(2,1)S(1)} %copy-done), kind=kOutput, calls=%fused_computation.22 | convolution fusion | flops 1630535680 | bytes 13631492 | tf_op jit(solution)/shard_map/cik,cjk->cij/dot_general | solution.py:33
  216.2 0.5 slice_bitcast_fusion.1
  216.6 0.9 copy-done.2
  217.6 0.5 copy-done.4
  218.0 3.1 %convolution_multiply_fusion.1 = f32[8,512,128]{2,1,0:T(8,128)S(1)} fusion(bf16[8,1024,768]{2,1,0:T(8,128)(2,1)} %all-gather.2.cloned.1.call-done, s32[]{:T(128)S(6)} %select_n.45, bf16[8,256,384]{2,1,0:T(8,128)(2,1)S(1)} %copy-done.4, bf16[8,256,384]{2,1,0:T(8,128)(2,1)S(1)} %copy-done.2, bf16[8,256,768]{2,1,0:T(8,128)(2,1)S(1)} %copy-done), kind=kOutput, calls=%fused_computation.39 | convolution fusion | flops 824705024 | bytes 9961476 | tf_op jit(solution)/shard_map/cik,cjk->cij/dot_general | solution.py:33
  221.2 0.2 slice_bitcast_fusion.5
  221.3 2.3 pad_maximum_fusion.1
  223.6 1.5 pad_maximum_fusion.2
  (8 shorter events, 0.0 us)
Async XLA Ops:
  7.2 203.5 %all-gather.2.cloned.1.call-start = ((), (), s32[]{:S(2)}) async-start(), calls=%async_computation.1 | async-start | bytes 15728640 | tf_op jit(solution)/shard_map/all_gather | solution.py:55
  125.4 1.9 copy-start
  127.6 2.5 %copy-start.1 = (bf16[8,256,384]{2,1,0:T(8,128)(2,1)}, bf16[8,256,384]{2,1,0:T(8,128)(2,1)S(1)}, u32[]{:S(2)}) copy-start(bf16[8,256,384]{2,1,0:T(8,128)(2,1)S(1)} %get-tuple-element.7) | copy-start | bytes 4718596
  127.6 2.5 %copy-start.3 = (bf16[8,256,384]{2,1,0:T(8,128)(2,1)}, bf16[8,256,384]{2,1,0:T(8,128)(2,1)S(1)}, u32[]{:S(2)}) copy-start(bf16[8,256,384]{2,1,0:T(8,128)(2,1)S(1)} %get-tuple-element.8) | copy-start | bytes 4718596
  216.2 1.4 copy-start.2
  216.2 1.9 copy-start.4
Sparse Core Ops, SparseCore 0:
  125.6 85.0 all-gather.1
where the time goes:
time: 234 us; the launch traced here: 232 us
  blocking collectives  86.5 us (37%)
  waiting for transfers between devices  77.8 us (33%)
  matrix products  18.9 us (8%)
  local copies, waits for them, and re-layouts  18.8 us (8%)
  other arithmetic  15.7 us (7%)
  between operations  14.2 us (6%)
    all_to_all x1, blocking collectives, on_device(): lax.all_to_all(spectrum, 'wide', split_axis=0, concat_axis=1, tiled=True)  86.5 us
    all_gather x1, waiting for transfers between devices, on_device(): whole = lax.all_gather(local, 'narrow', axis=1, tiled=True)  77.8 us
    dot_general x3, matrix products, cross_tile(): jnp.einsum('cik,cjk->cij', stacked, col_block, preferred_element_type=jnp...  11.1 us
    another operation x1, other arithmetic  9.28 us
    dot_general x1, matrix products, on_device(): jnp.einsum('pcn,isn->cips', table, filtered, preferred_element_type=jnp.f...  7.81 us
    another operation x3, other arithmetic, cross_tile(): return jnp.stack([product[:, :width], product[:, width:]])  6.19 us
    all_to_all x3, local copies, waits for them, and re-layouts, on_device(): lax.all_to_all(spectrum, 'wide', split_axis=0, concat_axis=1, tiled=True)  5.22 us
    reshape x1, local copies, waits for them, and re-layouts, on_device(): spectrum.astype(jnp.bfloat16).reshape(channels, inputs_dev, 2 * spectra)  4.72 us
  transfers between devices with their start and end apart: 1, of which 1 were waited for; matrix products, arithmetic and copies ran while one was open for 2% of the time, Pallas kernels for 0%

commit v1 on v0

v1 whole, which is shorter than its diff:
```python
import functools
import math

import jax
import jax.numpy as jnp
import numpy as np
from jax import lax
from jax.experimental import pallas as pl
from jax.experimental.pallas import tpu as pltpu
from jax.sharding import PartitionSpec as P

CHAN = 512
TAPS = 4
SPECTRA = 384
BLOCK = 256
FRAME = 2 * CHAN
SB = 128
NT = (((1,), (1,)), ((), ()))


def dft_table():
    positions = np.arange(FRAME, dtype=np.int32)
    bins = np.arange(CHAN, dtype=np.int32)
    phases = bins[:, None] * positions[None, :] % FRAME
    angles = phases.astype(np.float32) * np.float32(math.pi / CHAN)
    norming = np.float32(FRAME ** (-0.5))
    table = np.concatenate([np.cos(angles) * norming, -np.sin(angles) * norming])
    return table.astype(jnp.bfloat16)


def row_order():
    order = np.arange(256).reshape(32, 8).T.reshape(-1)
    return np.eye(256, dtype=np.float32)[order].astype(jnp.bfloat16)


def spectra_kernel(x_ref, halo_ref, taps_ref, table_ref, out_ref, frames, filtered):
    for f in range(SB):
        for n in range(0, FRAME, 128):
            frames[n // 128, 4 * f : 4 * f + 4, :] = x_ref[:, f * FRAME + n : f * FRAME + n + 128].astype(jnp.float32)
    for f in range(TAPS - 1):
        for n in range(0, FRAME, 128):
            frames[n // 128, 4 * (SB + f) : 4 * (SB + f) + 4, :] = halo_ref[
                :, f * FRAME + n : f * FRAME + n + 128
            ].astype(jnp.float32)
    for n in range(0, FRAME, 128):
        taps = [taps_ref[t : t + 1, n : n + 128] for t in range(TAPS)]
        for i in range(4):
            for s in range(0, SB, 16):
                total = frames[n // 128, pl.ds(i + 4 * s, 16, stride=4), :] * taps[0]
                for t in range(1, TAPS):
                    total = total + frames[n // 128, pl.ds(i + 4 * (s + t), 16, stride=4), :] * taps[t]
                filtered[i * SB + s : i * SB + s + 16, n : n + 128] = total.astype(jnp.bfloat16)
    for pair in range(2):
        product = lax.dot_general(
            table_ref[...], filtered[pair * 2 * SB : (pair + 1) * 2 * SB, :], NT,
            preferred_element_type=jnp.float32,
        )
        for p in range(2):
            part = product[p * CHAN : (p + 1) * CHAN]
            rows = jnp.concatenate(
                [part[:, :SB].reshape(CHAN // 8, 8, SB), part[:, SB:].reshape(CHAN // 8, 8, SB)], axis=1
            )
            out_ref[:, pair * 16 : pair * 16 + 16, p * SB : (p + 1) * SB] = rows.astype(jnp.bfloat16)


def filter_section(samples, pfb_taps, table, first, count):
    return pl.pallas_call(
        spectra_kernel,
        grid=(count,),
        in_specs=[
            pl.BlockSpec((4, SB * FRAME), lambda j: (0, first + j)),
            pl.BlockSpec((4, 4 * FRAME), lambda j: (0, (first + j + 1) * (SB // 4))),
            pl.BlockSpec((TAPS, FRAME), lambda j: (0, 0)),
            pl.BlockSpec((2 * CHAN, FRAME), lambda j: (0, 0)),
        ],
        out_specs=pl.BlockSpec((64, 32, 2 * SB), lambda j: (0, 0, j)),
        out_shape=jax.ShapeDtypeStruct((64, 32, count * 2 * SB), jnp.bfloat16),
        scratch_shapes=[
            pltpu.VMEM((FRAME // 128, 4 * (SB + 4), 128), jnp.float32),
            pltpu.VMEM((4 * SB, FRAME), jnp.bfloat16),
        ],
        compiler_params=pltpu.CompilerParams(vmem_limit_bytes=40 * 1024 * 1024),
        name="filter_section",
    )(samples, samples, pfb_taps, table)


def reorder(order, source, out_ref, groups, lane):
    width = source.shape[-1]
    for g in range(groups):
        rows = source[g * 8 : (g + 1) * 8].reshape(256, width)
        turned = jnp.dot(order, rows, preferred_element_type=jnp.float32).astype(jnp.bfloat16)
        for c in range(8):
            out_ref[c, g * 32 : (g + 1) * 32, lane : lane + width] = turned[c * 32 : (c + 1) * 32]


def stacked(rows):
    pieces = []
    for s in range(0, rows.shape[1], 2 * SB):
        pieces += [rows[:, s + SB : s + 2 * SB], -rows[:, s : s + SB]]
    return jnp.concatenate([rows, jnp.concatenate(pieces, axis=1)], axis=0)


def self_kernel(order_ref, own0_ref, own1_ref, own_ref, self_ref, held):
    step = pl.program_id(0)

    @pl.when(step == 0)
    def _():
        reorder(order_ref[...], own0_ref, held, 8, 0)
        reorder(order_ref[...], own1_ref, held, 8, 512)

    rows = held[step]
    own_ref[0] = rows
    product = lax.dot_general(stacked(rows), rows, NT, preferred_element_type=jnp.float32) * (1.0 / SPECTRA)
    self_ref[0, 0] = product[:BLOCK]
    self_ref[1, 0] = product[BLOCK:]


def self_tiles(order, own0, own1):
    whole = lambda a: pl.BlockSpec(a.shape, lambda c: (0,) * a.ndim)
    return pl.pallas_call(
        self_kernel,
        grid=(8,),
        in_specs=[whole(order), whole(own0), whole(own1)],
        out_specs=[
            pl.BlockSpec((1, BLOCK, 768), lambda c: (c, 0, 0)),
            pl.BlockSpec((2, 1, BLOCK, BLOCK), lambda c: (0, c, 0, 0)),
        ],
        out_shape=[
            jax.ShapeDtypeStruct((8, BLOCK, 768), jnp.bfloat16),
            jax.ShapeDtypeStruct((2, 8, BLOCK, BLOCK), jnp.float32),
        ],
        scratch_shapes=[pltpu.VMEM((8, BLOCK, 768), jnp.bfloat16)],
        compiler_params=pltpu.CompilerParams(vmem_limit_bytes=40 * 1024 * 1024),
        name="self_tiles",
    )(order, own0, own1)


def cross_kernel(order_ref, own_ref, prior0_ref, prior1_ref, fare0_ref, fare1_ref, faro0_ref, faro1_ref,
                 prior_ref, far_ref, held):
    step = pl.program_id(0)

    @pl.when(step == 0)
    def _():
        order = order_ref[...]
        reorder(order, prior0_ref, held, 8, 0)
        reorder(order, prior1_ref, held, 8, 512)
        far_held = held.at[:, BLOCK : BLOCK + BLOCK // 2]
        reorder(order, fare0_ref[...] + faro0_ref[...], far_held, 4, 0)
        reorder(order, fare1_ref[...] + faro1_ref[...], far_held, 4, 512)

    product = lax.dot_general(stacked(own_ref[0]), held[step], NT, preferred_element_type=jnp.float32) * (1.0 / SPECTRA)
    prior_ref[0, 0] = product[:BLOCK, :BLOCK]
    prior_ref[1, 0] = product[BLOCK:, :BLOCK]
    far_ref[0, 0] = product[:BLOCK, BLOCK:]
    far_ref[1, 0] = product[BLOCK:, BLOCK:]


def cross_tiles(order, own, *received):
    whole = lambda a: pl.BlockSpec(a.shape, lambda c: (0,) * a.ndim)
    return pl.pallas_call(
        cross_kernel,
        grid=(8,),
        in_specs=[whole(order), pl.BlockSpec((1, BLOCK, 768), lambda c: (c, 0, 0))] + [whole(a) for a in received],
        out_specs=[
            pl.BlockSpec((2, 1, BLOCK, BLOCK), lambda c: (0, c, 0, 0)),
            pl.BlockSpec((2, 1, BLOCK, BLOCK // 2), lambda c: (0, c, 0, 0)),
        ],
        out_shape=[
            jax.ShapeDtypeStruct((2, 8, BLOCK, BLOCK), jnp.float32),
            jax.ShapeDtypeStruct((2, 8, BLOCK, BLOCK // 2), jnp.float32),
        ],
        scratch_shapes=[pltpu.VMEM((8, BLOCK + BLOCK // 2, 768), jnp.bfloat16)],
        compiler_params=pltpu.CompilerParams(vmem_limit_bytes=48 * 1024 * 1024),
        name="cross_tiles",
    )(order, own, *received)


PRIOR = [(0, 1), (1, 2), (2, 3), (3, 0)]
FAR_EVEN = [(0, 2), (2, 0)]
FAR_ODD = [(0, 1), (2, 3)]


def on_device(table, order, samples, pfb_taps):
    chip = lax.axis_index("narrow") // 2
    chunks = [filter_section(samples, pfb_taps, table, 0, 2), filter_section(samples, pfb_taps, table, 2, 1)]
    own, prior, far_even, far_odd = [], [], [], []
    for chunk in chunks:
        local = lax.all_to_all(chunk, "wide", split_axis=0, concat_axis=0, tiled=True)
        own.append(local)
        before = lax.ppermute(local, "narrow", PRIOR)
        prior.append(before)
        leaving = lax.dynamic_slice_in_dim(local, (1 - chip) * 32, 32, 0)
        far_even.append(lax.ppermute(leaving, "narrow", FAR_EVEN))
        passed = lax.dynamic_slice_in_dim(before, chip * 32, 32, 0)
        far_odd.append(lax.ppermute(passed, "narrow", FAR_ODD))
    mine, self_vis = self_tiles(order, *own)
    prior_vis, far_vis = cross_tiles(order, mine, *prior, *far_even, *far_odd)
    return (self_vis, prior_vis, far_vis)


def solution(mesh):
    return jax.shard_map(
        functools.partial(on_device, dft_table(), row_order()),
        mesh=mesh,
        in_specs=(P(("narrow", "wide"), None), P()),
        out_specs=(
            P(None, "wide", "narrow", None),
            P(None, "wide", "narrow", None),
            P(None, "wide", "narrow", None),
        ),
        check_vma=False,
    )
```

time: 234 us -> 165 us (0.71)
  blocking collectives: 86.5 us -> 0 us
  starting transfers between devices: 0.04 us -> 29.5 us
  Pallas kernels: 0 us -> 23.9 us
  matrix products: 18.9 us -> 0 us
  waiting for transfers between devices: 77.8 us -> 95.1 us
  other arithmetic: 15.7 us -> 0 us
  between operations: 14.2 us -> 0.81 us
  local copies, waits for them, and re-layouts: 18.8 us -> 12.5 us
    all_to_all x1 -> x0, blocking collectives: 86.5 us -> none  [on_device(): lax.all_to_all(spectrum, 'wide', split_axis=0, concat_axis=1, tiled=True)]
    all_gather x1 -> x0, waiting for transfers between devices: 77.8 us -> none  [on_device(): whole = lax.all_gather(local, 'narrow', axis=1, tiled=True)]
    all_to_all x0 -> x2, waiting for transfers between devices: none -> 75.6 us  [on_device(): lax.all_to_all(chunk, 'wide', split_axis=0, concat_axis=0, tiled=True)]
    pallas_call x0 -> x4, Pallas kernels: none -> 23.9 us  [the longest x1 11 us: cross_tiles(): pl.pallas_call(cross_kernel, grid=(8,), in_specs=[whole(order), pl.BlockS...]
    ppermute x0 -> x6, waiting for transfers between devices: none -> 19.6 us  [the longest x2 19.5 us: on_device(): before = lax.ppermute(local, 'narrow', PRIOR)]
    all_to_all x0 -> x2, starting transfers between devices: none -> 18.9 us  [on_device(): lax.all_to_all(chunk, 'wide', split_axis=0, concat_axis=0, tiled=True)]
    dot_general x4 -> x0, matrix products: 18.9 us -> none  [the longest x3 11.1 us: cross_tile(): jnp.einsum('cik,cjk->cij', stacked, col_block, preferred_element_type=jnp...]
    another operation x4 -> x0, other arithmetic: 15.5 us -> none
  transfers between devices with their start and end apart: 1 -> 8, of which waited for: 1 -> 4; matrix products, arithmetic and copies ran while one was open for 2% -> 2% of each run, Pallas kernels for 0% -> 6%
where the time goes in v1:
time: 165 us; the launch traced here: 162 us
  waiting for transfers between devices  95.1 us (58%)
  starting transfers between devices  29.5 us (18%)
  Pallas kernels  23.9 us (14%)
  local copies, waits for them, and re-layouts  12.5 us (8%)
    all_to_all x2, waiting for transfers between devices, on_device(): lax.all_to_all(chunk, 'wide', split_axis=0, concat_axis=0, tiled=True)  75.6 us
    ppermute x2, waiting for transfers between devices, on_device(): before = lax.ppermute(local, 'narrow', PRIOR)  19.5 us
    all_to_all x2, starting transfers between devices, on_device(): lax.all_to_all(chunk, 'wide', split_axis=0, concat_axis=0, tiled=True)  18.9 us
    pallas_call x1, Pallas kernels, cross_tiles(): pl.pallas_call(cross_kernel, grid=(8,), in_specs=[whole(order), pl.BlockS...  11 us
    unnamed x20, local copies, waits for them, and re-layouts  9.73 us
    pallas_call x1, Pallas kernels, self_tiles(): pl.pallas_call(self_kernel, grid=(8,), in_specs=[whole(order), whole(own0...  7.88 us
    ppermute x2, starting transfers between devices, on_device(): far_even.append(lax.ppermute(leaving, 'narrow', FAR_EVEN))  7.83 us
    pallas_call x2, Pallas kernels, filter_section(): pl.pallas_call(spectra_kernel, grid=(count,), in_specs=[pl.BlockSpec((4,...  5.02 us
  transfers between devices with their start and end apart: 8, of which 4 were waited for; matrix products, arithmetic and copies ran while one was open for 2% of the time, Pallas kernels for 6%

profile of v1, /device:TPU:24, one launch (start us, length us, event | category | flops | bytes accessed | tf_op | source)
XLA Modules:
  0.0 161.8 jit_solution(18324340571678425162)
XLA Ops:
  0.6 1.9 %copy-done = bf16[4,396288]{1,0:T(4,128)(2,1)S(1)} copy-done((bf16[4,396288]{1,0:T(4,128)(2,1)S(1)}, bf16[4,396288]{1,0:T(4,128)(2,1)}, u32[]{:S(2)}) %copy-start) | copy-done | bytes 3170328
  2.5 1.6 copy-done.3
  4.1 0.7 copy-done.8
  4.8 3.4 %filter_section.2 = bf16[64,32,512]{2,1,0:T(8,128)(2,1)S(1)} custom-call(bf16[4,396288]{1,0:T(4,128)(2,1)S(1)} %copy-done, bf16[4,396288]{1,0:T(4,128)(2,1)S(1)} %copy-done, f32[4,1024]{1,0:T(4,128)S(1)} %copy-done.8, bf16[1024,1024]{1,0:T(8,128)(2,1)S(1)} %copy-done.3), custom_call_target="tpu_custom_call" | custom-call | tf_op jit(solution)/shard_map/filter_section/pallas_call | solution.py:67
  8.3 1.3 copy-done.2
  9.6 13.3 %all-to-all-start = ((bf16[64,32,512]{2,1,0:T(8,128)(2,1)}), bf16[64,32,512]{2,1,0:T(8,128)(2,1)}, u32[]{:S(2)}, u32[]{:S(2)}) async-start(bf16[64,32,512]{2,1,0:T(8,128)(2,1)} %copy-done.2), calls=%async_computation | async-start | bytes 4194304 | tf_op jit(solution)/shard_map/all_to_all | solution.py:188
  22.9 1.6 copy-done.4
  24.5 1.6 filter_section.3
  26.1 1.0 copy-done.5
  27.1 47.1 %all-to-all-done.own0_ref = bf16[64,32,512]{2,1,0:T(8,128)(2,1)} async-done(((bf16[64,32,512]{2,1,0:T(8,128)(2,1)}), bf16[64,32,512]{2,1,0:T(8,128)(2,1)}, u32[]{:S(2)}, u32[]{:S(2)}) %all-to-all-start) | async-done | bytes 2097184 | tf_op jit(solution)/shard_map/all_to_all | solution.py:188
  74.1 5.7 %all-to-all-start.1 = ((bf16[64,32,256]{2,1,0:T(8,128)(2,1)}), bf16[64,32,256]{2,1,0:T(8,128)(2,1)S(1)}, u32[]{:S(2)}, u32[]{:S(2)}) async-start(bf16[64,32,256]{2,1,0:T(8,128)(2,1)} %copy-done.5), calls=%async_computation.1 | async-start | bytes 2097152 | tf_op jit(solution)/shard_map/all_to_all | solution.py:188
  79.8 0.1 collective-permute-start
  79.9 28.5 %all-to-all-done.1.own1_ref = bf16[64,32,256]{2,1,0:T(8,128)(2,1)S(1)} async-done(((bf16[64,32,256]{2,1,0:T(8,128)(2,1)}), bf16[64,32,256]{2,1,0:T(8,128)(2,1)S(1)}, u32[]{:S(2)}, u32[]{:S(2)}) %all-to-all-start.1) | async-done | bytes 1048608 | tf_op jit(solution)/shard_map/all_to_all | solution.py:188
  108.4 1.3 constant_dynamic-slice_fusion.3
  109.8 4.8 %collective-permute-start.2 = (bf16[32,32,512]{2,1,0:T(8,128)(2,1)S(1)}, bf16[32,32,512]{2,1,0:T(8,128)(2,1)S(1)}, u32[]{:S(2)}, u32[]{:S(2)}) collective-permute-start(bf16[32,32,512]{2,1,0:T(8,128)(2,1)S(1)} %constant_dynamic-slice_fusion.3), channel_id=1, source_target_pairs={{0,2},{2,0},{4,6},{6,4},{8,10},{10,8},{12,14},{14,12},{16,18},{18,... | collective-permute-start | bytes 3145736 | tf_op jit(solution)/shard_map/ppermute | solution.py:193
  114.5 3.0 %collective-permute-done.prior0_ref = bf16[64,32,512]{2,1,0:T(8,128)(2,1)} collective-permute-done((bf16[64,32,512]{2,1,0:T(8,128)(2,1)}, bf16[64,32,512]{2,1,0:T(8,128)(2,1)}, u32[]{:S(2)}, u32[]{:S(2)}) %collective-permute-start) | collective-permute-done | bytes 2097184 | tf_op jit(solution)/shard_map/ppermute | solution.py:190
  117.5 1.3 constant_dynamic-slice_fusion.1
  118.9 1.4 collective-permute-start.4
  120.3 3.1 %collective-permute-start.3 = (bf16[32,32,256]{2,1,0:T(8,128)(2,1)S(1)}, bf16[32,32,256]{2,1,0:T(8,128)(2,1)S(1)}, u32[]{:S(2)}, u32[]{:S(2)}) collective-permute-start(bf16[32,32,256]{2,1,0:T(8,128)(2,1)S(1)} %constant_dynamic-slice_fusion.2), channel_id=1, source_target_pairs={{0,2},{2,0},{4,6},{6,4},{8,10},{10,8},{12,14},{14,12},{16,18},{18,... | collective-permute-start | bytes 1572872 | tf_op jit(solution)/shard_map/ppermute | solution.py:193
  123.3 16.6 %collective-permute-done.1.prior1_ref = bf16[64,32,256]{2,1,0:T(8,128)(2,1)S(1)} collective-permute-done((bf16[64,32,256]{2,1,0:T(8,128)(2,1)S(1)}, bf16[64,32,256]{2,1,0:T(8,128)(2,1)S(1)}, u32[]{:S(2)}, u32[]{:S(2)}) %collective-permute-start.1) | collective-permute-done | bytes 1048608 | tf_op jit(solution)/shard_map/ppermute | solution.py:190
  139.9 1.3 collective-permute-start.5
  141.3 7.9 %self_tiles.1 = (bf16[8,256,768]{2,1,0:T(8,128)(2,1)S(1)}, f32[2,8,256,256]{3,2,1,0:T(8,128)}) custom-call(bf16[256,256]{1,0:T(8,128)(2,1)S(1)} %copy-done.7, bf16[64,32,512]{2,1,0:T(8,128)(2,1)} %all-to-all-done.own0_ref, bf16[64,32,256]{2,1,0:T(8,128)(2,1)S(1)} %all-to-all-done.1.own1_ref), custom_call_target="tpu_custom_call" | custom-call | tf_op jit(solution)/shard_map/self_tiles/pallas_call | solution.py:120
  149.2 1.6 %copy-done.6 = bf16[8,256,768]{2,1,0:T(8,128)(2,1)} copy-done((bf16[8,256,768]{2,1,0:T(8,128)(2,1)}, bf16[8,256,768]{2,1,0:T(8,128)(2,1)S(1)}, u32[]{:S(2)}) %copy-start.6) | copy-done | bytes 3145752
  150.8 11.0 %cross_tiles.1 = (f32[2,8,256,256]{3,2,1,0:T(8,128)}, f32[2,8,256,128]{3,2,1,0:T(8,128)}) custom-call(bf16[256,256]{1,0:T(8,128)(2,1)S(1)} %copy-done.7, bf16[8,256,768]{2,1,0:T(8,128)(2,1)} %copy-done.6, bf16[64,32,512]{2,1,0:T(8,128)(2,1)} %collective-permute-done.prior0_ref, bf16[64,32,256]{2,1,0:T(8,128)(2,1)S(1)} %collective-permute-done.1.prior1_ref, ...), custom_call_target="tpu_custom_call" | custom-call | tf_op jit(solution)/shard_map/cross_tiles/pallas_call | solution.py:160
  (20 shorter events, 0.1 us)
Async XLA Ops:
  0.6 1.9 %copy-start = (bf16[4,396288]{1,0:T(4,128)(2,1)S(1)}, bf16[4,396288]{1,0:T(4,128)(2,1)}, u32[]{:S(2)}) copy-start(bf16[4,396288]{1,0:T(4,128)(2,1)} %halo_ref.3) | copy-start | bytes 9510916
  2.5 1.6 copy-start.3
  4.1 0.7 copy-start.8
  8.3 1.3 copy-start.2
  9.6 13.3 %copy-start.1 = (bf16[4,396288]{1,0:T(4,128)(2,1)S(1)}, bf16[4,396288]{1,0:T(4,128)(2,1)}, u32[]{:S(2)}) copy-start(bf16[4,396288]{1,0:T(4,128)(2,1)} %halo_ref.3) | copy-start | bytes 9510916
  9.6 13.3 %copy-start.9 = (f32[4,1024]{1,0:T(4,128)S(1)}, f32[4,1024]{1,0:T(4,128)}, u32[]{:S(2)}) copy-start(f32[4,1024]{1,0:T(4,128)} %taps_ref.3) | copy-start | bytes 49156
  9.6 64.6 %all-to-all-start = ((bf16[64,32,512]{2,1,0:T(8,128)(2,1)}), bf16[64,32,512]{2,1,0:T(8,128)(2,1)}, u32[]{:S(2)}, u32[]{:S(2)}) async-start(bf16[64,32,512]{2,1,0:T(8,128)(2,1)} %copy-done.2), calls=%async_computation | async-start | bytes 4194304 | tf_op jit(solution)/shard_map/all_to_all | solution.py:188
  22.9 1.6 copy-start.4
  26.1 1.0 copy-start.5
  74.1 34.3 %all-to-all-start.1 = ((bf16[64,32,256]{2,1,0:T(8,128)(2,1)}), bf16[64,32,256]{2,1,0:T(8,128)(2,1)S(1)}, u32[]{:S(2)}, u32[]{:S(2)}) async-start(bf16[64,32,256]{2,1,0:T(8,128)(2,1)} %copy-done.5), calls=%async_computation.1 | async-start | bytes 2097152 | tf_op jit(solution)/shard_map/all_to_all | solution.py:188
  79.8 37.7 %collective-permute-start = (bf16[64,32,512]{2,1,0:T(8,128)(2,1)}, bf16[64,32,512]{2,1,0:T(8,128)(2,1)}, u32[]{:S(2)}, u32[]{:S(2)}) collective-permute-start(bf16[64,32,512]{2,1,0:T(8,128)(2,1)} %all-to-all-done.own0_ref), channel_id=1, source_target_pairs={{0,1},{1,2},{2,3},{3,0},{4,5},{5,6},{6,7},{7,4},{8,9},{9,10},{10,1... | collective-permute-start | bytes 6291464 | tf_op jit(solution)/shard_map/ppermute | solution.py:190
  108.4 31.5 %collective-permute-start.1 = (bf16[64,32,256]{2,1,0:T(8,128)(2,1)S(1)}, bf16[64,32,256]{2,1,0:T(8,128)(2,1)S(1)}, u32[]{:S(2)}, u32[]{:S(2)}) collective-permute-start(bf16[64,32,256]{2,1,0:T(8,128)(2,1)S(1)} %all-to-all-done.1.own1_ref), channel_id=1, source_target_pairs={{0,1},{1,2},{2,3},{3,0},{4,5},{5,6},{6,7},{7,4},{8,9},{9,10},{10,1... | collective-permute-start | bytes 3145736 | tf_op jit(solution)/shard_map/ppermute | solution.py:190
  109.7 31.5 %copy-start.7 = (bf16[256,256]{1,0:T(8,128)(2,1)S(1)}, bf16[256,256]{1,0:T(8,128)(2,1)}, u32[]{:S(2)}) copy-start(bf16[256,256]{1,0:T(8,128)(2,1)} %constant.29.clone.order_ref) | copy-start | bytes 393220
  109.8 41.1 %collective-permute-start.2 = (bf16[32,32,512]{2,1,0:T(8,128)(2,1)S(1)}, bf16[32,32,512]{2,1,0:T(8,128)(2,1)S(1)}, u32[]{:S(2)}, u32[]{:S(2)}) collective-permute-start(bf16[32,32,512]{2,1,0:T(8,128)(2,1)S(1)} %constant_dynamic-slice_fusion.3), channel_id=1, source_target_pairs={{0,2},{2,0},{4,6},{6,4},{8,10},{10,8},{12,14},{14,12},{16,18},{18,... | collective-permute-start | bytes 3145736 | tf_op jit(solution)/shard_map/ppermute | solution.py:193
  118.9 32.0 %collective-permute-start.4 = (bf16[32,32,512]{2,1,0:T(8,128)(2,1)S(1)}, bf16[32,32,512]{2,1,0:T(8,128)(2,1)S(1)}, u32[]{:S(2)}, u32[]{:S(2)}) collective-permute-start(bf16[32,32,512]{2,1,0:T(8,128)(2,1)S(1)} %constant_dynamic-slice_fusion.1), channel_id=1, source_target_pairs={{0,1},{2,3},{4,5},{6,7},{8,9},{10,11},{12,13},{14,15},{16,17},{18,... | collective-permute-start | bytes 3145736 | tf_op jit(solution)/shard_map/ppermute | solution.py:195
  120.3 30.5 %collective-permute-start.3 = (bf16[32,32,256]{2,1,0:T(8,128)(2,1)S(1)}, bf16[32,32,256]{2,1,0:T(8,128)(2,1)S(1)}, u32[]{:S(2)}, u32[]{:S(2)}) collective-permute-start(bf16[32,32,256]{2,1,0:T(8,128)(2,1)S(1)} %constant_dynamic-slice_fusion.2), channel_id=1, source_target_pairs={{0,2},{2,0},{4,6},{6,4},{8,10},{10,8},{12,14},{14,12},{16,18},{18,... | collective-permute-start | bytes 1572872 | tf_op jit(solution)/shard_map/ppermute | solution.py:193
  139.9 10.9 %collective-permute-start.5 = (bf16[32,32,256]{2,1,0:T(8,128)(2,1)S(1)}, bf16[32,32,256]{2,1,0:T(8,128)(2,1)S(1)}, u32[]{:S(2)}, u32[]{:S(2)}) collective-permute-start(bf16[32,32,256]{2,1,0:T(8,128)(2,1)S(1)} %constant_dynamic-slice_fusion), channel_id=1, source_target_pairs={{0,1},{2,3},{4,5},{6,7},{8,9},{10,11},{12,13},{14,15},{16,17},{18,... | collective-permute-start | bytes 1572872 | tf_op jit(solution)/shard_map/ppermute | solution.py:195
  149.2 1.6 %copy-start.6 = (bf16[8,256,768]{2,1,0:T(8,128)(2,1)}, bf16[8,256,768]{2,1,0:T(8,128)(2,1)S(1)}, u32[]{:S(2)}) copy-start(bf16[8,256,768]{2,1,0:T(8,128)(2,1)S(1)} %get-tuple-element.8.own_ref) | copy-start | bytes 9437188

commit v2 on v1

v2 whole, which is shorter than its diff:
```python
import functools
import math

import jax
import jax.numpy as jnp
import numpy as np
from jax import lax
from jax.experimental import pallas as pl
from jax.experimental.pallas import tpu as pltpu
from jax.sharding import PartitionSpec as P

CHAN = 512
TAPS = 4
SPECTRA = 384
BLOCK = 256
FRAME = 2 * CHAN
SB = 128
NT = (((1,), (1,)), ((), ()))


def dft_table():
    positions = np.arange(FRAME, dtype=np.int32)
    bins = np.arange(CHAN, dtype=np.int32)
    phases = bins[:, None] * positions[None, :] % FRAME
    angles = phases.astype(np.float32) * np.float32(math.pi / CHAN)
    norming = np.float32(FRAME ** (-0.5))
    table = np.concatenate([np.cos(angles) * norming, -np.sin(angles) * norming])
    return table.astype(jnp.bfloat16)


def row_order():
    order = np.arange(256).reshape(32, 8).T.reshape(-1)
    return np.eye(256, dtype=np.float32)[order].astype(jnp.bfloat16)


def spectra_kernel(first, x_ref, table_ref, taps_ref, out_ref, x_held, table, frames, filtered, out_held, x_sem, table_sem, out_sem):
    count = x_held.shape[0]
    span = (SB + TAPS - 1) * FRAME
    arriving = [
        pltpu.make_async_copy(x_ref.at[:, pl.ds((first + j) * SB * FRAME, span)], x_held.at[j], x_sem.at[j])
        for j in range(count)
    ]
    table_arriving = pltpu.make_async_copy(table_ref, table, table_sem)
    arriving[0].start()
    table_arriving.start()
    for copy in arriving[1:]:
        copy.start()
    leaving = []
    for j in range(count):
        arriving[j].wait()
        for f in range(SB + TAPS - 1):
            for n in range(0, FRAME, 128):
                frames[n // 128, 4 * f : 4 * f + 4, :] = x_held[
                    j, :, f * FRAME + n : f * FRAME + n + 128
                ].astype(jnp.float32)
        for n in range(0, FRAME, 128):
            taps = [taps_ref[t : t + 1, n : n + 128] for t in range(TAPS)]
            for i in range(4):
                for s in range(0, SB, 16):
                    total = frames[n // 128, pl.ds(i + 4 * s, 16, stride=4), :] * taps[0]
                    for t in range(1, TAPS):
                        total = total + frames[n // 128, pl.ds(i + 4 * (s + t), 16, stride=4), :] * taps[t]
                    filtered[i * SB + s : i * SB + s + 16, n : n + 128] = total.astype(jnp.bfloat16)
        if j == 0:
            table_arriving.wait()
        for pair in range(2):
            product = lax.dot_general(
                table[...], filtered[pair * 2 * SB : (pair + 1) * 2 * SB, :], NT,
                preferred_element_type=jnp.float32,
            )
            for p in range(2):
                part = product[p * CHAN : (p + 1) * CHAN]
                rows = jnp.concatenate(
                    [part[:, :SB].reshape(CHAN // 8, 8, SB), part[:, SB:].reshape(CHAN // 8, 8, SB)], axis=1
                )
                out_held[j, :, pair * 16 : pair * 16 + 16, p * SB : (p + 1) * SB] = rows.astype(jnp.bfloat16)
        copy = pltpu.make_async_copy(
            out_held.at[j], out_ref.at[:, :, pl.ds(j * 2 * SB, 2 * SB)], out_sem.at[j]
        )
        copy.start()
        leaving.append(copy)
    for copy in leaving:
        copy.wait()


def filter_section(samples, pfb_taps, table, first, count):
    in_hbm = pl.BlockSpec(memory_space=pltpu.HBM)
    return pl.pallas_call(
        functools.partial(spectra_kernel, first),
        in_specs=[in_hbm, in_hbm, pl.BlockSpec(memory_space=pltpu.VMEM)],
        out_specs=in_hbm,
        out_shape=jax.ShapeDtypeStruct((64, 32, count * 2 * SB), jnp.bfloat16),
        scratch_shapes=[
            pltpu.VMEM((count, 4, (SB + TAPS - 1) * FRAME), jnp.bfloat16),
            pltpu.VMEM((2 * CHAN, FRAME), jnp.bfloat16),
            pltpu.VMEM((FRAME // 128, 4 * (SB + 4), 128), jnp.float32),
            pltpu.VMEM((4 * SB, FRAME), jnp.bfloat16),
            pltpu.VMEM((count, 64, 32, 2 * SB), jnp.bfloat16),
            pltpu.SemaphoreType.DMA((count,)),
            pltpu.SemaphoreType.DMA,
            pltpu.SemaphoreType.DMA((count,)),
        ],
        compiler_params=pltpu.CompilerParams(vmem_limit_bytes=40 * 1024 * 1024),
        name="filter_section",
    )(samples, table, pfb_taps)


def reorder(order, source, out_ref, groups, lane):
    width = source.shape[-1]
    for g in range(groups):
        rows = source[g * 8 : (g + 1) * 8].reshape(256, width)
        turned = jnp.dot(order, rows, preferred_element_type=jnp.float32).astype(jnp.bfloat16)
        for c in range(8):
            out_ref[c, g * 32 : (g + 1) * 32, lane : lane + width] = turned[c * 32 : (c + 1) * 32]


def stacked(rows):
    pieces = []
    for s in range(0, rows.shape[1], 2 * SB):
        pieces += [rows[:, s + SB : s + 2 * SB], -rows[:, s : s + SB]]
    return jnp.concatenate([rows, jnp.concatenate(pieces, axis=1)], axis=0)


def self_kernel(order_ref, own0_ref, own1_ref, own_ref, self_ref, held):
    step = pl.program_id(0)

    @pl.when(step == 0)
    def _():
        reorder(order_ref[...], own0_ref, held, 8, 0)
        reorder(order_ref[...], own1_ref, held, 8, 512)

    rows = held[step]
    own_ref[0] = rows
    product = lax.dot_general(stacked(rows), rows, NT, preferred_element_type=jnp.float32) * (1.0 / SPECTRA)
    self_ref[0, 0] = product[:BLOCK]
    self_ref[1, 0] = product[BLOCK:]


def self_tiles(order, own0, own1):
    whole = lambda a: pl.BlockSpec(a.shape, lambda c: (0,) * a.ndim)
    return pl.pallas_call(
        self_kernel,
        grid=(8,),
        in_specs=[whole(order), whole(own0), whole(own1)],
        out_specs=[
            pl.BlockSpec((1, BLOCK, 768), lambda c: (c, 0, 0)),
            pl.BlockSpec((2, 1, BLOCK, BLOCK), lambda c: (0, c, 0, 0)),
        ],
        out_shape=[
            jax.ShapeDtypeStruct((8, BLOCK, 768), jnp.bfloat16),
            jax.ShapeDtypeStruct((2, 8, BLOCK, BLOCK), jnp.float32),
        ],
        scratch_shapes=[pltpu.VMEM((8, BLOCK, 768), jnp.bfloat16)],
        compiler_params=pltpu.CompilerParams(vmem_limit_bytes=40 * 1024 * 1024),
        name="self_tiles",
    )(order, own0, own1)


def early_kernel(order_ref, prior_ref, fare_ref, faro_ref, out_ref):
    step = pl.program_id(0)

    @pl.when(step < 8)
    def _():
        reorder(order_ref[...], prior_ref, out_ref, 1, 0)

    @pl.when(step >= 8)
    def _():
        reorder(order_ref[...], fare_ref[...] + faro_ref[...], out_ref, 1, 0)


def early_columns(order, prior, far_even, far_odd):
    width = prior.shape[-1]
    far_spec = pl.BlockSpec((8, 32, width), lambda g: (jnp.maximum(g - 8, 0), 0, 0))
    return pl.pallas_call(
        early_kernel,
        grid=(12,),
        in_specs=[
            pl.BlockSpec(order.shape, lambda g: (0, 0)),
            pl.BlockSpec((8, 32, width), lambda g: (jnp.minimum(g, 7), 0, 0)),
            far_spec,
            far_spec,
        ],
        out_specs=pl.BlockSpec((8, 32, width), lambda g: (0, g, 0)),
        out_shape=jax.ShapeDtypeStruct((8, BLOCK + BLOCK // 2, width), jnp.bfloat16),
        compiler_params=pltpu.CompilerParams(vmem_limit_bytes=40 * 1024 * 1024),
        name="early_columns",
    )(order, prior, far_even, far_odd)


def cross_kernel(order_ref, own_ref, early_ref, late_prior_ref, late_fare_ref, late_faro_ref, prior_ref, far_ref, held):
    step = pl.program_id(0)
    width = early_ref.shape[-1]

    @pl.when(step == 0)
    def _():
        order = order_ref[...]
        reorder(order, late_prior_ref, held, 8, 0)
        reorder(order, late_fare_ref[...] + late_faro_ref[...], held.at[:, BLOCK : BLOCK + BLOCK // 2], 4, 0)

    rows = stacked(own_ref[0])
    product = lax.dot_general(rows[:, :width], early_ref[0], NT, preferred_element_type=jnp.float32)
    product += lax.dot_general(rows[:, width:], held[step], NT, preferred_element_type=jnp.float32)
    product *= 1.0 / SPECTRA
    prior_ref[0, 0] = product[:BLOCK, :BLOCK]
    prior_ref[1, 0] = product[BLOCK:, :BLOCK]
    far_ref[0, 0] = product[:BLOCK, BLOCK:]
    far_ref[1, 0] = product[BLOCK:, BLOCK:]


def cross_tiles(order, own, early, *late):
    whole = lambda a: pl.BlockSpec(a.shape, lambda c: (0,) * a.ndim)
    channel = lambda a: pl.BlockSpec((1,) + a.shape[1:], lambda c: (c, 0, 0))
    return pl.pallas_call(
        cross_kernel,
        grid=(8,),
        in_specs=[whole(order), channel(own), channel(early)] + [whole(a) for a in late],
        out_specs=[
            pl.BlockSpec((2, 1, BLOCK, BLOCK), lambda c: (0, c, 0, 0)),
            pl.BlockSpec((2, 1, BLOCK, BLOCK // 2), lambda c: (0, c, 0, 0)),
        ],
        out_shape=[
            jax.ShapeDtypeStruct((2, 8, BLOCK, BLOCK), jnp.float32),
            jax.ShapeDtypeStruct((2, 8, BLOCK, BLOCK // 2), jnp.float32),
        ],
        scratch_shapes=[pltpu.VMEM((8, BLOCK + BLOCK // 2, late[0].shape[-1]), jnp.bfloat16)],
        compiler_params=pltpu.CompilerParams(vmem_limit_bytes=48 * 1024 * 1024),
        name="cross_tiles",
    )(order, own, early, *late)


PRIOR = [(0, 1), (1, 2), (2, 3), (3, 0)]
FAR_EVEN = [(0, 2), (2, 0)]
FAR_ODD = [(0, 1), (2, 3)]


def on_device(table, order, samples, pfb_taps):
    chip = lax.axis_index("narrow") // 2
    early = filter_section(samples, pfb_taps, table, 0, 2)
    late = filter_section(samples, pfb_taps, table, 2, 1)

    def far_leaving(local):
        return lax.dynamic_slice_in_dim(local, (1 - chip) * 32, 32, 0)

    def far_passed(before):
        return lax.dynamic_slice_in_dim(before, chip * 32, 32, 0)

    own0 = lax.all_to_all(early, "wide", split_axis=0, concat_axis=0, tiled=True)
    late, own0 = lax.optimization_barrier((late, own0))
    own1 = lax.all_to_all(late, "wide", split_axis=0, concat_axis=0, tiled=True)
    prior0 = lax.ppermute(own0, "narrow", PRIOR)
    far_even0 = lax.ppermute(far_leaving(own0), "narrow", FAR_EVEN)
    far_odd0 = lax.ppermute(far_passed(prior0), "narrow", FAR_ODD)
    held0 = early_columns(order, prior0, far_even0, far_odd0)
    own1, held0 = lax.optimization_barrier((own1, held0))
    prior1 = lax.ppermute(own1, "narrow", PRIOR)
    far_even1 = lax.ppermute(far_leaving(own1), "narrow", FAR_EVEN)
    mine, self_vis = self_tiles(order, own0, own1)
    prior1, mine = lax.optimization_barrier((prior1, mine))
    far_odd1 = lax.ppermute(far_passed(prior1), "narrow", FAR_ODD)
    prior_vis, far_vis = cross_tiles(order, mine, held0, prior1, far_even1, far_odd1)
    return (self_vis, prior_vis, far_vis)


def solution(mesh):
    return jax.shard_map(
        functools.partial(on_device, dft_table(), row_order()),
        mesh=mesh,
        in_specs=(P(("narrow", "wide"), None), P()),
        out_specs=(
            P(None, "wide", "narrow", None),
            P(None, "wide", "narrow", None),
            P(None, "wide", "narrow", None),
        ),
        check_vma=False,
    )
```

time: 165 us -> 168 us (1.018); the launches traced: 162 us -> 167 us
  Pallas kernels: 23.9 us -> 28.8 us
    all_to_all x2, waiting for transfers between devices: 75.6 us -> 44.4 us  [the longest x1 44.4 us: on_device(): lax.all_to_all(early, 'wide', split_axis=0, concat_axis=0, tiled=True)]
    ppermute x6, waiting for transfers between devices: 19.6 us -> 49.2 us  [the longest x1 38.4 us: on_device(): prior0 = lax.ppermute(own0, 'narrow', PRIOR)]
    pallas_call x3 -> x4, Pallas kernels: 16 us -> 22.5 us  [the longest x1 9.39 us: cross_tiles(): pl.pallas_call(cross_kernel, grid=(8,), in_specs=[whole(order), channel(o...]
    unnamed x20, local copies, waits for them, and re-layouts: 9.73 us -> 11.6 us
    ppermute x6, starting transfers between devices: 10.6 us -> 12.4 us  [the longest x1 4.64 us: on_device(): far_even0 = lax.ppermute(far_leaving(own0), 'narrow', FAR_EVEN)]
  transfers between devices with their start and end apart: 8 -> 8, of which waited for: 4 -> 5; matrix products, arithmetic and copies ran while one was open for 2% -> 1% of each run, Pallas kernels for 6% -> 9%
where the time goes in v2:
time: 168 us; the launch traced here: 167 us
  waiting for transfers between devices  93.6 us (56%)
  starting transfers between devices  31 us (18%)
  Pallas kernels  28.8 us (17%)
  local copies, waits for them, and re-layouts  13.1 us (8%)
    all_to_all x1, waiting for transfers between devices, on_device(): lax.all_to_all(early, 'wide', split_axis=0, concat_axis=0, tiled=True)  44.4 us
    ppermute x1, waiting for transfers between devices, on_device(): prior0 = lax.ppermute(own0, 'narrow', PRIOR)  38.4 us
    all_to_all x1, starting transfers between devices, on_device(): lax.all_to_all(early, 'wide', split_axis=0, concat_axis=0, tiled=True)  12.9 us
    unnamed x20, local copies, waits for them, and re-layouts  11.6 us
    pallas_call x1, Pallas kernels, cross_tiles(): pl.pallas_call(cross_kernel, grid=(8,), in_specs=[whole(order), channel(o...  9.39 us
    pallas_call x2, Pallas kernels, filter_section(): pl.pallas_call(functools.partial(spectra_kernel, first), in_specs=[in_hbm...  6.9 us
    ppermute x1, waiting for transfers between devices, on_device(): prior1 = lax.ppermute(own1, 'narrow', PRIOR)  6.36 us
    pallas_call x1, Pallas kernels, self_tiles(): pl.pallas_call(self_kernel, grid=(8,), in_specs=[whole(order), whole(own0...  6.27 us
  transfers between devices with their start and end apart: 8, of which 5 were waited for; matrix products, arithmetic and copies ran while one was open for 1% of the time, Pallas kernels for 9%

profile of v2, /device:TPU:24, one launch (start us, length us, event | category | flops | bytes accessed | tf_op | source)
XLA Modules:
  0.0 167.3 jit_solution(5178929526475117862)
XLA Ops:
  0.6 1.9 %copy-done = bf16[4,396288]{1,0:T(4,128)(2,1)S(1)} copy-done((bf16[4,396288]{1,0:T(4,128)(2,1)S(1)}, bf16[4,396288]{1,0:T(4,128)(2,1)}, u32[]{:S(2)}) %copy-start) | copy-done | bytes 3170328
  2.5 1.6 copy-done.3
  4.8 4.4 %filter_section.3 = bf16[64,32,512]{2,1,0:T(8,128)(2,1)S(1)} custom-call(bf16[4,396288]{1,0:T(4,128)(2,1)S(1)} %copy-done, bf16[1024,1024]{1,0:T(8,128)(2,1)S(1)} %copy-done.3, f32[4,1024]{1,0:T(4,128)S(1)} %copy-done.8), custom_call_target="tpu_custom_call" | custom-call | tf_op jit(solution)/shard_map/filter_section/pallas_call | solution.py:88
  9.2 1.3 copy-done.5
  10.6 12.9 %all-to-all-start = ((bf16[64,32,512]{2,1,0:T(8,128)(2,1)}), bf16[64,32,512]{2,1,0:T(8,128)(2,1)S(1)}, u32[]{:S(2)}, u32[]{:S(2)}) async-start(bf16[64,32,512]{2,1,0:T(8,128)(2,1)} %copy-done.5), calls=%async_computation | async-start | bytes 4194304 | tf_op jit(solution)/shard_map/all_to_all | solution.py:247
  23.5 1.9 %copy-done.1 = bf16[4,396288]{1,0:T(4,128)(2,1)S(1)} copy-done((bf16[4,396288]{1,0:T(4,128)(2,1)S(1)}, bf16[4,396288]{1,0:T(4,128)(2,1)}, u32[]{:S(2)}) %copy-start.1) | copy-done | bytes 3170328
  25.4 1.6 copy-done.4
  27.0 2.5 %filter_section.2 = bf16[64,32,256]{2,1,0:T(8,128)(2,1)S(1)} custom-call(bf16[4,396288]{1,0:T(4,128)(2,1)S(1)} %copy-done.1, bf16[1024,1024]{1,0:T(8,128)(2,1)S(1)} %copy-done.4, f32[4,1024]{1,0:T(4,128)S(1)} %copy-done.9), custom_call_target="tpu_custom_call" | custom-call | tf_op jit(solution)/shard_map/filter_section/pallas_call | solution.py:88
  29.5 1.0 copy-done.6
  30.5 44.4 %all-to-all-done.own0_ref = bf16[64,32,512]{2,1,0:T(8,128)(2,1)S(1)} async-done(((bf16[64,32,512]{2,1,0:T(8,128)(2,1)}), bf16[64,32,512]{2,1,0:T(8,128)(2,1)S(1)}, u32[]{:S(2)}, u32[]{:S(2)}) %all-to-all-start) | async-done | bytes 2097184 | tf_op jit(solution)/shard_map/all_to_all | solution.py:247
  74.9 5.7 %all-to-all-start.1 = ((bf16[64,32,256]{2,1,0:T(8,128)(2,1)}), bf16[64,32,256]{2,1,0:T(8,128)(2,1)S(1)}, u32[]{:S(2)}, u32[]{:S(2)}) async-start(bf16[64,32,256]{2,1,0:T(8,128)(2,1)} %copy-done.6), calls=%async_computation.1 | async-start | bytes 2097152 | tf_op jit(solution)/shard_map/all_to_all | solution.py:249
  80.7 4.6 %collective-permute-start.1 = (bf16[32,32,512]{2,1,0:T(8,128)(2,1)S(1)}, bf16[32,32,512]{2,1,0:T(8,128)(2,1)S(1)}, u32[]{:S(2)}, u32[]{:S(2)}) collective-permute-start(bf16[32,32,512]{2,1,0:T(8,128)(2,1)S(1)} %constant_dynamic-slice_fusion.3), channel_id=1, source_target_pairs={{0,2},{2,0},{4,6},{6,4},{8,10},{10,8},{12,14},{14,12},{16,18},{18,... | collective-permute-start | bytes 3145736 | tf_op jit(solution)/shard_map/ppermute | solution.py:251
  85.4 38.4 %collective-permute-done.prior_ref = bf16[64,32,512]{2,1,0:T(8,128)(2,1)} collective-permute-done((bf16[64,32,512]{2,1,0:T(8,128)(2,1)S(1)}, bf16[64,32,512]{2,1,0:T(8,128)(2,1)}, u32[]{:S(2)}, u32[]{:S(2)}) %collective-permute-start) | collective-permute-done | bytes 2097184 | tf_op jit(solution)/shard_map/ppermute | solution.py:250
  123.7 1.3 constant_dynamic-slice_fusion.2
  125.0 1.4 collective-permute-start.2
  126.4 2.2 %collective-permute-done.2.faro_ref = bf16[32,32,512]{2,1,0:T(8,128)(2,1)S(1)} collective-permute-done((bf16[32,32,512]{2,1,0:T(8,128)(2,1)S(1)}, bf16[32,32,512]{2,1,0:T(8,128)(2,1)S(1)}, u32[]{:S(2)}, u32[]{:S(2)}) %collective-permute-start.2) | collective-permute-done | bytes 1048608 | tf_op jit(solution)/shard_map/ppermute | solution.py:252
  128.6 6.2 %early_columns.1.early_ref = bf16[8,384,512]{2,1,0:T(8,128)(2,1)S(1)} custom-call(bf16[256,256]{1,0:T(8,128)(2,1)S(1)} %copy-done.7, bf16[64,32,512]{2,1,0:T(8,128)(2,1)} %collective-permute-done.prior_ref, bf16[32,32,512]{2,1,0:T(8,128)(2,1)S(1)} %collective-permute-done.1.fare_ref, bf16[32,32,512]{2,1,0:T(8,128)(2,1)S(1)} %collective-permute-done.2.faro_ref), custom_call_target="tpu_custom_call" | custom-call | tf_op jit(solution)/shard_map/early_columns/pallas_call | solution.py:174
  134.9 1.6 copy-done.2
  136.9 6.3 %self_tiles.1 = (bf16[8,256,768]{2,1,0:T(8,128)(2,1)S(1)}, f32[2,8,256,256]{3,2,1,0:T(8,128)}) custom-call(bf16[256,256]{1,0:T(8,128)(2,1)S(1)} %copy-done.7, bf16[64,32,512]{2,1,0:T(8,128)(2,1)S(1)} %all-to-all-done.own0_ref, bf16[64,32,256]{2,1,0:T(8,128)(2,1)S(1)} %all-to-all-done.1.own1_ref), custom_call_target="tpu_custom_call" | custom-call | tf_op jit(solution)/shard_map/self_tiles/pallas_call | solution.py:141
  143.2 4.6 %collective-permute-start.4 = (bf16[32,32,256]{2,1,0:T(8,128)(2,1)S(1)}, bf16[32,32,256]{2,1,0:T(8,128)(2,1)S(1)}, u32[]{:S(2)}, u32[]{:S(2)}) collective-permute-start(bf16[32,32,256]{2,1,0:T(8,128)(2,1)S(1)} %constant_dynamic-slice_fusion.1), channel_id=1, source_target_pairs={{0,2},{2,0},{4,6},{6,4},{8,10},{10,8},{12,14},{14,12},{16,18},{18,... | collective-permute-start | bytes 1572872 | tf_op jit(solution)/shard_map/ppermute | solution.py:256
  147.9 6.4 %collective-permute-done.3.late_prior_ref = bf16[64,32,256]{2,1,0:T(8,128)(2,1)S(1)} collective-permute-done((bf16[64,32,256]{2,1,0:T(8,128)(2,1)S(1)}, bf16[64,32,256]{2,1,0:T(8,128)(2,1)S(1)}, u32[]{:S(2)}, u32[]{:S(2)}) %collective-permute-start.3) | collective-permute-done | bytes 1048608 | tf_op jit(solution)/shard_map/ppermute | solution.py:255
  154.3 1.3 collective-permute-start.5
  155.6 2.3 %collective-permute-done.4.late_fare_ref = bf16[32,32,256]{2,1,0:T(8,128)(2,1)S(1)} collective-permute-done((bf16[32,32,256]{2,1,0:T(8,128)(2,1)S(1)}, bf16[32,32,256]{2,1,0:T(8,128)(2,1)S(1)}, u32[]{:S(2)}, u32[]{:S(2)}) %collective-permute-start.4) | collective-permute-done | bytes 524320 | tf_op jit(solution)/shard_map/ppermute | solution.py:256
  157.9 9.4 %cross_tiles.1 = (f32[2,8,256,256]{3,2,1,0:T(8,128)}, f32[2,8,256,128]{3,2,1,0:T(8,128)}) custom-call(bf16[256,256]{1,0:T(8,128)(2,1)S(1)} %copy-done.7, bf16[8,256,768]{2,1,0:T(8,128)(2,1)S(1)} %get-tuple-element.18.own_ref, bf16[8,384,512]{2,1,0:T(8,128)(2,1)} %copy-done.2, bf16[64,32,256]{2,1,0:T(8,128)(2,1)S(1)} %collective-permute-done.3.late_prior_ref, ...), custom_call_target="tpu_custom_call" | custom-call | tf_op jit(solution)/shard_map/cross_tiles/pallas_call | solution.py:213
  (21 shorter events, 1.3 us)
Async XLA Ops:
  0.6 1.9 %copy-start = (bf16[4,396288]{1,0:T(4,128)(2,1)S(1)}, bf16[4,396288]{1,0:T(4,128)(2,1)}, u32[]{:S(2)}) copy-start(bf16[4,396288]{1,0:T(4,128)(2,1)} %x_ref.3) | copy-start | bytes 9510916
  2.5 1.6 copy-start.3
  4.1 0.7 copy-start.8
  9.2 1.3 copy-start.5
  10.5 12.9 %copy-start.9 = (f32[4,1024]{1,0:T(4,128)S(1)}, f32[4,1024]{1,0:T(4,128)}, u32[]{:S(2)}) copy-start(f32[4,1024]{1,0:T(4,128)} %taps_ref.3) | copy-start | bytes 49156
  10.6 64.3 %all-to-all-start = ((bf16[64,32,512]{2,1,0:T(8,128)(2,1)}), bf16[64,32,512]{2,1,0:T(8,128)(2,1)S(1)}, u32[]{:S(2)}, u32[]{:S(2)}) async-start(bf16[64,32,512]{2,1,0:T(8,128)(2,1)} %copy-done.5), calls=%async_computation | async-start | bytes 4194304 | tf_op jit(solution)/shard_map/all_to_all | solution.py:247
  23.5 1.9 %copy-start.1 = (bf16[4,396288]{1,0:T(4,128)(2,1)S(1)}, bf16[4,396288]{1,0:T(4,128)(2,1)}, u32[]{:S(2)}) copy-start(bf16[4,396288]{1,0:T(4,128)(2,1)} %x_ref.3) | copy-start | bytes 9510916
  25.4 1.6 copy-start.4
  29.5 1.0 copy-start.6
  74.9 48.8 %collective-permute-start = (bf16[64,32,512]{2,1,0:T(8,128)(2,1)S(1)}, bf16[64,32,512]{2,1,0:T(8,128)(2,1)}, u32[]{:S(2)}, u32[]{:S(2)}) collective-permute-start(bf16[64,32,512]{2,1,0:T(8,128)(2,1)S(1)} %all-to-all-done.own0_ref), channel_id=1, source_target_pairs={{0,1},{1,2},{2,3},{3,0},{4,5},{5,6},{6,7},{7,4},{8,9},{9,10},{10,1... | collective-permute-start | bytes 6291464 | tf_op jit(solution)/shard_map/ppermute | solution.py:250
  74.9 61.6 %all-to-all-start.1 = ((bf16[64,32,256]{2,1,0:T(8,128)(2,1)}), bf16[64,32,256]{2,1,0:T(8,128)(2,1)S(1)}, u32[]{:S(2)}, u32[]{:S(2)}) async-start(bf16[64,32,256]{2,1,0:T(8,128)(2,1)} %copy-done.6), calls=%async_computation.1 | async-start | bytes 2097152 | tf_op jit(solution)/shard_map/all_to_all | solution.py:249
  80.6 48.0 %copy-start.7 = (bf16[256,256]{1,0:T(8,128)(2,1)S(1)}, bf16[256,256]{1,0:T(8,128)(2,1)}, u32[]{:S(2)}) copy-start(bf16[256,256]{1,0:T(8,128)(2,1)} %constant.29.clone.order_ref) | copy-start | bytes 393220
  80.7 45.7 %collective-permute-start.1 = (bf16[32,32,512]{2,1,0:T(8,128)(2,1)S(1)}, bf16[32,32,512]{2,1,0:T(8,128)(2,1)S(1)}, u32[]{:S(2)}, u32[]{:S(2)}) collective-permute-start(bf16[32,32,512]{2,1,0:T(8,128)(2,1)S(1)} %constant_dynamic-slice_fusion.3), channel_id=1, source_target_pairs={{0,2},{2,0},{4,6},{6,4},{8,10},{10,8},{12,14},{14,12},{16,18},{18,... | collective-permute-start | bytes 3145736 | tf_op jit(solution)/shard_map/ppermute | solution.py:251
  125.0 3.6 %collective-permute-start.2 = (bf16[32,32,512]{2,1,0:T(8,128)(2,1)S(1)}, bf16[32,32,512]{2,1,0:T(8,128)(2,1)S(1)}, u32[]{:S(2)}, u32[]{:S(2)}) collective-permute-start(bf16[32,32,512]{2,1,0:T(8,128)(2,1)S(1)} %constant_dynamic-slice_fusion.2), channel_id=1, source_target_pairs={{0,1},{2,3},{4,5},{6,7},{8,9},{10,11},{12,13},{14,15},{16,17},{18,... | collective-permute-start | bytes 3145736 | tf_op jit(solution)/shard_map/ppermute | solution.py:252
  134.9 1.7 copy-start.2
  136.5 17.7 %collective-permute-start.3 = (bf16[64,32,256]{2,1,0:T(8,128)(2,1)S(1)}, bf16[64,32,256]{2,1,0:T(8,128)(2,1)S(1)}, u32[]{:S(2)}, u32[]{:S(2)}) collective-permute-start(bf16[64,32,256]{2,1,0:T(8,128)(2,1)S(1)} %all-to-all-done.1.own1_ref), channel_id=1, source_target_pairs={{0,1},{1,2},{2,3},{3,0},{4,5},{5,6},{6,7},{7,4},{8,9},{9,10},{10,1... | collective-permute-start | bytes 3145736 | tf_op jit(solution)/shard_map/ppermute | solution.py:255
  143.2 14.6 %collective-permute-start.4 = (bf16[32,32,256]{2,1,0:T(8,128)(2,1)S(1)}, bf16[32,32,256]{2,1,0:T(8,128)(2,1)S(1)}, u32[]{:S(2)}, u32[]{:S(2)}) collective-permute-start(bf16[32,32,256]{2,1,0:T(8,128)(2,1)S(1)} %constant_dynamic-slice_fusion.1), channel_id=1, source_target_pairs={{0,2},{2,0},{4,6},{6,4},{8,10},{10,8},{12,14},{14,12},{16,18},{18,... | collective-permute-start | bytes 1572872 | tf_op jit(solution)/shard_map/ppermute | solution.py:256
  154.3 3.6 %collective-permute-start.5 = (bf16[32,32,256]{2,1,0:T(8,128)(2,1)S(1)}, bf16[32,32,256]{2,1,0:T(8,128)(2,1)S(1)}, u32[]{:S(2)}, u32[]{:S(2)}) collective-permute-start(bf16[32,32,256]{2,1,0:T(8,128)(2,1)S(1)} %constant_dynamic-slice_fusion), channel_id=1, source_target_pairs={{0,1},{2,3},{4,5},{6,7},{8,9},{10,11},{12,13},{14,15},{16,17},{18,... | collective-permute-start | bytes 1572872 | tf_op jit(solution)/shard_map/ppermute | solution.py:259

commit v3 on v1

v3 whole, which is shorter than its diff:
```python
import functools
import math

import jax
import jax.numpy as jnp
import numpy as np
from jax import lax
from jax.experimental import pallas as pl
from jax.experimental.pallas import tpu as pltpu
from jax.sharding import PartitionSpec as P

CHAN = 512
TAPS = 4
SPECTRA = 384
BLOCK = 256
FRAME = 2 * CHAN
HALF = SPECTRA // 2
LANES = 2 * HALF
NT = (((1,), (1,)), ((), ()))


def dft_table():
    positions = np.arange(FRAME, dtype=np.int32)
    bins = np.arange(CHAN, dtype=np.int32)
    phases = bins[:, None] * positions[None, :] % FRAME
    angles = phases.astype(np.float32) * np.float32(math.pi / CHAN)
    norming = np.float32(FRAME ** (-0.5))
    table = np.concatenate([np.cos(angles) * norming, -np.sin(angles) * norming])
    return table.astype(jnp.bfloat16)


def row_order():
    order = np.arange(256).reshape(32, 8).T.reshape(-1)
    return np.eye(256, dtype=np.float32)[order].astype(jnp.bfloat16)


def spectra_kernel(first, x_ref, table_ref, taps_ref, out_ref, x_held, table, frames, filtered, out_held, x_sem, table_sem, out_sem):
    arriving = pltpu.make_async_copy(
        x_ref.at[:, pl.ds(first * FRAME, (HALF + TAPS - 1) * FRAME)], x_held, x_sem
    )
    table_arriving = pltpu.make_async_copy(table_ref, table, table_sem)
    arriving.start()
    table_arriving.start()
    arriving.wait()
    for f in range(HALF + TAPS - 1):
        for n in range(0, FRAME, 128):
            frames[n // 128, 4 * f : 4 * f + 4, :] = x_held[:, f * FRAME + n : f * FRAME + n + 128].astype(jnp.float32)
    for n in range(0, FRAME, 128):
        taps = [taps_ref[t : t + 1, n : n + 128] for t in range(TAPS)]
        for i in range(4):
            for s in range(0, HALF, 16):
                total = frames[n // 128, pl.ds(i + 4 * s, 16, stride=4), :] * taps[0]
                for t in range(1, TAPS):
                    total = total + frames[n // 128, pl.ds(i + 4 * (s + t), 16, stride=4), :] * taps[t]
                row = i * 128 + s if s < 128 else 512 + i * 64 + s - 128
                filtered[row : row + 16, n : n + 128] = total.astype(jnp.bfloat16)
    table_arriving.wait()

    def transform(row):
        return lax.dot_general(table[...], filtered[row : row + 256, :], NT, preferred_element_type=jnp.float32)

    def put(pair, lane, even, odd):
        rows = jnp.concatenate([even.reshape(CHAN // 8, 8, 128), odd.reshape(CHAN // 8, 8, 128)], axis=1)
        out_held[:, pair * 16 : pair * 16 + 16, lane : lane + 128] = rows.astype(jnp.bfloat16)

    for pair in range(2):
        product = transform(pair * 256)
        for p in range(2):
            part = product[p * CHAN : (p + 1) * CHAN]
            put(pair, p * 128, part[:, :128], part[:, 128:])
    product = transform(512)
    low = lax.broadcasted_iota(jnp.int32, (CHAN, 128), 1) < 64
    for pair in range(2):
        real = product[:CHAN, pair * 128 : (pair + 1) * 128]
        imag = product[CHAN:, pair * 128 : (pair + 1) * 128]
        put(
            pair, 256, jnp.where(low, real, pltpu.roll(imag, 64, 1)), jnp.where(low, pltpu.roll(real, 64, 1), imag)
        )
    leaving = pltpu.make_async_copy(out_held, out_ref, out_sem)
    leaving.start()
    leaving.wait()


def filter_section(samples, pfb_taps, table, first):
    in_hbm = pl.BlockSpec(memory_space=pltpu.HBM)
    return pl.pallas_call(
        functools.partial(spectra_kernel, first),
        in_specs=[in_hbm, in_hbm, pl.BlockSpec(memory_space=pltpu.VMEM)],
        out_specs=in_hbm,
        out_shape=pltpu.HBM((64, 32, LANES), jnp.bfloat16),
        scratch_shapes=[
            pltpu.VMEM((4, (HALF + TAPS - 1) * FRAME), jnp.bfloat16),
            pltpu.VMEM((2 * CHAN, FRAME), jnp.bfloat16),
            pltpu.VMEM((FRAME // 128, 4 * (HALF + 4), 128), jnp.float32),
            pltpu.VMEM((4 * HALF, FRAME), jnp.bfloat16),
            pltpu.VMEM((64, 32, LANES), jnp.bfloat16),
            pltpu.SemaphoreType.DMA,
            pltpu.SemaphoreType.DMA,
            pltpu.SemaphoreType.DMA,
        ],
        compiler_params=pltpu.CompilerParams(vmem_limit_bytes=40 * 1024 * 1024),
        name="filter_section",
    )(
        pltpu.with_memory_space_constraint(samples, pltpu.HBM),
        pltpu.with_memory_space_constraint(table, pltpu.HBM),
        pfb_taps,
    )


def reorder(order, source, out_ref, groups, row, lane):
    width = source.shape[-1]
    for g in range(groups):
        rows = source[g * 8 : (g + 1) * 8].reshape(256, width)
        turned = jnp.dot(order, rows, preferred_element_type=jnp.float32).astype(jnp.bfloat16)
        for c in range(8):
            out_ref[c, pl.ds(row + g * 32, 32), lane : lane + width] = turned[c * 32 : (c + 1) * 32]


def stacked(rows):
    low = lax.broadcasted_iota(jnp.int32, (rows.shape[0], 128), 1) < 64
    pieces = []
    for s in range(0, rows.shape[1], LANES):
        mixed = pltpu.roll(rows[:, s + 256 : s + 384].astype(jnp.float32), 64, 1)
        mixed = jnp.where(low, mixed, -mixed).astype(jnp.bfloat16)
        pieces += [rows[:, s + 128 : s + 256], -rows[:, s : s + 128], mixed]
    return jnp.concatenate([rows, jnp.concatenate(pieces, axis=1)], axis=0)


def self_kernel(order_ref, own0_ref, own1_ref, own_ref, self_ref, held):
    step = pl.program_id(0)

    @pl.when(step == 0)
    def _():
        reorder(order_ref[...], own0_ref, held, 8, 0, 0)
        reorder(order_ref[...], own1_ref, held, 8, 0, LANES)

    rows = held[step]
    own_ref[0] = rows
    product = lax.dot_general(stacked(rows), rows, NT, preferred_element_type=jnp.float32) * (1.0 / SPECTRA)
    self_ref[0, 0] = product[:BLOCK]
    self_ref[1, 0] = product[BLOCK:]


def self_tiles(order, own0, own1):
    whole = lambda a: pl.BlockSpec(a.shape, lambda c: (0,) * a.ndim)
    return pl.pallas_call(
        self_kernel,
        grid=(8,),
        in_specs=[whole(order), whole(own0), whole(own1)],
        out_specs=[
            pl.BlockSpec((1, BLOCK, 2 * LANES), lambda c: (c, 0, 0)),
            pl.BlockSpec((2, 1, BLOCK, BLOCK), lambda c: (0, c, 0, 0)),
        ],
        out_shape=[
            jax.ShapeDtypeStruct((8, BLOCK, 2 * LANES), jnp.bfloat16),
            jax.ShapeDtypeStruct((2, 8, BLOCK, BLOCK), jnp.float32),
        ],
        scratch_shapes=[pltpu.VMEM((8, BLOCK, 2 * LANES), jnp.bfloat16)],
        compiler_params=pltpu.CompilerParams(vmem_limit_bytes=40 * 1024 * 1024),
        name="self_tiles",
    )(order, own0, own1)


def columns(place_ref, order, f_ref, g_ref, h_ref, s_ref, out_ref):
    chip = place_ref[0]

    @pl.when(place_ref[1] == 0)
    def _():
        reorder(order, f_ref, out_ref, 4, pl.multiple_of(chip * 128, 128), 0)
        reorder(order, g_ref, out_ref, 4, pl.multiple_of((1 - chip) * 128, 128), 0)

    @pl.when(place_ref[1] == 1)
    def _():
        reorder(order, h_ref, out_ref, 8, 0, 0)

    reorder(order, s_ref, out_ref, 4, BLOCK, 0)


def early_kernel(place_ref, order_ref, f_ref, g_ref, h_ref, s_ref, out_ref):
    columns(place_ref, order_ref[...], f_ref, g_ref, h_ref, s_ref, out_ref)


SMALL = pl.BlockSpec(memory_space=pltpu.SMEM)
IN_VMEM = pl.BlockSpec(memory_space=pltpu.VMEM)


def early_columns(place, order, *received):
    return pl.pallas_call(
        early_kernel,
        in_specs=[SMALL] + [IN_VMEM] * 5,
        out_specs=IN_VMEM,
        out_shape=jax.ShapeDtypeStruct((8, BLOCK + BLOCK // 2, LANES), jnp.bfloat16),
        compiler_params=pltpu.CompilerParams(vmem_limit_bytes=40 * 1024 * 1024),
        name="early_columns",
    )(place, order, *received)


def cross_kernel(place_ref, order_ref, own_ref, early_ref, f_ref, g_ref, h_ref, s_ref, prior_ref, far_ref, held):
    step = pl.program_id(0)

    @pl.when(step == 0)
    def _():
        columns(place_ref, order_ref[...], f_ref, g_ref, h_ref, s_ref, held)

    cols = jnp.concatenate([early_ref[0], held[step]], axis=1)
    product = lax.dot_general(stacked(own_ref[0]), cols, NT, preferred_element_type=jnp.float32) * (1.0 / SPECTRA)
    prior_ref[0, 0] = product[:BLOCK, :BLOCK]
    prior_ref[1, 0] = product[BLOCK:, :BLOCK]
    far_ref[0, 0] = product[:BLOCK, BLOCK:]
    far_ref[1, 0] = product[BLOCK:, BLOCK:]


def cross_tiles(place, order, own, early, *late):
    whole = lambda a: pl.BlockSpec(a.shape, lambda c: (0,) * a.ndim)
    channel = lambda a: pl.BlockSpec((1,) + a.shape[1:], lambda c: (c, 0, 0))
    return pl.pallas_call(
        cross_kernel,
        grid=(8,),
        in_specs=[SMALL, whole(order), channel(own), channel(early)] + [whole(a) for a in late],
        out_specs=[
            pl.BlockSpec((2, 1, BLOCK, BLOCK), lambda c: (0, c, 0, 0)),
            pl.BlockSpec((2, 1, BLOCK, BLOCK // 2), lambda c: (0, c, 0, 0)),
        ],
        out_shape=[
            jax.ShapeDtypeStruct((2, 8, BLOCK, BLOCK), jnp.float32),
            jax.ShapeDtypeStruct((2, 8, BLOCK, BLOCK // 2), jnp.float32),
        ],
        scratch_shapes=[pltpu.VMEM((8, BLOCK + BLOCK // 2, LANES), jnp.bfloat16)],
        compiler_params=pltpu.CompilerParams(vmem_limit_bytes=48 * 1024 * 1024),
        name="cross_tiles",
    )(place, order, own, early, *late)


CROSSED = [(0, 3), (1, 2), (2, 1), (3, 0)]
ODD_OVER = [(1, 2), (3, 0)]
EVEN_UP = [(0, 1), (2, 3)]
SWAPPED = [(0, 1), (1, 0), (2, 3), (3, 2)]


def on_device(table, order, samples, pfb_taps):
    position = lax.axis_index("narrow")
    chip = position // 2
    place = jnp.stack([chip, position % 2]).astype(jnp.int32)

    def turn(chunk):
        return lax.all_to_all(chunk, "wide", split_axis=0, concat_axis=0, tiled=True)

    def halves(own):
        shape = (32,) + own.shape[1:]
        return tuple(lax.dynamic_slice(own, (start * 32, 0, 0), shape) for start in (1 - chip, chip))

    def exchange(own, crossing, rest):
        f = lax.ppermute(crossing, "narrow", CROSSED)
        g = lax.ppermute(rest, "narrow", ODD_OVER)
        h = lax.ppermute(own, "narrow", EVEN_UP)
        return f, g, h

    def swap(f):
        return lax.ppermute(f, "narrow", SWAPPED)

    early = filter_section(samples, pfb_taps, table, 0)
    late = filter_section(samples, pfb_taps, table, HALF)
    own0 = turn(early)
    late, own0 = lax.optimization_barrier((late, own0))
    own1 = turn(late)
    received = exchange(own0, *halves(own0))
    held0 = early_columns(place, order, *received, swap(received[0]))
    own1, held0 = lax.optimization_barrier((own1, held0))
    crossing, rest = halves(own1)
    f, g, h = exchange(own1, crossing, rest)
    own1, crossing, rest = lax.optimization_barrier((own1, crossing, rest))
    mine, self_vis = self_tiles(order, own0, own1)
    f, mine = lax.optimization_barrier((f, mine))
    prior_vis, far_vis = cross_tiles(place, order, mine, held0, f, g, h, swap(f))
    return (self_vis, prior_vis, far_vis)


def solution(mesh):
    return jax.shard_map(
        functools.partial(on_device, dft_table(), row_order()),
        mesh=mesh,
        in_specs=(P(("narrow", "wide"), None), P()),
        out_specs=(
            P(None, "wide", "narrow", None),
            P(None, "wide", "narrow", None),
            P(None, "wide", "narrow", None),
        ),
        check_vma=False,
    )
```

time: 165 us -> 155 us (0.939); the launches traced: 162 us -> 155 us
  waiting for transfers between devices: 95.1 us -> 84.8 us
  Pallas kernels: 23.9 us -> 32.2 us
  local copies, waits for them, and re-layouts: 12.5 us -> 5.04 us
  starting transfers between devices: 29.5 us -> 31.6 us
    all_to_all x2, waiting for transfers between devices: 75.6 us -> 34.1 us  [turn(): lax.all_to_all(chunk, 'wide', split_axis=0, concat_axis=0, tiled=True)]
    ppermute x6 -> x8, waiting for transfers between devices: 19.6 us -> 50.7 us  [the longest x2 34.5 us: exchange(): f = lax.ppermute(crossing, 'narrow', CROSSED)]
    pallas_call x3 -> x4, Pallas kernels: 16 us -> 25.6 us  [the longest x2 12 us: filter_section(): pl.pallas_call(functools.partial(spectra_kernel, first), in_specs=[in_hbm...]
    unnamed x20 -> x10, local copies, waits for them, and re-layouts: 9.73 us -> 3.84 us
    ppermute x6 -> x8, starting transfers between devices: 10.6 us -> 13.1 us  [the longest x2 8.24 us: exchange(): h = lax.ppermute(own, 'narrow', EVEN_UP)]
  transfers between devices with their start and end apart: 8 -> 10, of which waited for: 4 -> 5; matrix products, arithmetic and copies ran while one was open for 2% -> 1% of each run, Pallas kernels for 6% -> 10%
where the time goes in v3:
time: 155 us
  waiting for transfers between devices  84.8 us (55%)
  Pallas kernels  32.2 us (21%)
  starting transfers between devices  31.6 us (20%)
  local copies, waits for them, and re-layouts  5.04 us (3%)
    ppermute x2, waiting for transfers between devices, exchange(): f = lax.ppermute(crossing, 'narrow', CROSSED)  34.5 us
    all_to_all x2, waiting for transfers between devices, turn(): lax.all_to_all(chunk, 'wide', split_axis=0, concat_axis=0, tiled=True)  34.1 us
    all_to_all x2, starting transfers between devices, turn(): lax.all_to_all(chunk, 'wide', split_axis=0, concat_axis=0, tiled=True)  18.6 us
    ppermute x2, waiting for transfers between devices, exchange(): g = lax.ppermute(rest, 'narrow', ODD_OVER)  16.2 us
    pallas_call x2, Pallas kernels, filter_section(): pl.pallas_call(functools.partial(spectra_kernel, first), in_specs=[in_hbm...  12 us
    pallas_call x1, Pallas kernels, cross_tiles(): pl.pallas_call(cross_kernel, grid=(8,), in_specs=[SMALL, whole(order), ch...  10.4 us
    ppermute x2, starting transfers between devices, exchange(): h = lax.ppermute(own, 'narrow', EVEN_UP)  8.24 us
    pallas_call x1, Pallas kernels, self_tiles(): pl.pallas_call(self_kernel, grid=(8,), in_specs=[whole(order), whole(own0...  6.52 us
  transfers between devices with their start and end apart: 10, of which 5 were waited for; matrix products, arithmetic and copies ran while one was open for 1% of the time, Pallas kernels for 10%

profile of v3, /device:TPU:24, one launch (start us, length us, event | category | flops | bytes accessed | tf_op | source)
XLA Modules:
  0.0 154.5 jit_solution(9836573981406497444)
XLA Ops:
  0.6 0.7 copy-done.3
  1.4 6.0 %filter_section.3 = bf16[64,32,384]{2,1,0:T(8,128)(2,1)} custom-call(bf16[4,396288]{1,0:T(4,128)(2,1)} %x_ref.3, bf16[1024,1024]{1,0:T(8,128)(2,1)} %constant.38.clone.table_ref, f32[4,1024]{1,0:T(4,128)S(1)} %copy-done.3), custom_call_target="tpu_custom_call" | custom-call | tf_op jit(solution)/shard_map/filter_section/pallas_call | solution.py:86
  7.4 12.8 %all-to-all-start = ((bf16[64,32,384]{2,1,0:T(8,128)(2,1)}), bf16[64,32,384]{2,1,0:T(8,128)(2,1)S(1)}, u32[]{:S(2)}, u32[]{:S(2)}) async-start(bf16[64,32,384]{2,1,0:T(8,128)(2,1)} %filter_section.3), calls=%async_computation | async-start | bytes 3145728 | tf_op jit(solution)/shard_map/all_to_all | solution.py:246
  20.2 6.0 %filter_section.2 = bf16[64,32,384]{2,1,0:T(8,128)(2,1)} custom-call(bf16[4,396288]{1,0:T(4,128)(2,1)} %x_ref.3, bf16[1024,1024]{1,0:T(8,128)(2,1)} %constant.38.clone.table_ref, f32[4,1024]{1,0:T(4,128)S(1)} %copy-done.4), custom_call_target="tpu_custom_call" | custom-call | tf_op jit(solution)/shard_map/filter_section/pallas_call | solution.py:86
  26.2 34.1 %all-to-all-done.own0_ref = bf16[64,32,384]{2,1,0:T(8,128)(2,1)S(1)} async-done(((bf16[64,32,384]{2,1,0:T(8,128)(2,1)}), bf16[64,32,384]{2,1,0:T(8,128)(2,1)S(1)}, u32[]{:S(2)}, u32[]{:S(2)}) %all-to-all-start) | async-done | bytes 1572896 | tf_op jit(solution)/shard_map/all_to_all | solution.py:246
  60.3 5.8 %all-to-all-start.1 = ((bf16[64,32,384]{2,1,0:T(8,128)(2,1)}), bf16[64,32,384]{2,1,0:T(8,128)(2,1)S(1)}, u32[]{:S(2)}, u32[]{:S(2)}) async-start(bf16[64,32,384]{2,1,0:T(8,128)(2,1)} %filter_section.2), calls=%async_computation.1 | async-start | bytes 3145728 | tf_op jit(solution)/shard_map/all_to_all | solution.py:246
  66.1 1.0 constant_dynamic-slice_fusion.2
  67.2 0.8 collective-permute-start
  68.0 5.2 %collective-permute-start.2 = (bf16[64,32,384]{2,1,0:T(8,128)(2,1)S(1)}, bf16[64,32,384]{2,1,0:T(8,128)(2,1)}, u32[]{:S(2)}, u32[]{:S(2)}) collective-permute-start(bf16[64,32,384]{2,1,0:T(8,128)(2,1)S(1)} %all-to-all-done.own0_ref), channel_id=1, source_target_pairs={{0,1},{2,3},{4,5},{6,7},{8,9},{10,11},{12,13},{14,15},{16,17},{18,... | collective-permute-start | bytes 4718600 | tf_op jit(solution)/shard_map/ppermute | solution.py:255
  73.1 1.3 collective-permute-start.1
  74.4 27.8 %collective-permute-done.f_ref = bf16[32,32,384]{2,1,0:T(8,128)(2,1)} collective-permute-done((bf16[32,32,384]{2,1,0:T(8,128)(2,1)S(1)}, bf16[32,32,384]{2,1,0:T(8,128)(2,1)}, u32[]{:S(2)}, u32[]{:S(2)}) %collective-permute-start) | collective-permute-done | bytes 786464 | tf_op jit(solution)/shard_map/ppermute | solution.py:253
  102.2 1.4 collective-permute-start.3
  103.7 7.8 %collective-permute-done.1.g_ref = bf16[32,32,384]{2,1,0:T(8,128)(2,1)} collective-permute-done((bf16[32,32,384]{2,1,0:T(8,128)(2,1)}, bf16[32,32,384]{2,1,0:T(8,128)(2,1)}, u32[]{:S(2)}, u32[]{:S(2)}) %collective-permute-start.1) | collective-permute-done | bytes 786464 | tf_op jit(solution)/shard_map/ppermute | solution.py:254
  111.5 3.2 %early_columns.1.early_ref = bf16[8,384,384]{2,1,0:T(8,128)(2,1)S(1)} custom-call(s32[2]{0:T(128)S(1)} %pad_add_fusion.place_ref, bf16[256,256]{1,0:T(8,128)(2,1)S(1)} %copy-done.2, bf16[32,32,384]{2,1,0:T(8,128)(2,1)} %collective-permute-done.f_ref, bf16[32,32,384]{2,1,0:T(8,128)(2,1)} %collective-permute-done.1.g_ref, ...), custom_call_target="tpu_custom_call" | custom-call | tf_op jit(solution)/shard_map/early_columns/pallas_call | solution.py:188
  114.7 1.5 copy-done
  116.2 0.2 constant_dynamic-slice_fusion
  116.4 0.1 collective-permute-start.4
  116.5 3.1 %collective-permute-start.6 = (bf16[64,32,384]{2,1,0:T(8,128)(2,1)S(1)}, bf16[64,32,384]{2,1,0:T(8,128)(2,1)S(1)}, u32[]{:S(2)}, u32[]{:S(2)}) collective-permute-start(bf16[64,32,384]{2,1,0:T(8,128)(2,1)S(1)} %all-to-all-done.1.own1_ref), channel_id=1, source_target_pairs={{0,1},{2,3},{4,5},{6,7},{8,9},{10,11},{12,13},{14,15},{16,17},{18,... | collective-permute-start | bytes 4718600 | tf_op jit(solution)/shard_map/ppermute | solution.py:255
  119.6 1.3 collective-permute-start.5
  120.9 6.5 %self_tiles.1 = (bf16[8,256,768]{2,1,0:T(8,128)(2,1)S(1)}, f32[2,8,256,256]{3,2,1,0:T(8,128)}) custom-call(bf16[256,256]{1,0:T(8,128)(2,1)S(1)} %copy-done.2, bf16[64,32,384]{2,1,0:T(8,128)(2,1)S(1)} %all-to-all-done.own0_ref, bf16[64,32,384]{2,1,0:T(8,128)(2,1)S(1)} %all-to-all-done.1.own1_ref), custom_call_target="tpu_custom_call" | custom-call | tf_op jit(solution)/shard_map/self_tiles/pallas_call | solution.py:146
  127.4 1.7 %copy-done.1 = bf16[8,256,768]{2,1,0:T(8,128)(2,1)} copy-done((bf16[8,256,768]{2,1,0:T(8,128)(2,1)}, bf16[8,256,768]{2,1,0:T(8,128)(2,1)S(1)}, u32[]{:S(2)}) %copy-start.1) | copy-done | bytes 3145752
  129.0 6.6 %collective-permute-done.4.f_ref = bf16[32,32,384]{2,1,0:T(8,128)(2,1)S(1)} collective-permute-done((bf16[32,32,384]{2,1,0:T(8,128)(2,1)S(1)}, bf16[32,32,384]{2,1,0:T(8,128)(2,1)S(1)}, u32[]{:S(2)}, u32[]{:S(2)}) %collective-permute-start.4) | collective-permute-done | bytes 786464 | tf_op jit(solution)/shard_map/ppermute | solution.py:253
  135.7 8.4 %collective-permute-done.5.g_ref = bf16[32,32,384]{2,1,0:T(8,128)(2,1)S(1)} collective-permute-done((bf16[32,32,384]{2,1,0:T(8,128)(2,1)S(1)}, bf16[32,32,384]{2,1,0:T(8,128)(2,1)S(1)}, u32[]{:S(2)}, u32[]{:S(2)}) %collective-permute-start.5) | collective-permute-done | bytes 786464 | tf_op jit(solution)/shard_map/ppermute | solution.py:254
  144.1 10.4 %cross_tiles.1 = (f32[2,8,256,256]{3,2,1,0:T(8,128)}, f32[2,8,256,128]{3,2,1,0:T(8,128)}) custom-call(s32[2]{0:T(128)S(1)} %pad_add_fusion.place_ref, bf16[256,256]{1,0:T(8,128)(2,1)S(1)} %copy-done.2, bf16[8,256,768]{2,1,0:T(8,128)(2,1)} %copy-done.1, bf16[8,384,384]{2,1,0:T(8,128)(2,1)} %copy-done, bf16[32,32,384]{2,1,0:T(8,128)(2,1)S(1)} %collective-permute-done.4.f_ref, ...), custom_call_target="tpu_custom_call" | custom-call | tf_op jit(solution)/shard_map/cross_tiles/pallas_call | solution.py:216
  (14 shorter events, 0.1 us)
Async XLA Ops:
  0.6 0.7 copy-start.3
  7.4 12.8 %copy-start.4 = (f32[4,1024]{1,0:T(4,128)S(1)}, f32[4,1024]{1,0:T(4,128)}, u32[]{:S(2)}) copy-start(f32[4,1024]{1,0:T(4,128)} %taps_ref.3) | copy-start | bytes 49156
  7.4 53.0 %all-to-all-start = ((bf16[64,32,384]{2,1,0:T(8,128)(2,1)}), bf16[64,32,384]{2,1,0:T(8,128)(2,1)S(1)}, u32[]{:S(2)}, u32[]{:S(2)}) async-start(bf16[64,32,384]{2,1,0:T(8,128)(2,1)} %filter_section.3), calls=%async_computation | async-start | bytes 3145728 | tf_op jit(solution)/shard_map/all_to_all | solution.py:246
  60.3 55.8 %all-to-all-start.1 = ((bf16[64,32,384]{2,1,0:T(8,128)(2,1)}), bf16[64,32,384]{2,1,0:T(8,128)(2,1)S(1)}, u32[]{:S(2)}, u32[]{:S(2)}) async-start(bf16[64,32,384]{2,1,0:T(8,128)(2,1)} %filter_section.2), calls=%async_computation.1 | async-start | bytes 3145728 | tf_op jit(solution)/shard_map/all_to_all | solution.py:246
  66.1 45.4 %copy-start.2 = (bf16[256,256]{1,0:T(8,128)(2,1)S(1)}, bf16[256,256]{1,0:T(8,128)(2,1)}, u32[]{:S(2)}) copy-start(bf16[256,256]{1,0:T(8,128)(2,1)} %constant.39.clone.order_ref) | copy-start | bytes 393220
  67.2 35.0 %collective-permute-start = (bf16[32,32,384]{2,1,0:T(8,128)(2,1)S(1)}, bf16[32,32,384]{2,1,0:T(8,128)(2,1)}, u32[]{:S(2)}, u32[]{:S(2)}) collective-permute-start(bf16[32,32,384]{2,1,0:T(8,128)(2,1)S(1)} %get-tuple-element.28), channel_id=1, source_target_pairs={{0,3},{1,2},{2,1},{3,0},{4,7},{5,6},{6,5},{7,4},{8,11},{9,10},{10,... | collective-permute-start | bytes 2359304 | tf_op jit(solution)/shard_map/ppermute | solution.py:253
  68.0 43.5 %collective-permute-start.2 = (bf16[64,32,384]{2,1,0:T(8,128)(2,1)S(1)}, bf16[64,32,384]{2,1,0:T(8,128)(2,1)}, u32[]{:S(2)}, u32[]{:S(2)}) collective-permute-start(bf16[64,32,384]{2,1,0:T(8,128)(2,1)S(1)} %all-to-all-done.own0_ref), channel_id=1, source_target_pairs={{0,1},{2,3},{4,5},{6,7},{8,9},{10,11},{12,13},{14,15},{16,17},{18,... | collective-permute-start | bytes 4718600 | tf_op jit(solution)/shard_map/ppermute | solution.py:255
  73.1 38.4 %collective-permute-start.1 = (bf16[32,32,384]{2,1,0:T(8,128)(2,1)}, bf16[32,32,384]{2,1,0:T(8,128)(2,1)}, u32[]{:S(2)}, u32[]{:S(2)}) collective-permute-start(bf16[32,32,384]{2,1,0:T(8,128)(2,1)} %get-tuple-element.27), channel_id=1, source_target_pairs={{1,2},{3,0},{5,6},{7,4},{9,10},{11,8},{13,14},{15,12},{17,18},{19,... | collective-permute-start | bytes 2359304 | tf_op jit(solution)/shard_map/ppermute | solution.py:254
  102.2 9.3 %collective-permute-start.3 = (bf16[32,32,384]{2,1,0:T(8,128)(2,1)}, bf16[32,32,384]{2,1,0:T(8,128)(2,1)}, u32[]{:S(2)}, u32[]{:S(2)}) collective-permute-start(bf16[32,32,384]{2,1,0:T(8,128)(2,1)} %collective-permute-done.f_ref), channel_id=1, source_target_pairs={{0,1},{1,0},{2,3},{3,2},{4,5},{5,4},{6,7},{7,6},{8,9},{9,8},{10,11... | collective-permute-start | bytes 2359304 | tf_op jit(solution)/shard_map/ppermute | solution.py:259
  114.7 1.5 copy-start
  116.4 19.3 %collective-permute-start.4 = (bf16[32,32,384]{2,1,0:T(8,128)(2,1)S(1)}, bf16[32,32,384]{2,1,0:T(8,128)(2,1)S(1)}, u32[]{:S(2)}, u32[]{:S(2)}) collective-permute-start(bf16[32,32,384]{2,1,0:T(8,128)(2,1)S(1)} %get-tuple-element.26), channel_id=1, source_target_pairs={{0,3},{1,2},{2,1},{3,0},{4,7},{5,6},{6,5},{7,4},{8,11},{9,10},{10,... | collective-permute-start | bytes 2359304 | tf_op jit(solution)/shard_map/ppermute | solution.py:253
  116.5 27.6 %collective-permute-start.6 = (bf16[64,32,384]{2,1,0:T(8,128)(2,1)S(1)}, bf16[64,32,384]{2,1,0:T(8,128)(2,1)S(1)}, u32[]{:S(2)}, u32[]{:S(2)}) collective-permute-start(bf16[64,32,384]{2,1,0:T(8,128)(2,1)S(1)} %all-to-all-done.1.own1_ref), channel_id=1, source_target_pairs={{0,1},{2,3},{4,5},{6,7},{8,9},{10,11},{12,13},{14,15},{16,17},{18,... | collective-permute-start | bytes 4718600 | tf_op jit(solution)/shard_map/ppermute | solution.py:255
  119.6 24.5 %collective-permute-start.5 = (bf16[32,32,384]{2,1,0:T(8,128)(2,1)S(1)}, bf16[32,32,384]{2,1,0:T(8,128)(2,1)S(1)}, u32[]{:S(2)}, u32[]{:S(2)}) collective-permute-start(bf16[32,32,384]{2,1,0:T(8,128)(2,1)S(1)} %get-tuple-element.25), channel_id=1, source_target_pairs={{1,2},{3,0},{5,6},{7,4},{9,10},{11,8},{13,14},{15,12},{17,18},{19,... | collective-permute-start | bytes 2359304 | tf_op jit(solution)/shard_map/ppermute | solution.py:254
  127.4 1.7 %copy-start.1 = (bf16[8,256,768]{2,1,0:T(8,128)(2,1)}, bf16[8,256,768]{2,1,0:T(8,128)(2,1)S(1)}, u32[]{:S(2)}) copy-start(bf16[8,256,768]{2,1,0:T(8,128)(2,1)S(1)} %get-tuple-element.20.own_ref) | copy-start | bytes 9437188
  135.7 8.4 %collective-permute-start.7 = (bf16[32,32,384]{2,1,0:T(8,128)(2,1)S(1)}, bf16[32,32,384]{2,1,0:T(8,128)(2,1)S(1)}, u32[]{:S(2)}, u32[]{:S(2)}) collective-permute-start(bf16[32,32,384]{2,1,0:T(8,128)(2,1)S(1)} %collective-permute-done.4.f_ref), channel_id=1, source_target_pairs={{0,1},{1,0},{2,3},{3,2},{4,5},{5,4},{6,7},{7,6},{8,9},{9,8},{10,11... | collective-permute-start | bytes 2359304 | tf_op jit(solution)/shard_map/ppermute | solution.py:259

commit v4 on v3

v4 whole, which is shorter than its diff:
```python
import functools
import math

import jax
import jax.numpy as jnp
import numpy as np
from jax import lax
from jax.experimental import pallas as pl
from jax.experimental.pallas import tpu as pltpu
from jax.sharding import Mesh
from jax.sharding import PartitionSpec as P

CHAN = 512
TAPS = 4
SPECTRA = 384
BLOCK = 256
FRAME = 2 * CHAN
HALF = SPECTRA // 2
LANES = 2 * HALF
NT = (((1,), (1,)), ((), ()))
SMALL = pl.BlockSpec(memory_space=pltpu.SMEM)
IN_VMEM = pl.BlockSpec(memory_space=pltpu.VMEM)


def dft_table():
    positions = np.arange(FRAME, dtype=np.int32)
    bins = np.arange(CHAN, dtype=np.int32)
    phases = bins[:, None] * positions[None, :] % FRAME
    angles = phases.astype(np.float32) * np.float32(math.pi / CHAN)
    norming = np.float32(FRAME ** (-0.5))
    table = np.concatenate([np.cos(angles) * norming, -np.sin(angles) * norming])
    return table.astype(jnp.bfloat16)


def row_order():
    order = np.arange(256).reshape(32, 8).T.reshape(-1)
    return np.eye(256, dtype=np.float32)[order].astype(jnp.bfloat16)


PIECES = 3


def spectra_kernel(first, split, place_ref, x_ref, table_ref, taps_ref, *refs):
    outs, (x_held, table, taps_held, frames, filtered, out_held, x_sem, table_sem, taps_sem, out_sem) = refs[:-10], refs[-10:]
    step = (HALF + TAPS - 1) // PIECES
    arriving = [
        pltpu.make_async_copy(
            x_ref.at[:, pl.ds((first + j * step) * FRAME, step * FRAME)], x_held.at[j], x_sem.at[j]
        )
        for j in range(PIECES)
    ]
    table_arriving = pltpu.make_async_copy(table_ref, table, table_sem)
    taps_arriving = pltpu.make_async_copy(taps_ref, taps_held, taps_sem)
    arriving[0].start()
    taps_arriving.start()
    for copy in arriving[1:]:
        copy.start()
    table_arriving.start()
    for j in range(PIECES):
        arriving[j].wait()
        for f in range(step):
            for n in range(0, FRAME, 128):
                frames[n // 128, 4 * (j * step + f) : 4 * (j * step + f) + 4, :] = x_held[
                    j, :, f * FRAME + n : f * FRAME + n + 128
                ].astype(jnp.float32)
    taps_arriving.wait()
    for n in range(0, FRAME, 128):
        taps = [taps_held[t : t + 1, n : n + 128] for t in range(TAPS)]
        for i in range(4):
            for s in range(0, HALF, 16):
                total = frames[n // 128, pl.ds(i + 4 * s, 16, stride=4), :] * taps[0]
                for t in range(1, TAPS):
                    total = total + frames[n // 128, pl.ds(i + 4 * (s + t), 16, stride=4), :] * taps[t]
                row = i * 128 + s if s < 128 else 512 + i * 64 + s - 128
                filtered[row : row + 16, n : n + 128] = total.astype(jnp.bfloat16)
    table_arriving.wait()

    def transform(row):
        return lax.dot_general(table[...], filtered[row : row + 256, :], NT, preferred_element_type=jnp.float32)

    def put(pair, lane, even, odd):
        rows = jnp.concatenate([even.reshape(CHAN // 8, 8, 128), odd.reshape(CHAN // 8, 8, 128)], axis=1)
        out_held[:, pair * 16 : pair * 16 + 16, lane : lane + 128] = rows.astype(jnp.bfloat16)

    for pair in range(2):
        product = transform(pair * 256)
        for p in range(2):
            part = product[p * CHAN : (p + 1) * CHAN]
            put(pair, p * 128, part[:, :128], part[:, 128:])
    product = transform(512)
    low = lax.broadcasted_iota(jnp.int32, (CHAN, 128), 1) < 64
    for pair in range(2):
        real = product[:CHAN, pair * 128 : (pair + 1) * 128]
        imag = product[CHAN:, pair * 128 : (pair + 1) * 128]
        put(
            pair, 256, jnp.where(low, real, pltpu.roll(imag, 64, 1)), jnp.where(low, pltpu.roll(real, 64, 1), imag)
        )
    if split:
        side = place_ref[2]
        sources = [out_held.at[pl.ds(side * 32, 32)], out_held.at[pl.ds((1 - side) * 32, 32)]]
    else:
        sources = [out_held]
    leaving = [pltpu.make_async_copy(source, out, out_sem.at[j]) for j, (source, out) in enumerate(zip(sources, outs))]
    for copy in leaving:
        copy.start()
    for copy in leaving:
        copy.wait()


def filter_section(place, samples, pfb_taps, table, first, split):
    in_hbm = pl.BlockSpec(memory_space=pltpu.HBM)
    out_shape = [pltpu.HBM((32, 32, LANES), jnp.bfloat16)] * 2 if split else [pltpu.HBM((64, 32, LANES), jnp.bfloat16)]
    return pl.pallas_call(
        functools.partial(spectra_kernel, first, split),
        in_specs=[SMALL, in_hbm, in_hbm, in_hbm],
        out_specs=[in_hbm] * len(out_shape),
        out_shape=out_shape,
        scratch_shapes=[
            pltpu.VMEM((PIECES, 4, (HALF + TAPS - 1) // PIECES * FRAME), jnp.bfloat16),
            pltpu.VMEM((2 * CHAN, FRAME), jnp.bfloat16),
            pltpu.VMEM((TAPS, FRAME), jnp.float32),
            pltpu.VMEM((FRAME // 128, 4 * (HALF + 4), 128), jnp.float32),
            pltpu.VMEM((4 * HALF, FRAME), jnp.bfloat16),
            pltpu.VMEM((64, 32, LANES), jnp.bfloat16),
            pltpu.SemaphoreType.DMA((PIECES,)),
            pltpu.SemaphoreType.DMA,
            pltpu.SemaphoreType.DMA,
            pltpu.SemaphoreType.DMA((2,)),
        ],
        compiler_params=pltpu.CompilerParams(vmem_limit_bytes=40 * 1024 * 1024),
        name="filter_section",
    )(place, *(pltpu.with_memory_space_constraint(a, pltpu.HBM) for a in (samples, table, pfb_taps)))


def merge_kernel(place_ref, stay_ref, got_ref, out_ref, sem):
    side = place_ref[2]
    copies = [
        pltpu.make_async_copy(stay_ref, out_ref.at[:, side], sem.at[0]),
        pltpu.make_async_copy(got_ref, out_ref.at[:, 1 - side], sem.at[1]),
    ]
    for copy in copies:
        copy.start()
    for copy in copies:
        copy.wait()


def merge(place, stay, got):
    in_hbm = pl.BlockSpec(memory_space=pltpu.HBM)
    return pl.pallas_call(
        merge_kernel,
        in_specs=[SMALL, in_hbm, in_hbm],
        out_specs=in_hbm,
        out_shape=pltpu.HBM((32, 2, 32, LANES), jnp.bfloat16),
        scratch_shapes=[pltpu.SemaphoreType.DMA((2,))],
        name="merge_sides",
    )(place, *(pltpu.with_memory_space_constraint(a, pltpu.HBM) for a in (stay, got)))


def rows_kernel(place_ref, order_ref, source_ref, cross_ref, rest_ref, whole_ref):
    chip = place_ref[0]
    order = order_ref[...]
    for out_ref, half in ((cross_ref, 1 - chip), (rest_ref, chip)):
        for g in range(4):
            if len(source_ref.shape) == 3:
                rows = source_ref[pl.ds(half * 32 + g * 8, 8)]
            else:
                rows = source_ref[g * 8 : (g + 1) * 8, half]
            turned = jnp.dot(order, rows.reshape(256, LANES), preferred_element_type=jnp.float32).astype(jnp.bfloat16)
            for c in range(8):
                part = turned[c * 32 : (c + 1) * 32]
                out_ref[c, g * 32 : (g + 1) * 32, :] = part
                whole_ref[c, pl.ds(pl.multiple_of(half * 128 + g * 32, 32), 32), :] = part


def channel_rows(place, order, source):
    shapes = [(8, 128, LANES), (8, 128, LANES), (8, BLOCK, LANES)]
    return pl.pallas_call(
        rows_kernel,
        in_specs=[SMALL, IN_VMEM, IN_VMEM],
        out_specs=[IN_VMEM] * 3,
        out_shape=[jax.ShapeDtypeStruct(shape, jnp.bfloat16) for shape in shapes],
        compiler_params=pltpu.CompilerParams(vmem_limit_bytes=40 * 1024 * 1024),
        name="channel_rows",
    )(place, order, source)


def stacked(rows):
    low = lax.broadcasted_iota(jnp.int32, (rows.shape[0], 128), 1) < 64
    pieces = []
    for s in range(0, rows.shape[1], LANES):
        mixed = pltpu.roll(rows[:, s + 256 : s + 384].astype(jnp.float32), 64, 1)
        mixed = jnp.where(low, mixed, -mixed).astype(jnp.bfloat16)
        pieces += [rows[:, s + 128 : s + 256], -rows[:, s : s + 128], mixed]
    return jnp.concatenate([rows, jnp.concatenate(pieces, axis=1)], axis=0)


def tile_products(rows, cols):
    return lax.dot_general(stacked(rows), cols, NT, preferred_element_type=jnp.float32) * (1.0 / SPECTRA)


def self_kernel(own0_ref, own1_ref, self_ref, self_held, sem):
    copies = []
    for c in range(8):
        rows = jnp.concatenate([own0_ref[c], own1_ref[c]], axis=1)
        product = tile_products(rows, rows)
        self_held[0, c] = product[:BLOCK]
        self_held[1, c] = product[BLOCK:]
        copies.append(pltpu.make_async_copy(self_held.at[:, c], self_ref.at[:, c], sem.at[c]))
        copies[-1].start()
    for copy in copies:
        copy.wait()


def self_tiles(own0, own1):
    return pl.pallas_call(
        self_kernel,
        in_specs=[IN_VMEM] * 2,
        out_specs=pl.BlockSpec(memory_space=pltpu.HBM),
        out_shape=pltpu.HBM((2, 8, BLOCK, BLOCK), jnp.float32),
        scratch_shapes=[pltpu.VMEM((2, 8, BLOCK, BLOCK), jnp.float32), pltpu.SemaphoreType.DMA((8,))],
        compiler_params=pltpu.CompilerParams(vmem_limit_bytes=40 * 1024 * 1024),
        name="self_tiles",
    )(own0, own1)


def put_columns(place_ref, f_ref, g_ref, h_ref, s_ref, out_ref, lane):
    chip = place_ref[0]
    lanes = slice(lane, lane + LANES)

    @pl.when(place_ref[1] == 0)
    def _():
        out_ref[:, pl.ds(pl.multiple_of(chip * 128, 128), 128), lanes] = f_ref[...]
        out_ref[:, pl.ds(pl.multiple_of((1 - chip) * 128, 128), 128), lanes] = g_ref[...]

    @pl.when(place_ref[1] == 1)
    def _():
        out_ref[:, :BLOCK, lanes] = h_ref[...]

    out_ref[:, BLOCK:, lanes] = s_ref[...]


def early_kernel(place_ref, f_ref, g_ref, h_ref, s_ref, out_ref):
    put_columns(place_ref, f_ref, g_ref, h_ref, s_ref, out_ref, 0)


def early_columns(place, *received):
    return pl.pallas_call(
        early_kernel,
        in_specs=[SMALL] + [IN_VMEM] * 4,
        out_specs=IN_VMEM,
        out_shape=jax.ShapeDtypeStruct((8, BLOCK + BLOCK // 2, LANES), jnp.bfloat16),
        compiler_params=pltpu.CompilerParams(vmem_limit_bytes=40 * 1024 * 1024),
        name="early_columns",
    )(place, *received)


def cross_kernel(place_ref, own0_ref, own1_ref, early_ref, f_ref, g_ref, h_ref, s_ref, prior_ref, far_ref,
                 held, prior_held, far_held, prior_sem, far_sem):
    put_columns(place_ref, f_ref, g_ref, h_ref, s_ref, held, 0)
    copies = []
    for c in range(8):
        rows = jnp.concatenate([own0_ref[c], own1_ref[c]], axis=1)
        product = tile_products(rows, jnp.concatenate([early_ref[c], held[c]], axis=1))
        for p in range(2):
            prior_held[p, c] = product[p * BLOCK : (p + 1) * BLOCK, :BLOCK]
            far_held[p, c] = product[p * BLOCK : (p + 1) * BLOCK, BLOCK:]
        copies.append(pltpu.make_async_copy(prior_held.at[:, c], prior_ref.at[:, c], prior_sem.at[c]))
        copies.append(pltpu.make_async_copy(far_held.at[:, c], far_ref.at[:, c], far_sem.at[c]))
        copies[-2].start()
        copies[-1].start()
    for copy in copies:
        copy.wait()


def cross_tiles(place, own0, own1, early, *late):
    in_hbm = pl.BlockSpec(memory_space=pltpu.HBM)
    prior_shape, far_shape = (2, 8, BLOCK, BLOCK), (2, 8, BLOCK, BLOCK // 2)
    return pl.pallas_call(
        cross_kernel,
        in_specs=[SMALL] + [IN_VMEM] * (3 + len(late)),
        out_specs=[in_hbm, in_hbm],
        out_shape=[pltpu.HBM(prior_shape, jnp.float32), pltpu.HBM(far_shape, jnp.float32)],
        scratch_shapes=[
            pltpu.VMEM((8, BLOCK + BLOCK // 2, LANES), jnp.bfloat16),
            pltpu.VMEM(prior_shape, jnp.float32),
            pltpu.VMEM(far_shape, jnp.float32),
            pltpu.SemaphoreType.DMA((8,)),
            pltpu.SemaphoreType.DMA((8,)),
        ],
        compiler_params=pltpu.CompilerParams(vmem_limit_bytes=40 * 1024 * 1024),
        name="cross_tiles",
    )(place, own0, own1, early, *late)


CROSSED = [(0, 3), (1, 2), (2, 1), (3, 0)]
ODD_OVER = [(1, 2), (3, 0)]
EVEN_UP = [(0, 1), (2, 3)]
SWAPPED = [(0, 1), (1, 0), (2, 3), (3, 2)]


def on_device(table, order, samples, pfb_taps):
    position = lax.axis_index("narrow")
    place = jnp.stack([position // 2, position % 2, lax.axis_index("side")]).astype(jnp.int32)

    def exchange(crossing, rest, whole):
        f = lax.ppermute(crossing, "narrow", CROSSED)
        g = lax.ppermute(rest, "narrow", ODD_OVER)
        h = lax.ppermute(whole, "narrow", EVEN_UP)
        return f, g, h

    def swap(f):
        return lax.ppermute(f, "narrow", SWAPPED)

    (early,) = filter_section(place, samples, pfb_taps, table, 0, False)
    stay, leave = filter_section(place, samples, pfb_taps, table, HALF, True)
    source0 = lax.all_to_all(early, ("side", "plane"), split_axis=0, concat_axis=0, tiled=True)
    late = merge(place, stay, lax.ppermute(leave, "side", [(0, 1), (1, 0)]))
    late, source0 = lax.optimization_barrier((late, source0))
    source1 = lax.all_to_all(late, "plane", split_axis=0, concat_axis=0, tiled=True)
    crossing0, rest0, own0 = channel_rows(place, order, source0)
    f, g, h = exchange(crossing0, rest0, own0)
    held0 = early_columns(place, f, g, h, swap(f))
    source1, held0 = lax.optimization_barrier((source1, held0))
    crossing1, rest1, own1 = channel_rows(place, order, source1)
    f, g, h = exchange(crossing1, rest1, own1)
    self_vis = self_tiles(own0, own1)
    f, self_vis = lax.optimization_barrier((f, self_vis))
    prior_vis, far_vis = cross_tiles(place, own0, own1, held0, f, g, h, swap(f))
    return (self_vis, prior_vis, far_vis)


def solution(mesh):
    parted = Mesh(mesh.devices.reshape(2, mesh.devices.shape[0] // 2, mesh.devices.shape[1]), ("side", "plane", "narrow"))
    out_spec = P(None, ("side", "plane"), "narrow", None)
    return jax.shard_map(
        functools.partial(on_device, dft_table(), row_order()),
        mesh=parted,
        in_specs=(P(("narrow", "side", "plane"), None), P()),
        out_specs=(out_spec, out_spec, out_spec),
        check_vma=False,
    )
```

time: 155 us -> 194 us (1.25)
  Pallas kernels: 32.2 us -> 74.7 us
  waiting for transfers between devices: 84.8 us -> 79.6 us
  starting transfers between devices: 31.6 us -> 36.1 us
  local copies, waits for them, and re-layouts: 5.04 us -> 2.05 us
    pallas_call x5 -> x8, Pallas kernels: 32.2 us -> 74.7 us  [the longest x1 49.4 us: merge(): pl.pallas_call(merge_kernel, in_specs=[SMALL, in_hbm, in_hbm], out_specs=...]
    ppermute x2 -> x3, waiting for transfers between devices: 0.01 us -> 29.9 us  [the longest x1 29.9 us: on_device(): late = merge(place, stay, lax.ppermute(leave, 'side', [(0, 1), (1, 0)]))]
    all_to_all x2, waiting for transfers between devices: 34.1 us -> 7.2 us  [the longest x1 7.2 us: on_device(): lax.all_to_all(late, 'plane', split_axis=0, concat_axis=0, tiled=True)]
    ppermute x2, waiting for transfers between devices: 34.5 us -> 25.6 us  [exchange(): f = lax.ppermute(crossing, 'narrow', CROSSED)]
    all_to_all x2, starting transfers between devices: 18.6 us -> 21.8 us  [the longest x1 12.8 us: on_device(): lax.all_to_all(early, ('side', 'plane'), split_axis=0, concat_axis=0, til...]
    ppermute x2 -> x3, starting transfers between devices: 8.24 us -> 10.1 us  [the longest x2 8.47 us: exchange(): h = lax.ppermute(whole, 'narrow', EVEN_UP)]
  transfers between devices with their start and end apart: 10 -> 11, of which waited for: 5 -> 6; matrix products, arithmetic and copies ran while one was open for 1% -> 0% of each run, Pallas kernels for 10% -> 31%
where the time goes in v4:
time: 194 us; the launch traced here: 193 us
  waiting for transfers between devices  79.6 us (41%)
  Pallas kernels  74.7 us (39%)
  starting transfers between devices  36.1 us (19%)
  local copies, waits for them, and re-layouts  2.05 us (1%)
    pallas_call x1, Pallas kernels, merge(): pl.pallas_call(merge_kernel, in_specs=[SMALL, in_hbm, in_hbm], out_specs=...  49.4 us
    ppermute x1, waiting for transfers between devices, on_device(): late = merge(place, stay, lax.ppermute(leave, 'side', [(0, 1), (1, 0)]))  29.9 us
    ppermute x2, waiting for transfers between devices, exchange(): f = lax.ppermute(crossing, 'narrow', CROSSED)  25.6 us
    ppermute x2, waiting for transfers between devices, exchange(): g = lax.ppermute(rest, 'narrow', ODD_OVER)  16.8 us
    pallas_call x2, Pallas kernels, filter_section(): pl.pallas_call(functools.partial(spectra_kernel, first, split), in_specs=...  12.8 us
    all_to_all x1, starting transfers between devices, on_device(): lax.all_to_all(early, ('side', 'plane'), split_axis=0, concat_axis=0, til...  12.8 us
    all_to_all x1, starting transfers between devices, on_device(): lax.all_to_all(late, 'plane', split_axis=0, concat_axis=0, tiled=True)  9.02 us
    ppermute x2, starting transfers between devices, exchange(): h = lax.ppermute(whole, 'narrow', EVEN_UP)  8.47 us
  transfers between devices with their start and end apart: 11, of which 6 were waited for; matrix products, arithmetic and copies ran while one was open for 0% of the time, Pallas kernels for 31%

profile of v4, /device:TPU:24, one launch (start us, length us, event | category | flops | bytes accessed | tf_op | source)
XLA Modules:
  0.0 193.5 jit_solution(952319258877281481)
XLA Ops:
  0.7 6.4 %filter_section.3 = bf16[64,32,384]{2,1,0:T(8,128)(2,1)} custom-call(s32[3]{0:T(128)S(1)} %pad_add_fusion.place_ref, bf16[4,396288]{1,0:T(4,128)(2,1)} %x_ref.3, bf16[1024,1024]{1,0:T(8,128)(2,1)} %constant.38.clone.table_ref, f32[4,1024]{1,0:T(4,128)} %taps_ref.3), custom_call_target="tpu_custom_call" | custom-call | tf_op jit(solution)/shard_map/filter_section/pallas_call | solution.py:113
  7.2 12.8 %all-to-all-start = ((bf16[64,32,384]{2,1,0:T(8,128)(2,1)}), bf16[64,32,384]{2,1,0:T(8,128)(2,1)S(1)}, u32[]{:S(2)}, u32[]{:S(2)}) async-start(bf16[64,32,384]{2,1,0:T(8,128)(2,1)} %filter_section.3), calls=%async_computation | async-start | bytes 3145728 | tf_op jit(solution)/shard_map/all_to_all | solution.py:316
  20.0 6.4 %filter_section.2 = (bf16[32,32,384]{2,1,0:T(8,128)(2,1)}, bf16[32,32,384]{2,1,0:T(8,128)(2,1)}) custom-call(s32[3]{0:T(128)S(1)} %pad_add_fusion.place_ref, bf16[4,396288]{1,0:T(4,128)(2,1)} %x_ref.3, bf16[1024,1024]{1,0:T(8,128)(2,1)} %constant.38.clone.table_ref, f32[4,1024]{1,0:T(4,128)} %taps_ref.3), custom_call_target="tpu_custom_call" | custom-call | tf_op jit(solution)/shard_map/filter_section/pallas_call | solution.py:113
  26.4 1.7 collective-permute-start
  28.1 29.9 %collective-permute-done.got_ref = bf16[32,32,384]{2,1,0:T(8,128)(2,1)S(1)} collective-permute-done((bf16[32,32,384]{2,1,0:T(8,128)(2,1)}, bf16[32,32,384]{2,1,0:T(8,128)(2,1)S(1)}, u32[]{:S(2)}, u32[]{:S(2)}) %collective-permute-start) | collective-permute-done | bytes 786464 | tf_op jit(solution)/shard_map/ppermute | solution.py:317
  58.0 0.9 copy-done.5
  58.9 49.4 %merge_sides.1 = bf16[32,2,32,384]{3,2,1,0:T(8,128)(2,1)} custom-call(s32[3]{0:T(128)} %copy-done.3, bf16[32,32,384]{2,1,0:T(8,128)(2,1)} %get-tuple-element.19.stay_ref, bf16[32,32,384]{2,1,0:T(8,128)(2,1)} %copy-done.5), custom_call_target="tpu_custom_call" | custom-call | tf_op jit(solution)/shard_map/merge_sides/pallas_call | solution.py:149
  108.4 9.0 %all-to-all-start.1 = ((bf16[32,2,32,384]{3,2,1,0:T(8,128)(2,1)}), bf16[32,2,32,384]{3,2,1,0:T(8,128)(2,1)}, u32[]{:S(2)}, u32[]{:S(2)}) async-start(bf16[32,2,32,384]{3,2,1,0:T(8,128)(2,1)} %merge_sides.1), calls=%async_computation.1 | async-start | bytes 3145728 | tf_op jit(solution)/shard_map/all_to_all | solution.py:319
  117.4 1.2 channel_rows.2
  118.7 1.2 collective-permute-start.1
  119.9 3.7 %collective-permute-start.3 = (bf16[8,256,384]{2,1,0:T(8,128)(2,1)S(1)}, bf16[8,256,384]{2,1,0:T(8,128)(2,1)S(1)}, u32[]{:S(2)}, u32[]{:S(2)}) collective-permute-start(bf16[8,256,384]{2,1,0:T(8,128)(2,1)S(1)} %get-tuple-element.25.own0_ref), channel_id=1, source_target_pairs={{0,1},{2,3},{4,5},{6,7},{8,9},{10,11},{12,13},{14,15},{16,17},{18,... | collective-permute-start | bytes 4718600 | tf_op jit(solution)/shard_map/ppermute | solution.py:308
  123.6 1.1 copy-done
  124.8 1.3 collective-permute-start.2
  126.0 13.8 %collective-permute-done.1.f_ref = bf16[8,128,384]{2,1,0:T(8,128)(2,1)S(1)} collective-permute-done((bf16[8,128,384]{2,1,0:T(8,128)(2,1)S(1)}, bf16[8,128,384]{2,1,0:T(8,128)(2,1)S(1)}, u32[]{:S(2)}, u32[]{:S(2)}) %collective-permute-start.1) | collective-permute-done | bytes 786464 | tf_op jit(solution)/shard_map/ppermute | solution.py:306
  139.9 8.4 %collective-permute-done.2.g_ref = bf16[8,128,384]{2,1,0:T(8,128)(2,1)S(1)} collective-permute-done((bf16[8,128,384]{2,1,0:T(8,128)(2,1)S(1)}, bf16[8,128,384]{2,1,0:T(8,128)(2,1)S(1)}, u32[]{:S(2)}, u32[]{:S(2)}) %collective-permute-start.2) | collective-permute-done | bytes 786464 | tf_op jit(solution)/shard_map/ppermute | solution.py:307
  148.3 0.8 early_columns.1.early_ref
  149.1 7.2 %all-to-all-done.1.source_ref = bf16[32,2,32,384]{3,2,1,0:T(8,128)(2,1)} async-done(((bf16[32,2,32,384]{3,2,1,0:T(8,128)(2,1)}), bf16[32,2,32,384]{3,2,1,0:T(8,128)(2,1)}, u32[]{:S(2)}, u32[]{:S(2)}) %all-to-all-start.1) | async-done | bytes 1572896 | tf_op jit(solution)/shard_map/all_to_all | solution.py:319
  156.3 2.2 %channel_rows.3 = (bf16[8,128,384]{2,1,0:T(8,128)(2,1)S(1)}, bf16[8,128,384]{2,1,0:T(8,128)(2,1)S(1)}, bf16[8,256,384]{2,1,0:T(8,128)(2,1)S(1)}) custom-call(s32[3]{0:T(128)S(1)} %copy-done.4, bf16[256,256]{1,0:T(8,128)(2,1)S(1)} %copy-done.2, bf16[32,2,32,384]{3,2,1,0:T(8,128)(2,1)} %all-to-all-done.1.source_ref), custom_call_target="tpu_custom_call" | custom-call | tf_op jit(solution)/shard_map/channel_rows/pallas_call | solution.py:177
  158.9 4.8 %collective-permute-start.7 = (bf16[8,256,384]{2,1,0:T(8,128)(2,1)S(1)}, bf16[8,256,384]{2,1,0:T(8,128)(2,1)S(1)}, u32[]{:S(2)}, u32[]{:S(2)}) collective-permute-start(bf16[8,256,384]{2,1,0:T(8,128)(2,1)S(1)} %get-tuple-element.28.own1_ref), channel_id=1, source_target_pairs={{0,1},{2,3},{4,5},{6,7},{8,9},{10,11},{12,13},{14,15},{16,17},{18,... | collective-permute-start | bytes 4718600 | tf_op jit(solution)/shard_map/ppermute | solution.py:308
  163.6 3.1 %self_tiles.1 = f32[2,8,256,256]{3,2,1,0:T(8,128)} custom-call(bf16[8,256,384]{2,1,0:T(8,128)(2,1)S(1)} %copy-done.1, bf16[8,256,384]{2,1,0:T(8,128)(2,1)S(1)} %get-tuple-element.28.own1_ref), custom_call_target="tpu_custom_call" | custom-call | tf_op jit(solution)/shard_map/self_tiles/pallas_call | solution.py:215
  166.7 1.3 collective-permute-start.6
  168.0 11.7 %collective-permute-done.5.f_ref = bf16[8,128,384]{2,1,0:T(8,128)(2,1)S(1)} collective-permute-done((bf16[8,128,384]{2,1,0:T(8,128)(2,1)S(1)}, bf16[8,128,384]{2,1,0:T(8,128)(2,1)S(1)}, u32[]{:S(2)}, u32[]{:S(2)}) %collective-permute-start.5) | collective-permute-done | bytes 786464 | tf_op jit(solution)/shard_map/ppermute | solution.py:306
  179.7 8.4 %collective-permute-done.6.g_ref = bf16[8,128,384]{2,1,0:T(8,128)(2,1)S(1)} collective-permute-done((bf16[8,128,384]{2,1,0:T(8,128)(2,1)S(1)}, bf16[8,128,384]{2,1,0:T(8,128)(2,1)S(1)}, u32[]{:S(2)}, u32[]{:S(2)}) %collective-permute-start.6) | collective-permute-done | bytes 786464 | tf_op jit(solution)/shard_map/ppermute | solution.py:307
  188.2 5.2 %cross_tiles.1 = (f32[2,8,256,256]{3,2,1,0:T(8,128)}, f32[2,8,256,128]{3,2,1,0:T(8,128)}) custom-call(s32[3]{0:T(128)S(1)} %copy-done.4, bf16[8,256,384]{2,1,0:T(8,128)(2,1)S(1)} %copy-done.1, bf16[8,256,384]{2,1,0:T(8,128)(2,1)S(1)} %get-tuple-element.28.own1_ref, bf16[8,384,384]{2,1,0:T(8,128)(2,1)S(1)} %early_columns.1.early_ref, ...), custom_call_target="tpu_custom_call" | custom-call | tf_op jit(solution)/shard_map/cross_tiles/pallas_call | solution.py:278
  (19 shorter events, 0.4 us)
Async XLA Ops:
  0.7 19.3 %copy-start.3 = (s32[3]{0:T(128)}, s32[3]{0:T(128)S(1)}, u32[]{:S(2)}) copy-start(s32[3]{0:T(128)S(1)} %pad_add_fusion.place_ref) | copy-start | bytes 40
  7.2 101.2 %all-to-all-start = ((bf16[64,32,384]{2,1,0:T(8,128)(2,1)}), bf16[64,32,384]{2,1,0:T(8,128)(2,1)S(1)}, u32[]{:S(2)}, u32[]{:S(2)}) async-start(bf16[64,32,384]{2,1,0:T(8,128)(2,1)} %filter_section.3), calls=%async_computation | async-start | bytes 3145728 | tf_op jit(solution)/shard_map/all_to_all | solution.py:316
  26.4 31.6 %collective-permute-start = (bf16[32,32,384]{2,1,0:T(8,128)(2,1)}, bf16[32,32,384]{2,1,0:T(8,128)(2,1)S(1)}, u32[]{:S(2)}, u32[]{:S(2)}) collective-permute-start(bf16[32,32,384]{2,1,0:T(8,128)(2,1)} %get-tuple-element.20), channel_id=1, source_target_pairs={{0,128},{128,0},{1,129},{129,1},{2,130},{130,2},{3,131},{131,3},{4... | collective-permute-start | bytes 2359304 | tf_op jit(solution)/shard_map/ppermute | solution.py:317
  58.0 0.9 copy-start.5
  108.3 9.1 %copy-start.2 = (bf16[256,256]{1,0:T(8,128)(2,1)S(1)}, bf16[256,256]{1,0:T(8,128)(2,1)}, u32[]{:S(2)}) copy-start(bf16[256,256]{1,0:T(8,128)(2,1)} %constant.39.clone.order_ref) | copy-start | bytes 393220
  108.4 9.1 %copy-start.4 = (s32[3]{0:T(128)S(1)}, s32[3]{0:T(128)}, u32[]{:S(2)}) copy-start(s32[3]{0:T(128)} %copy-done.3) | copy-start | bytes 40
  108.4 47.9 %all-to-all-start.1 = ((bf16[32,2,32,384]{3,2,1,0:T(8,128)(2,1)}), bf16[32,2,32,384]{3,2,1,0:T(8,128)(2,1)}, u32[]{:S(2)}, u32[]{:S(2)}) async-start(bf16[32,2,32,384]{3,2,1,0:T(8,128)(2,1)} %merge_sides.1), calls=%async_computation.1 | async-start | bytes 3145728 | tf_op jit(solution)/shard_map/all_to_all | solution.py:319
  118.7 21.2 %collective-permute-start.1 = (bf16[8,128,384]{2,1,0:T(8,128)(2,1)S(1)}, bf16[8,128,384]{2,1,0:T(8,128)(2,1)S(1)}, u32[]{:S(2)}, u32[]{:S(2)}) collective-permute-start(bf16[8,128,384]{2,1,0:T(8,128)(2,1)S(1)} %get-tuple-element.23), channel_id=1, source_target_pairs={{0,3},{1,2},{2,1},{3,0},{4,7},{5,6},{6,5},{7,4},{8,11},{9,10},{10,... | collective-permute-start | bytes 2359304 | tf_op jit(solution)/shard_map/ppermute | solution.py:306
  119.9 28.4 %collective-permute-start.3 = (bf16[8,256,384]{2,1,0:T(8,128)(2,1)S(1)}, bf16[8,256,384]{2,1,0:T(8,128)(2,1)S(1)}, u32[]{:S(2)}, u32[]{:S(2)}) collective-permute-start(bf16[8,256,384]{2,1,0:T(8,128)(2,1)S(1)} %get-tuple-element.25.own0_ref), channel_id=1, source_target_pairs={{0,1},{2,3},{4,5},{6,7},{8,9},{10,11},{12,13},{14,15},{16,17},{18,... | collective-permute-start | bytes 4718600 | tf_op jit(solution)/shard_map/ppermute | solution.py:308
  123.6 1.1 copy-start
  124.8 23.6 %collective-permute-start.2 = (bf16[8,128,384]{2,1,0:T(8,128)(2,1)S(1)}, bf16[8,128,384]{2,1,0:T(8,128)(2,1)S(1)}, u32[]{:S(2)}, u32[]{:S(2)}) collective-permute-start(bf16[8,128,384]{2,1,0:T(8,128)(2,1)S(1)} %get-tuple-element.24), channel_id=1, source_target_pairs={{1,2},{3,0},{5,6},{7,4},{9,10},{11,8},{13,14},{15,12},{17,18},{19,... | collective-permute-start | bytes 2359304 | tf_op jit(solution)/shard_map/ppermute | solution.py:307
  139.9 8.4 %collective-permute-start.4 = (bf16[8,128,384]{2,1,0:T(8,128)(2,1)S(1)}, bf16[8,128,384]{2,1,0:T(8,128)(2,1)S(1)}, u32[]{:S(2)}, u32[]{:S(2)}) collective-permute-start(bf16[8,128,384]{2,1,0:T(8,128)(2,1)S(1)} %collective-permute-done.1.f_ref), channel_id=1, source_target_pairs={{0,1},{1,0},{2,3},{3,2},{4,5},{5,4},{6,7},{7,6},{8,9},{9,8},{10,11... | collective-permute-start | bytes 2359304 | tf_op jit(solution)/shard_map/ppermute | solution.py:312
  156.3 7.4 %copy-start.1 = (bf16[8,256,384]{2,1,0:T(8,128)(2,1)S(1)}, bf16[8,256,384]{2,1,0:T(8,128)(2,1)}, u32[]{:S(2)}) copy-start(bf16[8,256,384]{2,1,0:T(8,128)(2,1)} %copy-done) | copy-start | bytes 4718596
  158.5 21.2 %collective-permute-start.5 = (bf16[8,128,384]{2,1,0:T(8,128)(2,1)S(1)}, bf16[8,128,384]{2,1,0:T(8,128)(2,1)S(1)}, u32[]{:S(2)}, u32[]{:S(2)}) collective-permute-start(bf16[8,128,384]{2,1,0:T(8,128)(2,1)S(1)} %get-tuple-element.27), channel_id=1, source_target_pairs={{0,3},{1,2},{2,1},{3,0},{4,7},{5,6},{6,5},{7,4},{8,11},{9,10},{10,... | collective-permute-start | bytes 2359304 | tf_op jit(solution)/shard_map/ppermute | solution.py:306
  158.9 29.3 %collective-permute-start.7 = (bf16[8,256,384]{2,1,0:T(8,128)(2,1)S(1)}, bf16[8,256,384]{2,1,0:T(8,128)(2,1)S(1)}, u32[]{:S(2)}, u32[]{:S(2)}) collective-permute-start(bf16[8,256,384]{2,1,0:T(8,128)(2,1)S(1)} %get-tuple-element.28.own1_ref), channel_id=1, source_target_pairs={{0,1},{2,3},{4,5},{6,7},{8,9},{10,11},{12,13},{14,15},{16,17},{18,... | collective-permute-start | bytes 4718600 | tf_op jit(solution)/shard_map/ppermute | solution.py:308
  166.7 21.5 %collective-permute-start.6 = (bf16[8,128,384]{2,1,0:T(8,128)(2,1)S(1)}, bf16[8,128,384]{2,1,0:T(8,128)(2,1)S(1)}, u32[]{:S(2)}, u32[]{:S(2)}) collective-permute-start(bf16[8,128,384]{2,1,0:T(8,128)(2,1)S(1)} %get-tuple-element.32), channel_id=1, source_target_pairs={{1,2},{3,0},{5,6},{7,4},{9,10},{11,8},{13,14},{15,12},{17,18},{19,... | collective-permute-start | bytes 2359304 | tf_op jit(solution)/shard_map/ppermute | solution.py:307
  179.7 8.4 %collective-permute-start.8 = (bf16[8,128,384]{2,1,0:T(8,128)(2,1)S(1)}, bf16[8,128,384]{2,1,0:T(8,128)(2,1)S(1)}, u32[]{:S(2)}, u32[]{:S(2)}) collective-permute-start(bf16[8,128,384]{2,1,0:T(8,128)(2,1)S(1)} %collective-permute-done.5.f_ref), channel_id=1, source_target_pairs={{0,1},{1,0},{2,3},{3,2},{4,5},{5,4},{6,7},{7,6},{8,9},{9,8},{10,11... | collective-permute-start | bytes 2359304 | tf_op jit(solution)/shard_map/ppermute | solution.py:312

commit v5 on v4

v5 whole, which is shorter than its diff:
```python
import functools
import math

import jax
import jax.numpy as jnp
import numpy as np
from jax import lax
from jax.experimental import pallas as pl
from jax.experimental.pallas import tpu as pltpu
from jax.sharding import Mesh
from jax.sharding import PartitionSpec as P

CHAN = 512
TAPS = 4
SPECTRA = 384
BLOCK = 256
FRAME = 2 * CHAN
SB = 128
EARLY = 2
NT = (((1,), (1,)), ((), ()))
SMALL = pl.BlockSpec(memory_space=pltpu.SMEM)
IN_VMEM = pl.BlockSpec(memory_space=pltpu.VMEM)


def dft_table():
    positions = np.arange(FRAME, dtype=np.int32)
    bins = np.arange(CHAN, dtype=np.int32)
    phases = bins[:, None] * positions[None, :] % FRAME
    angles = phases.astype(np.float32) * np.float32(math.pi / CHAN)
    norming = np.float32(FRAME ** (-0.5))
    table = np.concatenate([np.cos(angles) * norming, -np.sin(angles) * norming])
    return table.astype(jnp.bfloat16)


def row_order():
    order = np.arange(256).reshape(32, 8).T.reshape(-1)
    return np.eye(256, dtype=np.float32)[order].astype(jnp.bfloat16)


def spectra_kernel(first, split, place_ref, x_ref, table_ref, taps_ref, *refs):
    outs, (x_held, table, taps_held, frames, filtered, out_held, x_sem, table_sem, taps_sem, out_sem) = refs[:-10], refs[-10:]
    blocks = x_held.shape[0]
    extra = TAPS - 1
    arriving = []
    for j in range(blocks):
        start, length = (first, SB + extra) if j == 0 else (first + j * SB + extra, SB)
        arriving.append(
            pltpu.make_async_copy(
                x_ref.at[:, pl.ds(start * FRAME, length * FRAME)], x_held.at[j, :, pl.ds(0, length * FRAME)], x_sem.at[j]
            )
        )
    table_arriving = pltpu.make_async_copy(table_ref, table, table_sem)
    taps_arriving = pltpu.make_async_copy(taps_ref, taps_held, taps_sem)
    taps_arriving.start()
    arriving[0].start()
    table_arriving.start()
    for copy in arriving[1:]:
        copy.start()
    taps_arriving.wait()
    leaving = []
    for j in range(blocks):
        arriving[j].wait()
        start, length = (0, SB + extra) if j == 0 else (j * SB + extra, SB)
        for f in range(length):
            for n in range(0, FRAME, 128):
                frames[n // 128, 4 * (start + f) : 4 * (start + f) + 4, :] = x_held[
                    j, :, f * FRAME + n : f * FRAME + n + 128
                ].astype(jnp.float32)
        for n in range(0, FRAME, 128):
            taps = [taps_held[t : t + 1, n : n + 128] for t in range(TAPS)]
            for i in range(4):
                for s in range(j * SB, (j + 1) * SB, 16):
                    total = frames[n // 128, pl.ds(i + 4 * s, 16, stride=4), :] * taps[0]
                    for t in range(1, TAPS):
                        total = total + frames[n // 128, pl.ds(i + 4 * (s + t), 16, stride=4), :] * taps[t]
                    row = i * SB + s - j * SB
                    filtered[row : row + 16, n : n + 128] = total.astype(jnp.bfloat16)
        if j == 0:
            table_arriving.wait()
        for pair in range(2):
            product = lax.dot_general(
                table[...], filtered[pair * 2 * SB : (pair + 1) * 2 * SB, :], NT, preferred_element_type=jnp.float32
            )
            for p in range(2):
                part = product[p * CHAN : (p + 1) * CHAN]
                rows = jnp.concatenate(
                    [part[:, :SB].reshape(CHAN // 8, 8, SB), part[:, SB:].reshape(CHAN // 8, 8, SB)], axis=1
                )
                out_held[j, :, pair * 16 : pair * 16 + 16, p * SB : (p + 1) * SB] = rows.astype(jnp.bfloat16)
        if split:
            side = place_ref[2]
            sources = [out_held.at[j, pl.ds(side * 32, 32)], out_held.at[j, pl.ds((1 - side) * 32, 32)]]
        else:
            sources = [out_held.at[j]]
        for k, (source, out) in enumerate(zip(sources, outs)):
            copy = pltpu.make_async_copy(source, out.at[:, :, pl.ds(j * 2 * SB, 2 * SB)], out_sem.at[2 * j + k])
            copy.start()
            leaving.append(copy)
    for copy in leaving:
        copy.wait()


def filter_section(place, samples, pfb_taps, table, first, blocks, split):
    in_hbm = pl.BlockSpec(memory_space=pltpu.HBM)
    lanes = blocks * 2 * SB
    out_shape = [pltpu.HBM((32, 32, lanes), jnp.bfloat16)] * 2 if split else [pltpu.HBM((64, 32, lanes), jnp.bfloat16)]
    return pl.pallas_call(
        functools.partial(spectra_kernel, first, split),
        in_specs=[SMALL, in_hbm, in_hbm, in_hbm],
        out_specs=[in_hbm] * len(out_shape),
        out_shape=out_shape,
        scratch_shapes=[
            pltpu.VMEM((blocks, 4, (SB + TAPS - 1) * FRAME), jnp.bfloat16),
            pltpu.VMEM((2 * CHAN, FRAME), jnp.bfloat16),
            pltpu.VMEM((TAPS, FRAME), jnp.float32),
            pltpu.VMEM((FRAME // 128, 4 * (blocks * SB + 4), 128), jnp.float32),
            pltpu.VMEM((4 * SB, FRAME), jnp.bfloat16),
            pltpu.VMEM((blocks, 64, 32, 2 * SB), jnp.bfloat16),
            pltpu.SemaphoreType.DMA((blocks,)),
            pltpu.SemaphoreType.DMA,
            pltpu.SemaphoreType.DMA,
            pltpu.SemaphoreType.DMA((2 * blocks,)),
        ],
        compiler_params=pltpu.CompilerParams(vmem_limit_bytes=40 * 1024 * 1024),
        name="filter_section",
    )(place, *(pltpu.with_memory_space_constraint(a, pltpu.HBM) for a in (samples, table, pfb_taps)))


def merge_kernel(place_ref, stay_ref, got_ref, out_ref, held, sem):
    side = place_ref[2]
    held[:, side] = stay_ref[...]
    held[:, 1 - side] = got_ref[...]
    copy = pltpu.make_async_copy(held, out_ref, sem)
    copy.start()
    copy.wait()


def merge(place, stay, got):
    shape = (32, 2) + stay.shape[1:]
    return pl.pallas_call(
        merge_kernel,
        in_specs=[SMALL, IN_VMEM, IN_VMEM],
        out_specs=pl.BlockSpec(memory_space=pltpu.HBM),
        out_shape=pltpu.HBM(shape, jnp.bfloat16),
        scratch_shapes=[pltpu.VMEM(shape, jnp.bfloat16), pltpu.SemaphoreType.DMA],
        compiler_params=pltpu.CompilerParams(vmem_limit_bytes=40 * 1024 * 1024),
        name="merge_sides",
    )(place, stay, got)


def rows_kernel(place_ref, order_ref, source_ref, cross_ref, rest_ref, whole_ref):
    chip = place_ref[0]
    order = order_ref[...]
    for out_ref, half in ((cross_ref, 1 - chip), (rest_ref, chip)):
        for g in range(4):
            if len(source_ref.shape) == 3:
                rows = source_ref[pl.ds(half * 32 + g * 8, 8)]
            else:
                rows = source_ref[g * 8 : (g + 1) * 8, half]
            turned = jnp.dot(order, rows.reshape(256, rows.shape[-1]), preferred_element_type=jnp.float32).astype(jnp.bfloat16)
            for c in range(8):
                part = turned[c * 32 : (c + 1) * 32]
                out_ref[c, g * 32 : (g + 1) * 32, :] = part
                whole_ref[c, pl.ds(pl.multiple_of(half * 128 + g * 32, 32), 32), :] = part


def channel_rows(place, order, source):
    lanes = source.shape[-1]
    shapes = [(8, 128, lanes), (8, 128, lanes), (8, BLOCK, lanes)]
    return pl.pallas_call(
        rows_kernel,
        in_specs=[SMALL, IN_VMEM, IN_VMEM],
        out_specs=[IN_VMEM] * 3,
        out_shape=[jax.ShapeDtypeStruct(shape, jnp.bfloat16) for shape in shapes],
        compiler_params=pltpu.CompilerParams(vmem_limit_bytes=40 * 1024 * 1024),
        name="channel_rows",
    )(place, order, source)


def stacked(rows):
    pieces = []
    for s in range(0, rows.shape[1], 2 * SB):
        pieces += [rows[:, s + SB : s + 2 * SB], -rows[:, s : s + SB]]
    return jnp.concatenate([rows, jnp.concatenate(pieces, axis=1)], axis=0)


def tile_products(rows, cols):
    return lax.dot_general(stacked(rows), cols, NT, preferred_element_type=jnp.float32) * (1.0 / SPECTRA)


def self_kernel(own0_ref, own1_ref, self_ref, self_held, sem):
    copies = []
    for c in range(8):
        rows = jnp.concatenate([own0_ref[c], own1_ref[c]], axis=1)
        product = tile_products(rows, rows)
        self_held[0, c] = product[:BLOCK]
        self_held[1, c] = product[BLOCK:]
        copies.append(pltpu.make_async_copy(self_held.at[:, c], self_ref.at[:, c], sem.at[c]))
        copies[-1].start()
    for copy in copies:
        copy.wait()


def self_tiles(own0, own1):
    return pl.pallas_call(
        self_kernel,
        in_specs=[IN_VMEM] * 2,
        out_specs=pl.BlockSpec(memory_space=pltpu.HBM),
        out_shape=pltpu.HBM((2, 8, BLOCK, BLOCK), jnp.float32),
        scratch_shapes=[pltpu.VMEM((2, 8, BLOCK, BLOCK), jnp.float32), pltpu.SemaphoreType.DMA((8,))],
        compiler_params=pltpu.CompilerParams(vmem_limit_bytes=40 * 1024 * 1024),
        name="self_tiles",
    )(own0, own1)


def put_columns(place_ref, f_ref, g_ref, h_ref, s_ref, out_ref):
    chip = place_ref[0]

    @pl.when(place_ref[1] == 0)
    def _():
        out_ref[:, pl.ds(pl.multiple_of(chip * 128, 128), 128), :] = f_ref[...]
        out_ref[:, pl.ds(pl.multiple_of((1 - chip) * 128, 128), 128), :] = g_ref[...]

    @pl.when(place_ref[1] == 1)
    def _():
        out_ref[:, :BLOCK, :] = h_ref[...]

    out_ref[:, BLOCK:, :] = s_ref[...]


def early_kernel(place_ref, f_ref, g_ref, h_ref, s_ref, out_ref):
    put_columns(place_ref, f_ref, g_ref, h_ref, s_ref, out_ref)


def early_columns(place, *received):
    return pl.pallas_call(
        early_kernel,
        in_specs=[SMALL] + [IN_VMEM] * 4,
        out_specs=IN_VMEM,
        out_shape=jax.ShapeDtypeStruct((8, BLOCK + BLOCK // 2, received[0].shape[-1]), jnp.bfloat16),
        compiler_params=pltpu.CompilerParams(vmem_limit_bytes=40 * 1024 * 1024),
        name="early_columns",
    )(place, *received)


def cross_kernel(place_ref, own0_ref, own1_ref, early_ref, f_ref, g_ref, h_ref, s_ref, prior_ref, far_ref,
                 held, prior_held, far_held, prior_sem, far_sem):
    put_columns(place_ref, f_ref, g_ref, h_ref, s_ref, held)
    copies = []
    for c in range(8):
        rows = jnp.concatenate([own0_ref[c], own1_ref[c]], axis=1)
        product = tile_products(rows, jnp.concatenate([early_ref[c], held[c]], axis=1))
        for p in range(2):
            prior_held[p, c] = product[p * BLOCK : (p + 1) * BLOCK, :BLOCK]
            far_held[p, c] = product[p * BLOCK : (p + 1) * BLOCK, BLOCK:]
        copies.append(pltpu.make_async_copy(prior_held.at[:, c], prior_ref.at[:, c], prior_sem.at[c]))
        copies.append(pltpu.make_async_copy(far_held.at[:, c], far_ref.at[:, c], far_sem.at[c]))
        copies[-2].start()
        copies[-1].start()
    for copy in copies:
        copy.wait()


def cross_tiles(place, own0, own1, early, *late):
    in_hbm = pl.BlockSpec(memory_space=pltpu.HBM)
    prior_shape, far_shape = (2, 8, BLOCK, BLOCK), (2, 8, BLOCK, BLOCK // 2)
    return pl.pallas_call(
        cross_kernel,
        in_specs=[SMALL] + [IN_VMEM] * (3 + len(late)),
        out_specs=[in_hbm, in_hbm],
        out_shape=[pltpu.HBM(prior_shape, jnp.float32), pltpu.HBM(far_shape, jnp.float32)],
        scratch_shapes=[
            pltpu.VMEM((8, BLOCK + BLOCK // 2, late[0].shape[-1]), jnp.bfloat16),
            pltpu.VMEM(prior_shape, jnp.float32),
            pltpu.VMEM(far_shape, jnp.float32),
            pltpu.SemaphoreType.DMA((8,)),
            pltpu.SemaphoreType.DMA((8,)),
        ],
        compiler_params=pltpu.CompilerParams(vmem_limit_bytes=40 * 1024 * 1024),
        name="cross_tiles",
    )(place, own0, own1, early, *late)


CROSSED = [(0, 3), (1, 2), (2, 1), (3, 0)]
ODD_OVER = [(1, 2), (3, 0)]
EVEN_UP = [(0, 1), (2, 3)]
SWAPPED = [(0, 1), (1, 0), (2, 3), (3, 2)]


def on_device(table, order, samples, pfb_taps):
    position = lax.axis_index("narrow")
    place = jnp.stack([position // 2, position % 2, lax.axis_index("side")]).astype(jnp.int32)

    def exchange(crossing, rest, whole):
        f = lax.ppermute(crossing, "narrow", CROSSED)
        g = lax.ppermute(rest, "narrow", ODD_OVER)
        h = lax.ppermute(whole, "narrow", EVEN_UP)
        return f, g, h

    def swap(f):
        return lax.ppermute(f, "narrow", SWAPPED)

    (early,) = filter_section(place, samples, pfb_taps, table, 0, EARLY, False)
    stay, leave = filter_section(place, samples, pfb_taps, table, EARLY * SB, 1, True)
    source0 = lax.all_to_all(early, ("side", "plane"), split_axis=0, concat_axis=0, tiled=True)
    late = merge(place, stay, lax.ppermute(leave, "side", [(0, 1), (1, 0)]))
    late, source0 = lax.optimization_barrier((late, source0))
    source1 = lax.all_to_all(late, "plane", split_axis=0, concat_axis=0, tiled=True)
    crossing0, rest0, own0 = channel_rows(place, order, source0)
    f, g, h = exchange(crossing0, rest0, own0)
    held0 = early_columns(place, f, g, h, swap(f))
    source1, held0 = lax.optimization_barrier((source1, held0))
    crossing1, rest1, own1 = channel_rows(place, order, source1)
    f, g, h = exchange(crossing1, rest1, own1)
    own1, h = lax.optimization_barrier((own1, h))
    self_vis = self_tiles(own0, own1)
    f, self_vis = lax.optimization_barrier((f, self_vis))
    prior_vis, far_vis = cross_tiles(place, own0, own1, held0, f, g, h, swap(f))
    return (self_vis, prior_vis, far_vis)


def solution(mesh):
    parted = Mesh(mesh.devices.reshape(2, mesh.devices.shape[0] // 2, mesh.devices.shape[1]), ("side", "plane", "narrow"))
    out_spec = P(None, ("side", "plane"), "narrow", None)
    return jax.shard_map(
        functools.partial(on_device, dft_table(), row_order()),
        mesh=parted,
        in_specs=(P(("narrow", "side", "plane"), None), P()),
        out_specs=(out_spec, out_spec, out_spec),
        check_vma=False,
    )
```

time: 194 us -> 147 us (0.76)
  Pallas kernels: 74.7 us -> 26.7 us
  local copies, waits for them, and re-layouts: 2.05 us -> 8.7 us
  starting transfers between devices: 36.1 us -> 30.1 us
    pallas_call x1, Pallas kernels: 49.4 us -> 1.59 us  [merge(): pl.pallas_call(merge_kernel, in_specs=[SMALL, IN_VMEM, IN_VMEM], out_spec...]
    all_to_all x1, waiting for transfers between devices: 0.01 us -> 23.3 us  [on_device(): lax.all_to_all(early, ('side', 'plane'), split_axis=0, concat_axis=0, til...]
    ppermute x1, waiting for transfers between devices: 29.9 us -> 18.7 us  [on_device(): late = merge(place, stay, lax.ppermute(leave, 'side', [(0, 1), (1, 0)]))]
    all_to_all x1, waiting for transfers between devices: 7.2 us -> 0.01 us  [on_device(): lax.all_to_all(late, 'plane', split_axis=0, concat_axis=0, tiled=True)]
    unnamed x12 -> x20, local copies, waits for them, and re-layouts: 2.05 us -> 8.7 us
    ppermute x2, waiting for transfers between devices: 25.6 us -> 21.2 us  [exchange(): f = lax.ppermute(crossing, 'narrow', CROSSED)]
    all_to_all x1, starting transfers between devices: 9.02 us -> 5.32 us  [on_device(): lax.all_to_all(late, 'plane', split_axis=0, concat_axis=0, tiled=True)]
  transfers between devices with their start and end apart: 11 -> 11, of which waited for: 6 -> 7; matrix products, arithmetic and copies ran while one was open for 0% -> 0% of each run, Pallas kernels for 31% -> 8%
where the time goes in v5:
time: 147 us; the launch traced here: 146 us
  waiting for transfers between devices  79.8 us (54%)
  starting transfers between devices  30.1 us (20%)
  Pallas kernels  26.7 us (18%)
  local copies, waits for them, and re-layouts  8.7 us (6%)
    all_to_all x1, waiting for transfers between devices, on_device(): lax.all_to_all(early, ('side', 'plane'), split_axis=0, concat_axis=0, til...  23.3 us
    ppermute x2, waiting for transfers between devices, exchange(): f = lax.ppermute(crossing, 'narrow', CROSSED)  21.2 us
    ppermute x1, waiting for transfers between devices, on_device(): late = merge(place, stay, lax.ppermute(leave, 'side', [(0, 1), (1, 0)]))  18.7 us
    ppermute x2, waiting for transfers between devices, exchange(): g = lax.ppermute(rest, 'narrow', ODD_OVER)  15.9 us
    all_to_all x1, starting transfers between devices, on_device(): lax.all_to_all(early, ('side', 'plane'), split_axis=0, concat_axis=0, til...  12.8 us
    pallas_call x2, Pallas kernels, filter_section(): pl.pallas_call(functools.partial(spectra_kernel, first, split), in_specs=...  11.6 us
    unnamed x20, local copies, waits for them, and re-layouts  8.7 us
    ppermute x2, starting transfers between devices, exchange(): h = lax.ppermute(whole, 'narrow', EVEN_UP)  7.28 us
  transfers between devices with their start and end apart: 11, of which 7 were waited for; matrix products, arithmetic and copies ran while one was open for 0% of the time, Pallas kernels for 8%

profile of v5, /device:TPU:24, one launch (start us, length us, event | category | flops | bytes accessed | tf_op | source)
XLA Modules:
  0.0 146.4 jit_solution(7022248194050722199)
XLA Ops:
  0.7 6.6 %filter_section.3 = bf16[64,32,512]{2,1,0:T(8,128)(2,1)} custom-call(s32[3]{0:T(128)S(1)} %pad_add_fusion.place_ref, bf16[4,396288]{1,0:T(4,128)(2,1)} %x_ref.3, bf16[1024,1024]{1,0:T(8,128)(2,1)} %constant.38.clone.table_ref, f32[4,1024]{1,0:T(4,128)} %taps_ref.3), custom_call_target="tpu_custom_call" | custom-call | tf_op jit(solution)/shard_map/filter_section/pallas_call | solution.py:107
  7.4 12.8 %all-to-all-start = ((bf16[64,32,512]{2,1,0:T(8,128)(2,1)}), bf16[64,32,512]{2,1,0:T(8,128)(2,1)S(1)}, u32[]{:S(2)}, u32[]{:S(2)}) async-start(bf16[64,32,512]{2,1,0:T(8,128)(2,1)} %filter_section.3), calls=%async_computation | async-start | bytes 4194304 | tf_op jit(solution)/shard_map/all_to_all | solution.py:305
  20.2 5.0 %filter_section.2 = (bf16[32,32,256]{2,1,0:T(8,128)(2,1)}, bf16[32,32,256]{2,1,0:T(8,128)(2,1)}) custom-call(s32[3]{0:T(128)S(1)} %pad_add_fusion.place_ref, bf16[4,396288]{1,0:T(4,128)(2,1)} %x_ref.3, bf16[1024,1024]{1,0:T(8,128)(2,1)} %constant.38.clone.table_ref, f32[4,1024]{1,0:T(4,128)} %taps_ref.3), custom_call_target="tpu_custom_call" | custom-call | tf_op jit(solution)/shard_map/filter_section/pallas_call | solution.py:107
  25.2 1.7 %collective-permute-start = (bf16[32,32,256]{2,1,0:T(8,128)(2,1)}, bf16[32,32,256]{2,1,0:T(8,128)(2,1)S(1)}, u32[]{:S(2)}, u32[]{:S(2)}) collective-permute-start(bf16[32,32,256]{2,1,0:T(8,128)(2,1)} %get-tuple-element.22), channel_id=1, source_target_pairs={{0,128},{128,0},{1,129},{129,1},{2,130},{130,2},{3,131},{131,3},{4... | collective-permute-start | bytes 1572872 | tf_op jit(solution)/shard_map/ppermute | solution.py:306
  26.8 18.7 %collective-permute-done.got_ref = bf16[32,32,256]{2,1,0:T(8,128)(2,1)S(1)} collective-permute-done((bf16[32,32,256]{2,1,0:T(8,128)(2,1)}, bf16[32,32,256]{2,1,0:T(8,128)(2,1)S(1)}, u32[]{:S(2)}, u32[]{:S(2)}) %collective-permute-start) | collective-permute-done | bytes 524320 | tf_op jit(solution)/shard_map/ppermute | solution.py:306
  46.6 1.6 %merge_sides.1 = bf16[32,2,32,256]{3,2,1,0:T(8,128)(2,1)} custom-call(s32[3]{0:T(128)S(1)} %pad_add_fusion.place_ref, bf16[32,32,256]{2,1,0:T(8,128)(2,1)S(1)} %copy-done.7, bf16[32,32,256]{2,1,0:T(8,128)(2,1)S(1)} %collective-permute-done.got_ref), custom_call_target="tpu_custom_call" | custom-call | tf_op jit(solution)/shard_map/merge_sides/pallas_call | solution.py:140
  48.2 23.3 %all-to-all-done.source_ref = bf16[64,32,512]{2,1,0:T(8,128)(2,1)S(1)} async-done(((bf16[64,32,512]{2,1,0:T(8,128)(2,1)}), bf16[64,32,512]{2,1,0:T(8,128)(2,1)S(1)}, u32[]{:S(2)}, u32[]{:S(2)}) %all-to-all-start) | async-done | bytes 2097184 | tf_op jit(solution)/shard_map/all_to_all | solution.py:305
  71.6 1.3 copy-done.3
  72.9 1.6 %copy-done.4 = bf16[64,32,512]{2,1,0:T(8,128)(2,1)S(1)} copy-done((bf16[64,32,512]{2,1,0:T(8,128)(2,1)S(1)}, bf16[64,32,512]{2,1,0:T(8,128)(2,1)}, u32[]{:S(2)}) %copy-start.4) | copy-done | bytes 2097176
  74.5 2.0 %channel_rows.2 = (bf16[8,128,512]{2,1,0:T(8,128)(2,1)}, bf16[8,128,512]{2,1,0:T(8,128)(2,1)S(1)}, bf16[8,256,512]{2,1,0:T(8,128)(2,1)S(1)}) custom-call(s32[3]{0:T(128)S(1)} %pad_add_fusion.place_ref, bf16[256,256]{1,0:T(8,128)(2,1)S(1)} %copy-done.8, bf16[64,32,512]{2,1,0:T(8,128)(2,1)S(1)} %copy-done.4), custom_call_target="tpu_custom_call" | custom-call | tf_op jit(solution)/shard_map/channel_rows/pallas_call | solution.py:170
  77.5 5.9 %collective-permute-start.3 = (bf16[8,256,512]{2,1,0:T(8,128)(2,1)S(1)}, bf16[8,256,512]{2,1,0:T(8,128)(2,1)}, u32[]{:S(2)}, u32[]{:S(2)}) collective-permute-start(bf16[8,256,512]{2,1,0:T(8,128)(2,1)S(1)} %get-tuple-element.27.own0_ref), channel_id=1, source_target_pairs={{0,1},{2,3},{4,5},{6,7},{8,9},{10,11},{12,13},{14,15},{16,17},{18,... | collective-permute-start | bytes 6291464 | tf_op jit(solution)/shard_map/ppermute | solution.py:297
  83.5 5.3 %all-to-all-start.1 = ((bf16[32,2,32,256]{3,2,1,0:T(8,128)(2,1)}), bf16[32,2,32,256]{3,2,1,0:T(8,128)(2,1)}, u32[]{:S(2)}, u32[]{:S(2)}) async-start(bf16[32,2,32,256]{3,2,1,0:T(8,128)(2,1)} %merge_sides.1), calls=%async_computation.1 | async-start | bytes 2097152 | tf_op jit(solution)/shard_map/all_to_all | solution.py:308
  88.8 1.3 collective-permute-start.2
  90.1 14.2 %collective-permute-done.1.f_ref = bf16[8,128,512]{2,1,0:T(8,128)(2,1)S(1)} collective-permute-done((bf16[8,128,512]{2,1,0:T(8,128)(2,1)}, bf16[8,128,512]{2,1,0:T(8,128)(2,1)S(1)}, u32[]{:S(2)}, u32[]{:S(2)}) %collective-permute-start.1) | collective-permute-done | bytes 1048608 | tf_op jit(solution)/shard_map/ppermute | solution.py:295
  105.3 10.3 %collective-permute-done.2.g_ref = bf16[8,128,512]{2,1,0:T(8,128)(2,1)S(1)} collective-permute-done((bf16[8,128,512]{2,1,0:T(8,128)(2,1)}, bf16[8,128,512]{2,1,0:T(8,128)(2,1)S(1)}, u32[]{:S(2)}, u32[]{:S(2)}) %collective-permute-start.2) | collective-permute-done | bytes 1048608 | tf_op jit(solution)/shard_map/ppermute | solution.py:296
  116.8 1.8 %early_columns.1.early_ref = bf16[8,384,512]{2,1,0:T(8,128)(2,1)S(1)} custom-call(s32[3]{0:T(128)S(1)} %pad_add_fusion.place_ref, bf16[8,128,512]{2,1,0:T(8,128)(2,1)S(1)} %copy-done.6, bf16[8,128,512]{2,1,0:T(8,128)(2,1)S(1)} %collective-permute-done.2.g_ref, bf16[8,256,512]{2,1,0:T(8,128)(2,1)} %collective-permute-done.3.h_ref, ...), custom_call_target="tpu_custom_call" | custom-call | tf_op jit(solution)/shard_map/early_columns/pallas_call | solution.py:236
  118.7 1.7 %channel_rows.3 = (bf16[8,128,256]{2,1,0:T(8,128)(2,1)S(1)}, bf16[8,128,256]{2,1,0:T(8,128)(2,1)S(1)}, bf16[8,256,256]{2,1,0:T(8,128)(2,1)S(1)}) custom-call(s32[3]{0:T(128)S(1)} %pad_add_fusion.place_ref, bf16[256,256]{1,0:T(8,128)(2,1)S(1)} %copy-done.8, bf16[32,2,32,256]{3,2,1,0:T(8,128)(2,1)} %all-to-all-done.1.source_ref), custom_call_target="tpu_custom_call" | custom-call | tf_op jit(solution)/shard_map/channel_rows/pallas_call | solution.py:170
  120.3 1.4 collective-permute-start.6
  121.8 1.5 %collective-permute-start.7 = (bf16[8,128,256]{2,1,0:T(8,128)(2,1)S(1)}, bf16[8,128,256]{2,1,0:T(8,128)(2,1)S(1)}, u32[]{:S(2)}, u32[]{:S(2)}) collective-permute-start(bf16[8,128,256]{2,1,0:T(8,128)(2,1)S(1)} %get-tuple-element.35), channel_id=1, source_target_pairs={{1,2},{3,0},{5,6},{7,4},{9,10},{11,8},{13,14},{15,12},{17,18},{19,... | collective-permute-start | bytes 1572872 | tf_op jit(solution)/shard_map/ppermute | solution.py:296
  123.9 1.6 %copy-done.1 = bf16[8,256,512]{2,1,0:T(8,128)(2,1)S(1)} copy-done((bf16[8,256,512]{2,1,0:T(8,128)(2,1)S(1)}, bf16[8,256,512]{2,1,0:T(8,128)(2,1)}, u32[]{:S(2)}) %copy-start.1) | copy-done | bytes 2097176
  125.5 3.1 %self_tiles.1 = f32[2,8,256,256]{3,2,1,0:T(8,128)} custom-call(bf16[8,256,512]{2,1,0:T(8,128)(2,1)S(1)} %copy-done.1, bf16[8,256,256]{2,1,0:T(8,128)(2,1)S(1)} %get-tuple-element.31.own1_ref), custom_call_target="tpu_custom_call" | custom-call | tf_op jit(solution)/shard_map/self_tiles/pallas_call | solution.py:205
  128.6 7.0 %collective-permute-done.5.f_ref = bf16[8,128,256]{2,1,0:T(8,128)(2,1)S(1)} collective-permute-done((bf16[8,128,256]{2,1,0:T(8,128)(2,1)S(1)}, bf16[8,128,256]{2,1,0:T(8,128)(2,1)S(1)}, u32[]{:S(2)}, u32[]{:S(2)}) %collective-permute-start.5) | collective-permute-done | bytes 524320 | tf_op jit(solution)/shard_map/ppermute | solution.py:295
  135.5 5.6 %collective-permute-done.7.g_ref = bf16[8,128,256]{2,1,0:T(8,128)(2,1)S(1)} collective-permute-done((bf16[8,128,256]{2,1,0:T(8,128)(2,1)S(1)}, bf16[8,128,256]{2,1,0:T(8,128)(2,1)S(1)}, u32[]{:S(2)}, u32[]{:S(2)}) %collective-permute-start.7) | collective-permute-done | bytes 524320 | tf_op jit(solution)/shard_map/ppermute | solution.py:296
  141.2 5.0 %cross_tiles.1 = (f32[2,8,256,256]{3,2,1,0:T(8,128)}, f32[2,8,256,128]{3,2,1,0:T(8,128)}) custom-call(s32[3]{0:T(128)S(1)} %pad_add_fusion.place_ref, bf16[8,256,512]{2,1,0:T(8,128)(2,1)S(1)} %copy-done.2, bf16[8,256,256]{2,1,0:T(8,128)(2,1)S(1)} %get-tuple-element.31.own1_ref, bf16[8,384,512]{2,1,0:T(8,128)(2,1)S(1)} %early_columns.1.early_ref, ...), custom_call_target="tpu_custom_call" | custom-call | tf_op jit(solution)/shard_map/cross_tiles/pallas_call | solution.py:267
  (27 shorter events, 5.2 us)
Async XLA Ops:
  7.4 64.2 %all-to-all-start = ((bf16[64,32,512]{2,1,0:T(8,128)(2,1)}), bf16[64,32,512]{2,1,0:T(8,128)(2,1)S(1)}, u32[]{:S(2)}, u32[]{:S(2)}) async-start(bf16[64,32,512]{2,1,0:T(8,128)(2,1)} %filter_section.3), calls=%async_computation | async-start | bytes 4194304 | tf_op jit(solution)/shard_map/all_to_all | solution.py:305
  20.2 52.7 %copy-start.8 = (bf16[256,256]{1,0:T(8,128)(2,1)S(1)}, bf16[256,256]{1,0:T(8,128)(2,1)}, u32[]{:S(2)}) copy-start(bf16[256,256]{1,0:T(8,128)(2,1)} %constant.39.clone.order_ref) | copy-start | bytes 393220
  25.2 20.4 %collective-permute-start = (bf16[32,32,256]{2,1,0:T(8,128)(2,1)}, bf16[32,32,256]{2,1,0:T(8,128)(2,1)S(1)}, u32[]{:S(2)}, u32[]{:S(2)}) collective-permute-start(bf16[32,32,256]{2,1,0:T(8,128)(2,1)} %get-tuple-element.22), channel_id=1, source_target_pairs={{0,128},{128,0},{1,129},{129,1},{2,130},{130,2},{3,131},{131,3},{4... | collective-permute-start | bytes 1572872 | tf_op jit(solution)/shard_map/ppermute | solution.py:306
  45.6 1.0 copy-start.7
  71.6 1.3 copy-start.3
  72.9 1.6 %copy-start.4 = (bf16[64,32,512]{2,1,0:T(8,128)(2,1)S(1)}, bf16[64,32,512]{2,1,0:T(8,128)(2,1)}, u32[]{:S(2)}) copy-start(bf16[64,32,512]{2,1,0:T(8,128)(2,1)} %copy-done.3) | copy-start | bytes 6291460
  76.4 1.0 copy-start.9
  77.4 38.2 %copy-start = (bf16[8,256,512]{2,1,0:T(8,128)(2,1)}, bf16[8,256,512]{2,1,0:T(8,128)(2,1)S(1)}, u32[]{:S(2)}) copy-start(bf16[8,256,512]{2,1,0:T(8,128)(2,1)S(1)} %get-tuple-element.27.own0_ref) | copy-start | bytes 6291460
  77.4 27.0 %collective-permute-start.1 = (bf16[8,128,512]{2,1,0:T(8,128)(2,1)}, bf16[8,128,512]{2,1,0:T(8,128)(2,1)S(1)}, u32[]{:S(2)}, u32[]{:S(2)}) collective-permute-start(bf16[8,128,512]{2,1,0:T(8,128)(2,1)} %get-tuple-element.25), channel_id=1, source_target_pairs={{0,3},{1,2},{2,1},{3,0},{4,7},{5,6},{6,5},{7,4},{8,11},{9,10},{10,... | collective-permute-start | bytes 3145736 | tf_op jit(solution)/shard_map/ppermute | solution.py:295
  77.5 38.0 %collective-permute-start.3 = (bf16[8,256,512]{2,1,0:T(8,128)(2,1)S(1)}, bf16[8,256,512]{2,1,0:T(8,128)(2,1)}, u32[]{:S(2)}, u32[]{:S(2)}) collective-permute-start(bf16[8,256,512]{2,1,0:T(8,128)(2,1)S(1)} %get-tuple-element.27.own0_ref), channel_id=1, source_target_pairs={{0,1},{2,3},{4,5},{6,7},{8,9},{10,11},{12,13},{14,15},{16,17},{18,... | collective-permute-start | bytes 6291464 | tf_op jit(solution)/shard_map/ppermute | solution.py:297
  83.5 35.2 %all-to-all-start.1 = ((bf16[32,2,32,256]{3,2,1,0:T(8,128)(2,1)}), bf16[32,2,32,256]{3,2,1,0:T(8,128)(2,1)}, u32[]{:S(2)}, u32[]{:S(2)}) async-start(bf16[32,2,32,256]{3,2,1,0:T(8,128)(2,1)} %merge_sides.1), calls=%async_computation.1 | async-start | bytes 2097152 | tf_op jit(solution)/shard_map/all_to_all | solution.py:308
  88.8 26.8 %collective-permute-start.2 = (bf16[8,128,512]{2,1,0:T(8,128)(2,1)}, bf16[8,128,512]{2,1,0:T(8,128)(2,1)S(1)}, u32[]{:S(2)}, u32[]{:S(2)}) collective-permute-start(bf16[8,128,512]{2,1,0:T(8,128)(2,1)} %copy-done.9), channel_id=1, source_target_pairs={{1,2},{3,0},{5,6},{7,4},{9,10},{11,8},{13,14},{15,12},{17,18},{19,... | collective-permute-start | bytes 3145736 | tf_op jit(solution)/shard_map/ppermute | solution.py:296
  104.3 11.2 %collective-permute-start.4 = (bf16[8,128,512]{2,1,0:T(8,128)(2,1)S(1)}, bf16[8,128,512]{2,1,0:T(8,128)(2,1)S(1)}, u32[]{:S(2)}, u32[]{:S(2)}) collective-permute-start(bf16[8,128,512]{2,1,0:T(8,128)(2,1)S(1)} %collective-permute-done.1.f_ref), channel_id=1, source_target_pairs={{0,1},{1,0},{2,3},{3,2},{4,5},{5,4},{6,7},{7,6},{8,9},{9,8},{10,11... | collective-permute-start | bytes 3145736 | tf_op jit(solution)/shard_map/ppermute | solution.py:301
  104.4 1.0 copy-start.5
  115.6 1.2 copy-start.6
  120.3 3.6 %collective-permute-start.6 = (bf16[8,256,256]{2,1,0:T(8,128)(2,1)S(1)}, bf16[8,256,256]{2,1,0:T(8,128)(2,1)S(1)}, u32[]{:S(2)}, u32[]{:S(2)}) collective-permute-start(bf16[8,256,256]{2,1,0:T(8,128)(2,1)S(1)} %get-tuple-element.31.own1_ref), channel_id=1, source_target_pairs={{0,1},{2,3},{4,5},{6,7},{8,9},{10,11},{12,13},{14,15},{16,17},{18,... | collective-permute-start | bytes 3145736 | tf_op jit(solution)/shard_map/ppermute | solution.py:297
  121.7 13.8 %collective-permute-start.5 = (bf16[8,128,256]{2,1,0:T(8,128)(2,1)S(1)}, bf16[8,128,256]{2,1,0:T(8,128)(2,1)S(1)}, u32[]{:S(2)}, u32[]{:S(2)}) collective-permute-start(bf16[8,128,256]{2,1,0:T(8,128)(2,1)S(1)} %get-tuple-element.29), channel_id=1, source_target_pairs={{0,3},{1,2},{2,1},{3,0},{4,7},{5,6},{6,5},{7,4},{8,11},{9,10},{10,... | collective-permute-start | bytes 1572872 | tf_op jit(solution)/shard_map/ppermute | solution.py:295
  121.8 19.3 %collective-permute-start.7 = (bf16[8,128,256]{2,1,0:T(8,128)(2,1)S(1)}, bf16[8,128,256]{2,1,0:T(8,128)(2,1)S(1)}, u32[]{:S(2)}, u32[]{:S(2)}) collective-permute-start(bf16[8,128,256]{2,1,0:T(8,128)(2,1)S(1)} %get-tuple-element.35), channel_id=1, source_target_pairs={{1,2},{3,0},{5,6},{7,4},{9,10},{11,8},{13,14},{15,12},{17,18},{19,... | collective-permute-start | bytes 1572872 | tf_op jit(solution)/shard_map/ppermute | solution.py:296
  123.9 1.6 %copy-start.1 = (bf16[8,256,512]{2,1,0:T(8,128)(2,1)S(1)}, bf16[8,256,512]{2,1,0:T(8,128)(2,1)}, u32[]{:S(2)}) copy-start(bf16[8,256,512]{2,1,0:T(8,128)(2,1)} %copy-done) | copy-start | bytes 6291460
  125.5 15.6 %copy-start.2 = (bf16[8,256,512]{2,1,0:T(8,128)(2,1)S(1)}, bf16[8,256,512]{2,1,0:T(8,128)(2,1)}, u32[]{:S(2)}) copy-start(bf16[8,256,512]{2,1,0:T(8,128)(2,1)} %copy-done) | copy-start | bytes 6291460
  135.5 5.6 %collective-permute-start.8 = (bf16[8,128,256]{2,1,0:T(8,128)(2,1)S(1)}, bf16[8,128,256]{2,1,0:T(8,128)(2,1)S(1)}, u32[]{:S(2)}, u32[]{:S(2)}) collective-permute-start(bf16[8,128,256]{2,1,0:T(8,128)(2,1)S(1)} %collective-permute-done.5.f_ref), channel_id=1, source_target_pairs={{0,1},{1,0},{2,3},{3,2},{4,5},{5,4},{6,7},{7,6},{8,9},{9,8},{10,11... | collective-permute-start | bytes 1572872 | tf_op jit(solution)/shard_map/ppermute | solution.py:301

commit v6 on v5

--- a/solution.py
+++ b/solution.py
@@ -148,30 +148,47 @@
     )(place, stay, got)
 
 
-def rows_kernel(place_ref, order_ref, source_ref, cross_ref, rest_ref, whole_ref):
+def rows_kernel(place_ref, order_ref, source_ref, cross_ref, rest_ref, whole_ref, source, held, in_sem, out_sem, whole_sem):
     chip = place_ref[0]
-    order = order_ref[...]
-    for out_ref, half in ((cross_ref, 1 - chip), (rest_ref, chip)):
+    halves = (1 - chip, chip)
+    arriving = []
+    for k, half in enumerate(halves):
+        part = source_ref.at[pl.ds(half * 32, 32)] if len(source_ref.shape) == 3 else source_ref.at[:, half]
+        arriving.append(pltpu.make_async_copy(part, source.at[k], in_sem.at[k]))
+        arriving[k].start()
+    leaving = []
+    for k, (half, out_ref) in enumerate(zip(halves, (cross_ref, rest_ref))):
+        arriving[k].wait()
         for g in range(4):
-            if len(source_ref.shape) == 3:
-                rows = source_ref[pl.ds(half * 32 + g * 8, 8)]
-            else:
-                rows = source_ref[g * 8 : (g + 1) * 8, half]
-            turned = jnp.dot(order, rows.reshape(256, rows.shape[-1]), preferred_element_type=jnp.float32).astype(jnp.bfloat16)
+            rows = source[k, g * 8 : (g + 1) * 8].reshape(256, source.shape[-1])
+            turned = jnp.dot(order_ref[...], rows, preferred_element_type=jnp.float32).astype(jnp.bfloat16)
             for c in range(8):
-                part = turned[c * 32 : (c + 1) * 32]
-                out_ref[c, g * 32 : (g + 1) * 32, :] = part
-                whole_ref[c, pl.ds(pl.multiple_of(half * 128 + g * 32, 32), 32), :] = part
+                held[k, c, g * 32 : (g + 1) * 32, :] = turned[c * 32 : (c + 1) * 32]
+        block_half = whole_ref.at[:, pl.ds(pl.multiple_of(half * 128, 128), 128)]
+        leaving.append(pltpu.make_async_copy(held.at[k], out_ref, out_sem.at[k]))
+        leaving.append(pltpu.make_async_copy(held.at[k], block_half, whole_sem.at[k]))
+        leaving[-2].start()
+        leaving[-1].start()
+    for copy in leaving:
+        copy.wait()
 
 
 def channel_rows(place, order, source):
     lanes = source.shape[-1]
+    in_hbm = pl.BlockSpec(memory_space=pltpu.HBM)
     shapes = [(8, 128, lanes), (8, 128, lanes), (8, BLOCK, lanes)]
     return pl.pallas_call(
         rows_kernel,
-        in_specs=[SMALL, IN_VMEM, IN_VMEM],
-        out_specs=[IN_VMEM] * 3,
-        out_shape=[jax.ShapeDtypeStruct(shape, jnp.bfloat16) for shape in shapes],
+        in_specs=[SMALL, IN_VMEM, pl.BlockSpec(memory_space=pl.ANY)],
+        out_specs=[in_hbm] * 3,
+        out_shape=[pltpu.HBM(shape, jnp.bfloat16) for shape in shapes],
+        scratch_shapes=[
+            pltpu.VMEM((2, 32, 32, lanes), jnp.bfloat16),
+            pltpu.VMEM((2, 8, 128, lanes), jnp.bfloat16),
+            pltpu.SemaphoreType.DMA((2,)),
+            pltpu.SemaphoreType.DMA((2,)),
+            pltpu.SemaphoreType.DMA((2,)),
+        ],
         compiler_params=pltpu.CompilerParams(vmem_limit_bytes=40 * 1024 * 1024),
         name="channel_rows",
     )(place, order, source)
@@ -185,14 +202,14 @@
 
 
 def tile_products(rows, cols):
-    return lax.dot_general(stacked(rows), cols, NT, preferred_element_type=jnp.float32) * (1.0 / SPECTRA)
+    return lax.dot_general(stacked(rows), cols, NT, preferred_element_type=jnp.float32)
 
 
 def self_kernel(own0_ref, own1_ref, self_ref, self_held, sem):
     copies = []
     for c in range(8):
         rows = jnp.concatenate([own0_ref[c], own1_ref[c]], axis=1)
-        product = tile_products(rows, rows)
+        product = tile_products(rows, rows) * (1.0 / SPECTRA)
         self_held[0, c] = product[:BLOCK]
         self_held[1, c] = product[BLOCK:]
         copies.append(pltpu.make_async_copy(self_held.at[:, c], self_ref.at[:, c], sem.at[c]))
@@ -228,28 +245,31 @@
     out_ref[:, BLOCK:, :] = s_ref[...]
 
 
-def early_kernel(place_ref, f_ref, g_ref, h_ref, s_ref, out_ref):
-    put_columns(place_ref, f_ref, g_ref, h_ref, s_ref, out_ref)
-
-
-def early_columns(place, *received):
+def early_kernel(place_ref, own_ref, f_ref, g_ref, h_ref, s_ref, out_ref, held):
+    put_columns(place_ref, f_ref, g_ref, h_ref, s_ref, held)
+    for c in range(8):
+        out_ref[c] = tile_products(own_ref[c], held[c])
+
+
+def early_products(place, own, *received):
+    columns = BLOCK + BLOCK // 2
     return pl.pallas_call(
         early_kernel,
-        in_specs=[SMALL] + [IN_VMEM] * 4,
+        in_specs=[SMALL] + [IN_VMEM] * 5,
         out_specs=IN_VMEM,
-        out_shape=jax.ShapeDtypeStruct((8, BLOCK + BLOCK // 2, received[0].shape[-1]), jnp.bfloat16),
-        compiler_params=pltpu.CompilerParams(vmem_limit_bytes=40 * 1024 * 1024),
-        name="early_columns",
-    )(place, *received)
-
-
-def cross_kernel(place_ref, own0_ref, own1_ref, early_ref, f_ref, g_ref, h_ref, s_ref, prior_ref, far_ref,
+        out_shape=jax.ShapeDtypeStruct((8, 2 * BLOCK, columns), jnp.float32),
+        scratch_shapes=[pltpu.VMEM((8, columns, own.shape[-1]), jnp.bfloat16)],
+        compiler_params=pltpu.CompilerParams(vmem_limit_bytes=40 * 1024 * 1024),
+        name="early_products",
+    )(place, own, *received)
+
+
+def cross_kernel(place_ref, own_ref, early_ref, f_ref, g_ref, h_ref, s_ref, prior_ref, far_ref,
                  held, prior_held, far_held, prior_sem, far_sem):
     put_columns(place_ref, f_ref, g_ref, h_ref, s_ref, held)
     copies = []
     for c in range(8):
-        rows = jnp.concatenate([own0_ref[c], own1_ref[c]], axis=1)
-        product = tile_products(rows, jnp.concatenate([early_ref[c], held[c]], axis=1))
+        product = (tile_products(own_ref[c], held[c]) + early_ref[c]) * (1.0 / SPECTRA)
         for p in range(2):
             prior_held[p, c] = product[p * BLOCK : (p + 1) * BLOCK, :BLOCK]
             far_held[p, c] = product[p * BLOCK : (p + 1) * BLOCK, BLOCK:]
@@ -261,12 +281,12 @@
         copy.wait()
 
 
-def cross_tiles(place, own0, own1, early, *late):
+def cross_tiles(place, own, early, *late):
     in_hbm = pl.BlockSpec(memory_space=pltpu.HBM)
     prior_shape, far_shape = (2, 8, BLOCK, BLOCK), (2, 8, BLOCK, BLOCK // 2)
     return pl.pallas_call(
         cross_kernel,
-        in_specs=[SMALL] + [IN_VMEM] * (3 + len(late)),
+        in_specs=[SMALL] + [IN_VMEM] * (2 + len(late)),
         out_specs=[in_hbm, in_hbm],
         out_shape=[pltpu.HBM(prior_shape, jnp.float32), pltpu.HBM(far_shape, jnp.float32)],
         scratch_shapes=[
@@ -278,7 +298,7 @@
         ],
         compiler_params=pltpu.CompilerParams(vmem_limit_bytes=40 * 1024 * 1024),
         name="cross_tiles",
-    )(place, own0, own1, early, *late)
+    )(place, own, early, *late)
 
 
 CROSSED = [(0, 3), (1, 2), (2, 1), (3, 0)]
@@ -307,15 +327,16 @@
     late, source0 = lax.optimization_barrier((late, source0))
     source1 = lax.all_to_all(late, "plane", split_axis=0, concat_axis=0, tiled=True)
     crossing0, rest0, own0 = channel_rows(place, order, source0)
-    f, g, h = exchange(crossing0, rest0, own0)
-    held0 = early_columns(place, f, g, h, swap(f))
-    source1, held0 = lax.optimization_barrier((source1, held0))
+    f0, g0, h0 = exchange(crossing0, rest0, own0)
+    s0 = swap(f0)
+    source1, f0, g0, h0, s0 = lax.optimization_barrier((source1, f0, g0, h0, s0))
     crossing1, rest1, own1 = channel_rows(place, order, source1)
-    f, g, h = exchange(crossing1, rest1, own1)
-    own1, h = lax.optimization_barrier((own1, h))
+    f1, g1, h1 = exchange(crossing1, rest1, own1)
+    own0, own1, f0, h1 = lax.optimization_barrier((own0, own1, f0, h1))
+    early = early_products(place, own0, f0, g0, h0, s0)
     self_vis = self_tiles(own0, own1)
-    f, self_vis = lax.optimization_barrier((f, self_vis))
-    prior_vis, far_vis = cross_tiles(place, own0, own1, held0, f, g, h, swap(f))
+    f1, self_vis, early = lax.optimization_barrier((f1, self_vis, early))
+    prior_vis, far_vis = cross_tiles(place, own1, early, f1, g1, h1, swap(f1))
     return (self_vis, prior_vis, far_vis)
 
 

time: 147 us -> 142 us (0.966)
  local copies, waits for them, and re-layouts: 8.7 us -> 3.27 us
  Pallas kernels: 26.7 us -> 30.2 us
  waiting for transfers between devices: 79.8 us -> 76.6 us
    unnamed x20 -> x14, local copies, waits for them, and re-layouts: 8.7 us -> 3.27 us
    ppermute x2, waiting for transfers between devices: 21.2 us -> 16.9 us  [exchange(): f = lax.ppermute(crossing, 'narrow', CROSSED)]
    pallas_call x4, Pallas kernels: 10.5 us -> 14 us  [the longest x2 5.49 us: channel_rows(): pl.pallas_call(rows_kernel, in_specs=[SMALL, IN_VMEM, pl.BlockSpec(memory...]
  transfers between devices with their start and end apart: 11 -> 11, of which waited for: 7 -> 7; matrix products, arithmetic and copies ran while one was open for 0% -> 0% of each run, Pallas kernels for 8% -> 10%
where the time goes in v6:
time: 142 us; the launch traced here: 141 us
  waiting for transfers between devices  76.6 us (54%)
  Pallas kernels  30.2 us (21%)
  starting transfers between devices  30.1 us (21%)
  local copies, waits for them, and re-layouts  3.27 us (2%)
    all_to_all x1, waiting for transfers between devices, on_device(): lax.all_to_all(early, ('side', 'plane'), split_axis=0, concat_axis=0, til...  23.3 us
    ppermute x1, waiting for transfers between devices, on_device(): late = merge(place, stay, lax.ppermute(leave, 'side', [(0, 1), (1, 0)]))  18.7 us
    ppermute x2, waiting for transfers between devices, exchange(): f = lax.ppermute(crossing, 'narrow', CROSSED)  16.9 us
    ppermute x2, waiting for transfers between devices, exchange(): g = lax.ppermute(rest, 'narrow', ODD_OVER)  16.7 us
    all_to_all x1, starting transfers between devices, on_device(): lax.all_to_all(early, ('side', 'plane'), split_axis=0, concat_axis=0, til...  12.8 us
    pallas_call x2, Pallas kernels, filter_section(): pl.pallas_call(functools.partial(spectra_kernel, first, split), in_specs=...  11.6 us
    ppermute x2, starting transfers between devices, exchange(): h = lax.ppermute(whole, 'narrow', EVEN_UP)  7.28 us
    pallas_call x2, Pallas kernels, channel_rows(): pl.pallas_call(rows_kernel, in_specs=[SMALL, IN_VMEM, pl.BlockSpec(memory...  5.49 us
  transfers between devices with their start and end apart: 11, of which 7 were waited for; matrix products, arithmetic and copies ran while one was open for 0% of the time, Pallas kernels for 10%

profile of v6, /device:TPU:24, one launch (start us, length us, event | category | flops | bytes accessed | tf_op | source)
XLA Modules:
  0.0 141.2 jit_solution(1656411549274608253)
XLA Ops:
  0.7 6.6 %filter_section.3 = bf16[64,32,512]{2,1,0:T(8,128)(2,1)} custom-call(s32[3]{0:T(128)S(1)} %pad_add_fusion.place_ref, bf16[4,396288]{1,0:T(4,128)(2,1)} %x_ref.3, bf16[1024,1024]{1,0:T(8,128)(2,1)} %constant.38.clone.table_ref, f32[4,1024]{1,0:T(4,128)} %taps_ref.3), custom_call_target="tpu_custom_call" | custom-call | tf_op jit(solution)/shard_map/filter_section/pallas_call | solution.py:107
  7.4 12.8 %all-to-all-start = ((bf16[64,32,512]{2,1,0:T(8,128)(2,1)}), bf16[64,32,512]{2,1,0:T(8,128)(2,1)S(1)}, u32[]{:S(2)}, u32[]{:S(2)}) async-start(bf16[64,32,512]{2,1,0:T(8,128)(2,1)} %filter_section.3), calls=%async_computation | async-start | bytes 4194304 | tf_op jit(solution)/shard_map/all_to_all | solution.py:325
  20.2 5.0 %filter_section.2 = (bf16[32,32,256]{2,1,0:T(8,128)(2,1)}, bf16[32,32,256]{2,1,0:T(8,128)(2,1)}) custom-call(s32[3]{0:T(128)S(1)} %pad_add_fusion.place_ref, bf16[4,396288]{1,0:T(4,128)(2,1)} %x_ref.3, bf16[1024,1024]{1,0:T(8,128)(2,1)} %constant.38.clone.table_ref, f32[4,1024]{1,0:T(4,128)} %taps_ref.3), custom_call_target="tpu_custom_call" | custom-call | tf_op jit(solution)/shard_map/filter_section/pallas_call | solution.py:107
  25.2 1.7 %collective-permute-start = (bf16[32,32,256]{2,1,0:T(8,128)(2,1)}, bf16[32,32,256]{2,1,0:T(8,128)(2,1)S(1)}, u32[]{:S(2)}, u32[]{:S(2)}) collective-permute-start(bf16[32,32,256]{2,1,0:T(8,128)(2,1)} %get-tuple-element.28), channel_id=1, source_target_pairs={{0,128},{128,0},{1,129},{129,1},{2,130},{130,2},{3,131},{131,3},{4... | collective-permute-start | bytes 1572872 | tf_op jit(solution)/shard_map/ppermute | solution.py:326
  26.8 18.7 %collective-permute-done.got_ref = bf16[32,32,256]{2,1,0:T(8,128)(2,1)S(1)} collective-permute-done((bf16[32,32,256]{2,1,0:T(8,128)(2,1)}, bf16[32,32,256]{2,1,0:T(8,128)(2,1)S(1)}, u32[]{:S(2)}, u32[]{:S(2)}) %collective-permute-start) | collective-permute-done | bytes 524320 | tf_op jit(solution)/shard_map/ppermute | solution.py:326
  45.6 1.0 copy-done.5
  46.6 1.6 %merge_sides.1 = bf16[32,2,32,256]{3,2,1,0:T(8,128)(2,1)} custom-call(s32[3]{0:T(128)S(1)} %pad_add_fusion.place_ref, bf16[32,32,256]{2,1,0:T(8,128)(2,1)S(1)} %copy-done.5, bf16[32,32,256]{2,1,0:T(8,128)(2,1)S(1)} %collective-permute-done.got_ref), custom_call_target="tpu_custom_call" | custom-call | tf_op jit(solution)/shard_map/merge_sides/pallas_call | solution.py:140
  48.2 23.3 %all-to-all-done.source_ref = bf16[64,32,512]{2,1,0:T(8,128)(2,1)S(1)} async-done(((bf16[64,32,512]{2,1,0:T(8,128)(2,1)}), bf16[64,32,512]{2,1,0:T(8,128)(2,1)S(1)}, u32[]{:S(2)}, u32[]{:S(2)}) %all-to-all-start) | async-done | bytes 2097184 | tf_op jit(solution)/shard_map/all_to_all | solution.py:325
  71.6 3.2 %channel_rows.2 = (bf16[8,128,512]{2,1,0:T(8,128)(2,1)}, bf16[8,128,512]{2,1,0:T(8,128)(2,1)}, bf16[8,256,512]{2,1,0:T(8,128)(2,1)}) custom-call(s32[3]{0:T(128)S(1)} %pad_add_fusion.place_ref, bf16[256,256]{1,0:T(8,128)(2,1)S(1)} %copy-done.6, bf16[64,32,512]{2,1,0:T(8,128)(2,1)S(1)} %all-to-all-done.source_ref), custom_call_target="tpu_custom_call" | custom-call | tf_op jit(solution)/shard_map/channel_rows/pallas_call | solution.py:180
  75.0 5.9 %collective-permute-start.3 = (bf16[8,256,512]{2,1,0:T(8,128)(2,1)}, bf16[8,256,512]{2,1,0:T(8,128)(2,1)}, u32[]{:S(2)}, u32[]{:S(2)}) collective-permute-start(bf16[8,256,512]{2,1,0:T(8,128)(2,1)} %get-tuple-element.38.own0_ref.own_ref), channel_id=1, source_target_pairs={{0,1},{2,3},{4,5},{6,7},{8,9},{10,11},{12,13},{14,15},{16,17},{18,... | collective-permute-start | bytes 6291464 | tf_op jit(solution)/shard_map/ppermute | solution.py:317
  80.9 5.3 %all-to-all-start.1 = ((bf16[32,2,32,256]{3,2,1,0:T(8,128)(2,1)}), bf16[32,2,32,256]{3,2,1,0:T(8,128)(2,1)S(1)}, u32[]{:S(2)}, u32[]{:S(2)}) async-start(bf16[32,2,32,256]{3,2,1,0:T(8,128)(2,1)} %merge_sides.1), calls=%async_computation.1 | async-start | bytes 2097152 | tf_op jit(solution)/shard_map/all_to_all | solution.py:328
  86.2 1.3 collective-permute-start.2
  87.5 14.4 %collective-permute-done.1.f_ref = bf16[8,128,512]{2,1,0:T(8,128)(2,1)} collective-permute-done((bf16[8,128,512]{2,1,0:T(8,128)(2,1)}, bf16[8,128,512]{2,1,0:T(8,128)(2,1)}, u32[]{:S(2)}, u32[]{:S(2)}) %collective-permute-start.1) | collective-permute-done | bytes 1048608 | tf_op jit(solution)/shard_map/ppermute | solution.py:315
  101.9 11.1 %collective-permute-done.2.g_ref = bf16[8,128,512]{2,1,0:T(8,128)(2,1)S(1)} collective-permute-done((bf16[8,128,512]{2,1,0:T(8,128)(2,1)}, bf16[8,128,512]{2,1,0:T(8,128)(2,1)S(1)}, u32[]{:S(2)}, u32[]{:S(2)}) %collective-permute-start.2) | collective-permute-done | bytes 1048608 | tf_op jit(solution)/shard_map/ppermute | solution.py:316
  113.1 1.0 copy-done.3
  114.0 2.3 %channel_rows.3 = (bf16[8,128,256]{2,1,0:T(8,128)(2,1)}, bf16[8,128,256]{2,1,0:T(8,128)(2,1)}, bf16[8,256,256]{2,1,0:T(8,128)(2,1)}) custom-call(s32[3]{0:T(128)S(1)} %pad_add_fusion.place_ref, bf16[256,256]{1,0:T(8,128)(2,1)S(1)} %copy-done.6, bf16[32,2,32,256]{3,2,1,0:T(8,128)(2,1)S(1)} %all-to-all-done.1.source_ref), custom_call_target="tpu_custom_call" | custom-call | tf_op jit(solution)/shard_map/channel_rows/pallas_call | solution.py:180
  116.4 1.4 collective-permute-start.6
  117.8 1.5 %collective-permute-start.7 = (bf16[8,128,256]{2,1,0:T(8,128)(2,1)}, bf16[8,128,256]{2,1,0:T(8,128)(2,1)S(1)}, u32[]{:S(2)}, u32[]{:S(2)}) collective-permute-start(bf16[8,128,256]{2,1,0:T(8,128)(2,1)} %get-tuple-element.47), channel_id=1, source_target_pairs={{1,2},{3,0},{5,6},{7,4},{9,10},{11,8},{13,14},{15,12},{17,18},{19,... | collective-permute-start | bytes 1572872 | tf_op jit(solution)/shard_map/ppermute | solution.py:316
  120.1 1.2 copy-done.1
  121.4 3.1 %self_tiles.1 = f32[2,8,256,256]{3,2,1,0:T(8,128)} custom-call(bf16[8,256,512]{2,1,0:T(8,128)(2,1)S(1)} %copy-done, bf16[8,256,256]{2,1,0:T(8,128)(2,1)S(1)} %copy-done.1), custom_call_target="tpu_custom_call" | custom-call | tf_op jit(solution)/shard_map/self_tiles/pallas_call | solution.py:222
  124.5 4.8 %early_products.1.early_ref = f32[8,512,384]{2,1,0:T(8,128)S(1)} custom-call(s32[3]{0:T(128)S(1)} %pad_add_fusion.place_ref, bf16[8,256,512]{2,1,0:T(8,128)(2,1)S(1)} %copy-done, bf16[8,128,512]{2,1,0:T(8,128)(2,1)} %collective-permute-done.1.f_ref, bf16[8,128,512]{2,1,0:T(8,128)(2,1)S(1)} %copy-done.4, bf16[8,256,512]{2,1,0:T(8,128)(2,1)} %collective-permute-done.3.h_ref, ...), custom_call_target="tpu_custom_call" | custom-call | tf_op jit(solution)/shard_map/early_products/pallas_call | solution.py:256
  129.2 2.5 %collective-permute-done.5.f_ref = bf16[8,128,256]{2,1,0:T(8,128)(2,1)S(1)} collective-permute-done((bf16[8,128,256]{2,1,0:T(8,128)(2,1)}, bf16[8,128,256]{2,1,0:T(8,128)(2,1)S(1)}, u32[]{:S(2)}, u32[]{:S(2)}) %collective-permute-start.5) | collective-permute-done | bytes 524320 | tf_op jit(solution)/shard_map/ppermute | solution.py:315
  131.8 5.6 %collective-permute-done.7.g_ref = bf16[8,128,256]{2,1,0:T(8,128)(2,1)S(1)} collective-permute-done((bf16[8,128,256]{2,1,0:T(8,128)(2,1)}, bf16[8,128,256]{2,1,0:T(8,128)(2,1)S(1)}, u32[]{:S(2)}, u32[]{:S(2)}) %collective-permute-start.7) | collective-permute-done | bytes 524320 | tf_op jit(solution)/shard_map/ppermute | solution.py:316
  137.4 3.7 %cross_tiles.1 = (f32[2,8,256,256]{3,2,1,0:T(8,128)}, f32[2,8,256,128]{3,2,1,0:T(8,128)}) custom-call(s32[3]{0:T(128)S(1)} %pad_add_fusion.place_ref, bf16[8,256,256]{2,1,0:T(8,128)(2,1)S(1)} %copy-done.2, f32[8,512,384]{2,1,0:T(8,128)S(1)} %early_products.1.early_ref, bf16[8,128,256]{2,1,0:T(8,128)(2,1)S(1)} %collective-permute-done.5.f_ref, ...), custom_call_target="tpu_custom_call" | custom-call | tf_op jit(solution)/shard_map/cross_tiles/pallas_call | solution.py:287
  (21 shorter events, 1.3 us)
Async XLA Ops:
  7.4 64.2 %all-to-all-start = ((bf16[64,32,512]{2,1,0:T(8,128)(2,1)}), bf16[64,32,512]{2,1,0:T(8,128)(2,1)S(1)}, u32[]{:S(2)}, u32[]{:S(2)}) async-start(bf16[64,32,512]{2,1,0:T(8,128)(2,1)} %filter_section.3), calls=%async_computation | async-start | bytes 4194304 | tf_op jit(solution)/shard_map/all_to_all | solution.py:325
  20.2 51.4 %copy-start.6 = (bf16[256,256]{1,0:T(8,128)(2,1)S(1)}, bf16[256,256]{1,0:T(8,128)(2,1)}, u32[]{:S(2)}) copy-start(bf16[256,256]{1,0:T(8,128)(2,1)} %constant.39.clone.order_ref) | copy-start | bytes 393220
  25.2 20.4 %collective-permute-start = (bf16[32,32,256]{2,1,0:T(8,128)(2,1)}, bf16[32,32,256]{2,1,0:T(8,128)(2,1)S(1)}, u32[]{:S(2)}, u32[]{:S(2)}) collective-permute-start(bf16[32,32,256]{2,1,0:T(8,128)(2,1)} %get-tuple-element.28), channel_id=1, source_target_pairs={{0,128},{128,0},{1,129},{129,1},{2,130},{130,2},{3,131},{131,3},{4... | collective-permute-start | bytes 1572872 | tf_op jit(solution)/shard_map/ppermute | solution.py:326
  45.6 1.0 copy-start.5
  74.8 45.4 %copy-start = (bf16[8,256,512]{2,1,0:T(8,128)(2,1)S(1)}, bf16[8,256,512]{2,1,0:T(8,128)(2,1)}, u32[]{:S(2)}) copy-start(bf16[8,256,512]{2,1,0:T(8,128)(2,1)} %get-tuple-element.38.own0_ref.own_ref) | copy-start | bytes 6291460
  74.8 27.1 %collective-permute-start.1 = (bf16[8,128,512]{2,1,0:T(8,128)(2,1)}, bf16[8,128,512]{2,1,0:T(8,128)(2,1)}, u32[]{:S(2)}, u32[]{:S(2)}) collective-permute-start(bf16[8,128,512]{2,1,0:T(8,128)(2,1)} %get-tuple-element.31), channel_id=1, source_target_pairs={{0,3},{1,2},{2,1},{3,0},{4,7},{5,6},{6,5},{7,4},{8,11},{9,10},{10,... | collective-permute-start | bytes 3145736 | tf_op jit(solution)/shard_map/ppermute | solution.py:315
  75.0 39.0 %collective-permute-start.3 = (bf16[8,256,512]{2,1,0:T(8,128)(2,1)}, bf16[8,256,512]{2,1,0:T(8,128)(2,1)}, u32[]{:S(2)}, u32[]{:S(2)}) collective-permute-start(bf16[8,256,512]{2,1,0:T(8,128)(2,1)} %get-tuple-element.38.own0_ref.own_ref), channel_id=1, source_target_pairs={{0,1},{2,3},{4,5},{6,7},{8,9},{10,11},{12,13},{14,15},{16,17},{18,... | collective-permute-start | bytes 6291464 | tf_op jit(solution)/shard_map/ppermute | solution.py:317
  80.9 33.1 %all-to-all-start.1 = ((bf16[32,2,32,256]{3,2,1,0:T(8,128)(2,1)}), bf16[32,2,32,256]{3,2,1,0:T(8,128)(2,1)S(1)}, u32[]{:S(2)}, u32[]{:S(2)}) async-start(bf16[32,2,32,256]{3,2,1,0:T(8,128)(2,1)} %merge_sides.1), calls=%async_computation.1 | async-start | bytes 2097152 | tf_op jit(solution)/shard_map/all_to_all | solution.py:328
  86.2 26.8 %collective-permute-start.2 = (bf16[8,128,512]{2,1,0:T(8,128)(2,1)}, bf16[8,128,512]{2,1,0:T(8,128)(2,1)S(1)}, u32[]{:S(2)}, u32[]{:S(2)}) collective-permute-start(bf16[8,128,512]{2,1,0:T(8,128)(2,1)} %get-tuple-element.32), channel_id=1, source_target_pairs={{1,2},{3,0},{5,6},{7,4},{9,10},{11,8},{13,14},{15,12},{17,18},{19,... | collective-permute-start | bytes 3145736 | tf_op jit(solution)/shard_map/ppermute | solution.py:316
  101.9 12.1 %collective-permute-start.4 = (bf16[8,128,512]{2,1,0:T(8,128)(2,1)}, bf16[8,128,512]{2,1,0:T(8,128)(2,1)}, u32[]{:S(2)}, u32[]{:S(2)}) collective-permute-start(bf16[8,128,512]{2,1,0:T(8,128)(2,1)} %collective-permute-done.1.f_ref), channel_id=1, source_target_pairs={{0,1},{1,0},{2,3},{3,2},{4,5},{5,4},{6,7},{7,6},{8,9},{9,8},{10,11... | collective-permute-start | bytes 3145736 | tf_op jit(solution)/shard_map/ppermute | solution.py:321
  113.1 1.0 copy-start.3
  116.4 3.8 %collective-permute-start.6 = (bf16[8,256,256]{2,1,0:T(8,128)(2,1)}, bf16[8,256,256]{2,1,0:T(8,128)(2,1)S(1)}, u32[]{:S(2)}, u32[]{:S(2)}) collective-permute-start(bf16[8,256,256]{2,1,0:T(8,128)(2,1)} %get-tuple-element.39.own1_ref.own_ref), channel_id=1, source_target_pairs={{0,1},{2,3},{4,5},{6,7},{8,9},{10,11},{12,13},{14,15},{16,17},{18,... | collective-permute-start | bytes 3145736 | tf_op jit(solution)/shard_map/ppermute | solution.py:317
  117.7 14.0 %collective-permute-start.5 = (bf16[8,128,256]{2,1,0:T(8,128)(2,1)}, bf16[8,128,256]{2,1,0:T(8,128)(2,1)S(1)}, u32[]{:S(2)}, u32[]{:S(2)}) collective-permute-start(bf16[8,128,256]{2,1,0:T(8,128)(2,1)} %get-tuple-element.35), channel_id=1, source_target_pairs={{0,3},{1,2},{2,1},{3,0},{4,7},{5,6},{6,5},{7,4},{8,11},{9,10},{10,... | collective-permute-start | bytes 1572872 | tf_op jit(solution)/shard_map/ppermute | solution.py:315
  117.8 19.5 %collective-permute-start.7 = (bf16[8,128,256]{2,1,0:T(8,128)(2,1)}, bf16[8,128,256]{2,1,0:T(8,128)(2,1)S(1)}, u32[]{:S(2)}, u32[]{:S(2)}) collective-permute-start(bf16[8,128,256]{2,1,0:T(8,128)(2,1)} %get-tuple-element.47), channel_id=1, source_target_pairs={{1,2},{3,0},{5,6},{7,4},{9,10},{11,8},{13,14},{15,12},{17,18},{19,... | collective-permute-start | bytes 1572872 | tf_op jit(solution)/shard_map/ppermute | solution.py:316
  120.1 1.2 copy-start.1
  121.4 3.1 %copy-start.4 = (bf16[8,128,512]{2,1,0:T(8,128)(2,1)S(1)}, bf16[8,128,512]{2,1,0:T(8,128)(2,1)}, u32[]{:S(2)}) copy-start(bf16[8,128,512]{2,1,0:T(8,128)(2,1)} %copy-done.3) | copy-start | bytes 3145732
  124.4 12.9 %copy-start.2 = (bf16[8,256,256]{2,1,0:T(8,128)(2,1)S(1)}, bf16[8,256,256]{2,1,0:T(8,128)(2,1)}, u32[]{:S(2)}) copy-start(bf16[8,256,256]{2,1,0:T(8,128)(2,1)} %get-tuple-element.39.own1_ref.own_ref) | copy-start | bytes 3145732
  131.8 5.6 %collective-permute-start.8 = (bf16[8,128,256]{2,1,0:T(8,128)(2,1)S(1)}, bf16[8,128,256]{2,1,0:T(8,128)(2,1)S(1)}, u32[]{:S(2)}, u32[]{:S(2)}) collective-permute-start(bf16[8,128,256]{2,1,0:T(8,128)(2,1)S(1)} %collective-permute-done.5.f_ref), channel_id=1, source_target_pairs={{0,1},{1,0},{2,3},{3,2},{4,5},{5,4},{6,7},{7,6},{8,9},{9,8},{10,11... | collective-permute-start | bytes 1572872 | tf_op jit(solution)/shard_map/ppermute | solution.py:321

commit v7 on v5

--- a/solution.py
+++ b/solution.py
@@ -126,52 +126,77 @@
     )(place, *(pltpu.with_memory_space_constraint(a, pltpu.HBM) for a in (samples, table, pfb_taps)))
 
 
-def merge_kernel(place_ref, stay_ref, got_ref, out_ref, held, sem):
+def merge_kernel(place_ref, stay_ref, got_ref, far_ref, out_ref, held, sem):
     side = place_ref[2]
     held[:, side] = stay_ref[...]
     held[:, 1 - side] = got_ref[...]
+    held[:, 2] = far_ref[...]
     copy = pltpu.make_async_copy(held, out_ref, sem)
     copy.start()
     copy.wait()
 
 
-def merge(place, stay, got):
-    shape = (32, 2) + stay.shape[1:]
+def merge(place, stay, got, far):
+    shape = (32, 3) + stay.shape[1:]
     return pl.pallas_call(
         merge_kernel,
-        in_specs=[SMALL, IN_VMEM, IN_VMEM],
+        in_specs=[SMALL] + [IN_VMEM] * 3,
         out_specs=pl.BlockSpec(memory_space=pltpu.HBM),
         out_shape=pltpu.HBM(shape, jnp.bfloat16),
         scratch_shapes=[pltpu.VMEM(shape, jnp.bfloat16), pltpu.SemaphoreType.DMA],
         compiler_params=pltpu.CompilerParams(vmem_limit_bytes=40 * 1024 * 1024),
         name="merge_sides",
-    )(place, stay, got)
-
-
-def rows_kernel(place_ref, order_ref, source_ref, cross_ref, rest_ref, whole_ref):
+    )(place, stay, got, far)
+
+
+def rows_kernel(place_ref, order_ref, source_ref, first_ref, second_ref, whole_ref, source, held, in_sem, out_sem, whole_sem):
     chip = place_ref[0]
-    order = order_ref[...]
-    for out_ref, half in ((cross_ref, 1 - chip), (rest_ref, chip)):
+    late = len(source_ref.shape) == 4
+    if late:
+        parts = [source_ref.at[:, chip], source_ref.at[:, 2], source_ref.at[:, 1 - chip]]
+        steps = [(first_ref, chip), (second_ref, None), (None, 1 - chip)]
+    else:
+        parts = [source_ref.at[pl.ds(half * 32, 32)] for half in (1 - chip, chip)]
+        steps = [(first_ref, 1 - chip), (second_ref, chip)]
+    arriving = [pltpu.make_async_copy(part, source.at[k], in_sem.at[k]) for k, part in enumerate(parts)]
+    for copy in arriving:
+        copy.start()
+    leaving = []
+    for k, (out_ref, half) in enumerate(steps):
+        arriving[k].wait()
         for g in range(4):
-            if len(source_ref.shape) == 3:
-                rows = source_ref[pl.ds(half * 32 + g * 8, 8)]
-            else:
-                rows = source_ref[g * 8 : (g + 1) * 8, half]
-            turned = jnp.dot(order, rows.reshape(256, rows.shape[-1]), preferred_element_type=jnp.float32).astype(jnp.bfloat16)
+            rows = source[k, g * 8 : (g + 1) * 8].reshape(256, source.shape[-1])
+            turned = jnp.dot(order_ref[...], rows, preferred_element_type=jnp.float32).astype(jnp.bfloat16)
             for c in range(8):
-                part = turned[c * 32 : (c + 1) * 32]
-                out_ref[c, g * 32 : (g + 1) * 32, :] = part
-                whole_ref[c, pl.ds(pl.multiple_of(half * 128 + g * 32, 32), 32), :] = part
+                held[k, c, g * 32 : (g + 1) * 32, :] = turned[c * 32 : (c + 1) * 32]
+        if out_ref is not None:
+            leaving.append(pltpu.make_async_copy(held.at[k], out_ref, out_sem.at[k]))
+            leaving[-1].start()
+        if half is not None:
+            block_half = whole_ref.at[:, pl.ds(pl.multiple_of(half * 128, 128), 128)]
+            leaving.append(pltpu.make_async_copy(held.at[k], block_half, whole_sem.at[k]))
+            leaving[-1].start()
+    for copy in leaving:
+        copy.wait()
 
 
 def channel_rows(place, order, source):
     lanes = source.shape[-1]
+    count = 3 if source.ndim == 4 else 2
+    in_hbm = pl.BlockSpec(memory_space=pltpu.HBM)
     shapes = [(8, 128, lanes), (8, 128, lanes), (8, BLOCK, lanes)]
     return pl.pallas_call(
         rows_kernel,
-        in_specs=[SMALL, IN_VMEM, IN_VMEM],
-        out_specs=[IN_VMEM] * 3,
-        out_shape=[jax.ShapeDtypeStruct(shape, jnp.bfloat16) for shape in shapes],
+        in_specs=[SMALL, IN_VMEM, pl.BlockSpec(memory_space=pl.ANY)],
+        out_specs=[in_hbm] * 3,
+        out_shape=[pltpu.HBM(shape, jnp.bfloat16) for shape in shapes],
+        scratch_shapes=[
+            pltpu.VMEM((count, 32, 32, lanes), jnp.bfloat16),
+            pltpu.VMEM((count, 8, 128, lanes), jnp.bfloat16),
+            pltpu.SemaphoreType.DMA((count,)),
+            pltpu.SemaphoreType.DMA((count,)),
+            pltpu.SemaphoreType.DMA((count,)),
+        ],
         compiler_params=pltpu.CompilerParams(vmem_limit_bytes=40 * 1024 * 1024),
         name="channel_rows",
     )(place, order, source)
@@ -185,14 +210,14 @@
 
 
 def tile_products(rows, cols):
-    return lax.dot_general(stacked(rows), cols, NT, preferred_element_type=jnp.float32) * (1.0 / SPECTRA)
+    return lax.dot_general(stacked(rows), cols, NT, preferred_element_type=jnp.float32)
 
 
 def self_kernel(own0_ref, own1_ref, self_ref, self_held, sem):
     copies = []
     for c in range(8):
         rows = jnp.concatenate([own0_ref[c], own1_ref[c]], axis=1)
-        product = tile_products(rows, rows)
+        product = tile_products(rows, rows) * (1.0 / SPECTRA)
         self_held[0, c] = product[:BLOCK]
         self_held[1, c] = product[BLOCK:]
         copies.append(pltpu.make_async_copy(self_held.at[:, c], self_ref.at[:, c], sem.at[c]))
@@ -249,7 +274,7 @@
     copies = []
     for c in range(8):
         rows = jnp.concatenate([own0_ref[c], own1_ref[c]], axis=1)
-        product = tile_products(rows, jnp.concatenate([early_ref[c], held[c]], axis=1))
+        product = tile_products(rows, jnp.concatenate([early_ref[c], held[c]], axis=1)) * (1.0 / SPECTRA)
         for p in range(2):
             prior_held[p, c] = product[p * BLOCK : (p + 1) * BLOCK, :BLOCK]
             far_held[p, c] = product[p * BLOCK : (p + 1) * BLOCK, BLOCK:]
@@ -303,19 +328,24 @@
     (early,) = filter_section(place, samples, pfb_taps, table, 0, EARLY, False)
     stay, leave = filter_section(place, samples, pfb_taps, table, EARLY * SB, 1, True)
     source0 = lax.all_to_all(early, ("side", "plane"), split_axis=0, concat_axis=0, tiled=True)
-    late = merge(place, stay, lax.ppermute(leave, "side", [(0, 1), (1, 0)]))
+    got = lax.ppermute(leave, "side", [(0, 1), (1, 0)])
+    far = lax.ppermute(jnp.where(place[2] == 1 - place[0], stay, got), "narrow", CROSSED)
+    late = merge(place, stay, got, far)
     late, source0 = lax.optimization_barrier((late, source0))
     source1 = lax.all_to_all(late, "plane", split_axis=0, concat_axis=0, tiled=True)
     crossing0, rest0, own0 = channel_rows(place, order, source0)
-    f, g, h = exchange(crossing0, rest0, own0)
-    held0 = early_columns(place, f, g, h, swap(f))
-    source1, held0 = lax.optimization_barrier((source1, held0))
-    crossing1, rest1, own1 = channel_rows(place, order, source1)
-    f, g, h = exchange(crossing1, rest1, own1)
-    own1, h = lax.optimization_barrier((own1, h))
+    f0, g0, h0 = exchange(crossing0, rest0, own0)
+    s0 = swap(f0)
+    source1, f0 = lax.optimization_barrier((source1, f0))
+    rest1, f1, own1 = channel_rows(place, order, source1)
+    g1 = lax.ppermute(rest1, "narrow", ODD_OVER)
+    h1 = lax.ppermute(own1, "narrow", EVEN_UP)
+    s1 = swap(f1)
+    own0, own1, h1 = lax.optimization_barrier((own0, own1, h1))
     self_vis = self_tiles(own0, own1)
-    f, self_vis = lax.optimization_barrier((f, self_vis))
-    prior_vis, far_vis = cross_tiles(place, own0, own1, held0, f, g, h, swap(f))
+    held0 = early_columns(place, f0, g0, h0, s0)
+    g1, self_vis, held0 = lax.optimization_barrier((g1, self_vis, held0))
+    prior_vis, far_vis = cross_tiles(place, own0, own1, held0, f1, g1, h1, s1)
     return (self_vis, prior_vis, far_vis)
 
 

time: 147 us -> 145 us (0.986)
  local copies, waits for them, and re-layouts: 8.7 us -> 1.07 us
  starting transfers between devices: 30.1 us -> 36.7 us
  waiting for transfers between devices: 79.8 us -> 75.7 us
  Pallas kernels: 26.7 us -> 30 us
    ppermute x1 -> x4, waiting for transfers between devices: 18.7 us -> 46.4 us  [the longest x1 24.6 us: on_device(): lax.ppermute(jnp.where(place[2] == 1 - place[0], stay, got), 'narrow', CR...]
    all_to_all x1, waiting for transfers between devices: 23.3 us -> 0.01 us  [on_device(): lax.all_to_all(early, ('side', 'plane'), split_axis=0, concat_axis=0, til...]
    ppermute x2 -> x1, waiting for transfers between devices: 15.9 us -> 0.01 us  [exchange(): g = lax.ppermute(rest, 'narrow', ODD_OVER)]
    all_to_all x1, waiting for transfers between devices: 0.01 us -> 8.39 us  [on_device(): lax.all_to_all(late, 'plane', split_axis=0, concat_axis=0, tiled=True)]
    unnamed x20 -> x10, local copies, waits for them, and re-layouts: 8.7 us -> 1.07 us
    ppermute x1 -> x4, starting transfers between devices: 1.67 us -> 5.53 us  [the longest x1 1.93 us: on_device(): h1 = lax.ppermute(own1, 'narrow', EVEN_UP)]
    all_to_all x1, starting transfers between devices: 5.32 us -> 9.04 us  [on_device(): lax.all_to_all(late, 'plane', split_axis=0, concat_axis=0, tiled=True)]
    ppermute x2 -> x1, starting transfers between devices: 7.28 us -> 3.85 us  [exchange(): h = lax.ppermute(whole, 'narrow', EVEN_UP)]
  transfers between devices with their start and end apart: 11 -> 11, of which waited for: 7 -> 5; matrix products, arithmetic and copies ran while one was open for 0% -> 0% of each run, Pallas kernels for 8% -> 13%
where the time goes in v7:
time: 145 us
  waiting for transfers between devices  75.7 us (52%)
  starting transfers between devices  36.7 us (25%)
  Pallas kernels  30 us (21%)
    ppermute x1, waiting for transfers between devices, on_device(): lax.ppermute(jnp.where(place[2] == 1 - place[0], stay, got), 'narrow', CR...  24.6 us
    ppermute x1, waiting for transfers between devices, exchange(): f = lax.ppermute(crossing, 'narrow', CROSSED)  20.9 us
    ppermute x1, waiting for transfers between devices, on_device(): got = lax.ppermute(leave, 'side', [(0, 1), (1, 0)])  18.7 us
    all_to_all x1, starting transfers between devices, on_device(): lax.all_to_all(early, ('side', 'plane'), split_axis=0, concat_axis=0, til...  12.8 us
    pallas_call x2, Pallas kernels, filter_section(): pl.pallas_call(functools.partial(spectra_kernel, first, split), in_specs=...  11.6 us
    all_to_all x1, starting transfers between devices, on_device(): lax.all_to_all(late, 'plane', split_axis=0, concat_axis=0, tiled=True)  9.04 us
    all_to_all x1, waiting for transfers between devices, on_device(): lax.all_to_all(late, 'plane', split_axis=0, concat_axis=0, tiled=True)  8.39 us
    pallas_call x2, Pallas kernels, channel_rows(): pl.pallas_call(rows_kernel, in_specs=[SMALL, IN_VMEM, pl.BlockSpec(memory...  6.56 us
  transfers between devices with their start and end apart: 11, of which 5 were waited for; matrix products, arithmetic and copies ran while one was open for 0% of the time, Pallas kernels for 13%

profile of v7, /device:TPU:24, one launch (start us, length us, event | category | flops | bytes accessed | tf_op | source)
XLA Modules:
  0.0 144.7 jit_solution(5880479270678475178)
XLA Ops:
  0.7 6.6 %filter_section.3 = bf16[64,32,512]{2,1,0:T(8,128)(2,1)} custom-call(s32[3]{0:T(128)S(1)} %pad_add_fusion.place_ref, bf16[4,396288]{1,0:T(4,128)(2,1)} %x_ref.3, bf16[1024,1024]{1,0:T(8,128)(2,1)} %constant.39.clone.table_ref, f32[4,1024]{1,0:T(4,128)} %taps_ref.3), custom_call_target="tpu_custom_call" | custom-call | tf_op jit(solution)/shard_map/filter_section/pallas_call | solution.py:107
  7.4 12.8 %all-to-all-start = ((bf16[64,32,512]{2,1,0:T(8,128)(2,1)}), bf16[64,32,512]{2,1,0:T(8,128)(2,1)S(1)}, u32[]{:S(2)}, u32[]{:S(2)}) async-start(bf16[64,32,512]{2,1,0:T(8,128)(2,1)} %filter_section.3), calls=%async_computation | async-start | bytes 4194304 | tf_op jit(solution)/shard_map/all_to_all | solution.py:330
  20.2 5.0 %filter_section.2 = (bf16[32,32,256]{2,1,0:T(8,128)(2,1)}, bf16[32,32,256]{2,1,0:T(8,128)(2,1)}) custom-call(s32[3]{0:T(128)S(1)} %pad_add_fusion.place_ref, bf16[4,396288]{1,0:T(4,128)(2,1)} %x_ref.3, bf16[1024,1024]{1,0:T(8,128)(2,1)} %constant.39.clone.table_ref, f32[4,1024]{1,0:T(4,128)} %taps_ref.3), custom_call_target="tpu_custom_call" | custom-call | tf_op jit(solution)/shard_map/filter_section/pallas_call | solution.py:107
  25.2 1.7 %collective-permute-start = (bf16[32,32,256]{2,1,0:T(8,128)(2,1)}, bf16[32,32,256]{2,1,0:T(8,128)(2,1)S(1)}, u32[]{:S(2)}, u32[]{:S(2)}) collective-permute-start(bf16[32,32,256]{2,1,0:T(8,128)(2,1)} %get-tuple-element.24), channel_id=1, source_target_pairs={{0,128},{128,0},{1,129},{129,1},{2,130},{130,2},{3,131},{131,3},{4... | collective-permute-start | bytes 1572872 | tf_op jit(solution)/shard_map/ppermute | solution.py:331
  26.8 18.7 %collective-permute-done.got_ref = bf16[32,32,256]{2,1,0:T(8,128)(2,1)S(1)} collective-permute-done((bf16[32,32,256]{2,1,0:T(8,128)(2,1)}, bf16[32,32,256]{2,1,0:T(8,128)(2,1)S(1)}, u32[]{:S(2)}, u32[]{:S(2)}) %collective-permute-start) | collective-permute-done | bytes 524320 | tf_op jit(solution)/shard_map/ppermute | solution.py:331
  45.7 0.6 collective-permute-start.1
  46.3 24.6 %collective-permute-done.1.far_ref = bf16[32,32,256]{2,1,0:T(8,128)(2,1)S(1)} collective-permute-done((bf16[32,32,256]{2,1,0:T(8,128)(2,1)S(1)}, bf16[32,32,256]{2,1,0:T(8,128)(2,1)S(1)}, u32[]{:S(2)}, u32[]{:S(2)}) %collective-permute-start.1) | collective-permute-done | bytes 524320 | tf_op jit(solution)/shard_map/ppermute | solution.py:332
  70.9 1.0 copy-done.2
  72.0 1.8 %merge_sides.1 = bf16[32,3,32,256]{3,2,1,0:T(8,128)(2,1)} custom-call(s32[3]{0:T(128)S(1)} %pad_add_fusion.place_ref, bf16[32,32,256]{2,1,0:T(8,128)(2,1)S(1)} %copy-done.2, bf16[32,32,256]{2,1,0:T(8,128)(2,1)S(1)} %collective-permute-done.got_ref, bf16[32,32,256]{2,1,0:T(8,128)(2,1)S(1)} %collective-permute-done.1.far_ref), custom_call_target="tpu_custom_call" | custom-call | tf_op jit(solution)/shard_map/merge_sides/pallas_call | solution.py:141
  73.8 9.0 %all-to-all-start.1 = ((bf16[32,3,32,256]{3,2,1,0:T(8,128)(2,1)}), bf16[32,3,32,256]{3,2,1,0:T(8,128)(2,1)}, u32[]{:S(2)}, u32[]{:S(2)}) async-start(bf16[32,3,32,256]{3,2,1,0:T(8,128)(2,1)} %merge_sides.1), calls=%async_computation.1 | async-start | bytes 3145728 | tf_op jit(solution)/shard_map/all_to_all | solution.py:335
  82.8 3.2 %channel_rows.2 = (bf16[8,128,512]{2,1,0:T(8,128)(2,1)}, bf16[8,128,512]{2,1,0:T(8,128)(2,1)}, bf16[8,256,512]{2,1,0:T(8,128)(2,1)}) custom-call(s32[3]{0:T(128)S(1)} %pad_add_fusion.place_ref, bf16[256,256]{1,0:T(8,128)(2,1)S(1)} %copy-done.4, bf16[64,32,512]{2,1,0:T(8,128)(2,1)S(1)} %all-to-all-done.source_ref), custom_call_target="tpu_custom_call" | custom-call | tf_op jit(solution)/shard_map/channel_rows/pallas_call | solution.py:188
  86.0 1.2 collective-permute-start.2
  87.2 3.8 %collective-permute-start.6 = (bf16[8,256,512]{2,1,0:T(8,128)(2,1)}, bf16[8,256,512]{2,1,0:T(8,128)(2,1)S(1)}, u32[]{:S(2)}, u32[]{:S(2)}) collective-permute-start(bf16[8,256,512]{2,1,0:T(8,128)(2,1)} %get-tuple-element.32.own0_ref), channel_id=1, source_target_pairs={{0,1},{2,3},{4,5},{6,7},{8,9},{10,11},{12,13},{14,15},{16,17},{18,... | collective-permute-start | bytes 6291464 | tf_op jit(solution)/shard_map/ppermute | solution.py:322
  91.0 1.3 collective-permute-start.5
  92.3 20.9 %collective-permute-done.2.f_ref = bf16[8,128,512]{2,1,0:T(8,128)(2,1)S(1)} collective-permute-done((bf16[8,128,512]{2,1,0:T(8,128)(2,1)}, bf16[8,128,512]{2,1,0:T(8,128)(2,1)S(1)}, u32[]{:S(2)}, u32[]{:S(2)}) %collective-permute-start.2) | collective-permute-done | bytes 1048608 | tf_op jit(solution)/shard_map/ppermute | solution.py:320
  113.6 8.4 %all-to-all-done.1.source_ref = bf16[32,3,32,256]{3,2,1,0:T(8,128)(2,1)} async-done(((bf16[32,3,32,256]{3,2,1,0:T(8,128)(2,1)}), bf16[32,3,32,256]{3,2,1,0:T(8,128)(2,1)}, u32[]{:S(2)}, u32[]{:S(2)}) %all-to-all-start.1) | async-done | bytes 1572896 | tf_op jit(solution)/shard_map/all_to_all | solution.py:335
  122.0 3.4 %channel_rows.3 = (bf16[8,128,256]{2,1,0:T(8,128)(2,1)}, bf16[8,128,256]{2,1,0:T(8,128)(2,1)}, bf16[8,256,256]{2,1,0:T(8,128)(2,1)}) custom-call(s32[3]{0:T(128)S(1)} %pad_add_fusion.place_ref, bf16[256,256]{1,0:T(8,128)(2,1)S(1)} %copy-done.4, bf16[32,3,32,256]{3,2,1,0:T(8,128)(2,1)} %all-to-all-done.1.source_ref), custom_call_target="tpu_custom_call" | custom-call | tf_op jit(solution)/shard_map/channel_rows/pallas_call | solution.py:188
  125.3 1.9 %collective-permute-start.4 = (bf16[8,256,256]{2,1,0:T(8,128)(2,1)}, bf16[8,256,256]{2,1,0:T(8,128)(2,1)S(1)}, u32[]{:S(2)}, u32[]{:S(2)}) collective-permute-start(bf16[8,256,256]{2,1,0:T(8,128)(2,1)} %get-tuple-element.33.own1_ref), channel_id=1, source_target_pairs={{0,1},{2,3},{4,5},{6,7},{8,9},{10,11},{12,13},{14,15},{16,17},{18,... | collective-permute-start | bytes 3145736 | tf_op jit(solution)/shard_map/ppermute | solution.py:342
  127.3 1.3 collective-permute-start.3
  128.6 2.7 %collective-permute-start.8 = (bf16[8,128,256]{2,1,0:T(8,128)(2,1)}, bf16[8,128,256]{2,1,0:T(8,128)(2,1)S(1)}, u32[]{:S(2)}, u32[]{:S(2)}) collective-permute-start(bf16[8,128,256]{2,1,0:T(8,128)(2,1)} %get-tuple-element.38.f_ref), channel_id=1, source_target_pairs={{0,1},{1,0},{2,3},{3,2},{4,5},{5,4},{6,7},{7,6},{8,9},{9,8},{10,11... | collective-permute-start | bytes 1572872 | tf_op jit(solution)/shard_map/ppermute | solution.py:326
  131.3 1.9 %early_columns.1.early_ref = bf16[8,384,512]{2,1,0:T(8,128)(2,1)S(1)} custom-call(s32[3]{0:T(128)S(1)} %pad_add_fusion.place_ref, bf16[8,128,512]{2,1,0:T(8,128)(2,1)S(1)} %collective-permute-done.2.f_ref, bf16[8,128,512]{2,1,0:T(8,128)(2,1)} %collective-permute-done.5.g_ref, bf16[8,256,512]{2,1,0:T(8,128)(2,1)S(1)} %collective-permute-done.6.h_ref, ...), custom_call_target="tpu_custom_call" | custom-call | tf_op jit(solution)/shard_map/early_columns/pallas_call | solution.py:261
  133.3 3.1 %self_tiles.1 = f32[2,8,256,256]{3,2,1,0:T(8,128)} custom-call(bf16[8,256,512]{2,1,0:T(8,128)(2,1)S(1)} %copy-done, bf16[8,256,256]{2,1,0:T(8,128)(2,1)S(1)} %copy-done.1), custom_call_target="tpu_custom_call" | custom-call | tf_op jit(solution)/shard_map/self_tiles/pallas_call | solution.py:230
  136.4 3.1 %collective-permute-done.3.g_ref = bf16[8,128,256]{2,1,0:T(8,128)(2,1)S(1)} collective-permute-done((bf16[8,128,256]{2,1,0:T(8,128)(2,1)}, bf16[8,128,256]{2,1,0:T(8,128)(2,1)S(1)}, u32[]{:S(2)}, u32[]{:S(2)}) %collective-permute-start.3) | collective-permute-done | bytes 524320 | tf_op jit(solution)/shard_map/ppermute | solution.py:341
  139.5 5.0 %cross_tiles.1 = (f32[2,8,256,256]{3,2,1,0:T(8,128)}, f32[2,8,256,128]{3,2,1,0:T(8,128)}) custom-call(s32[3]{0:T(128)S(1)} %pad_add_fusion.place_ref, bf16[8,256,512]{2,1,0:T(8,128)(2,1)S(1)} %copy-done, bf16[8,256,256]{2,1,0:T(8,128)(2,1)S(1)} %copy-done.1, bf16[8,384,512]{2,1,0:T(8,128)(2,1)S(1)} %early_columns.1.early_ref, ...), custom_call_target="tpu_custom_call" | custom-call | tf_op jit(solution)/shard_map/cross_tiles/pallas_call | solution.py:292
  (18 shorter events, 0.5 us)
Async XLA Ops:
  7.4 66.4 %all-to-all-start = ((bf16[64,32,512]{2,1,0:T(8,128)(2,1)}), bf16[64,32,512]{2,1,0:T(8,128)(2,1)S(1)}, u32[]{:S(2)}, u32[]{:S(2)}) async-start(bf16[64,32,512]{2,1,0:T(8,128)(2,1)} %filter_section.3), calls=%async_computation | async-start | bytes 4194304 | tf_op jit(solution)/shard_map/all_to_all | solution.py:330
  25.2 20.4 %collective-permute-start = (bf16[32,32,256]{2,1,0:T(8,128)(2,1)}, bf16[32,32,256]{2,1,0:T(8,128)(2,1)S(1)}, u32[]{:S(2)}, u32[]{:S(2)}) collective-permute-start(bf16[32,32,256]{2,1,0:T(8,128)(2,1)} %get-tuple-element.24), channel_id=1, source_target_pairs={{0,128},{128,0},{1,129},{129,1},{2,130},{130,2},{3,131},{131,3},{4... | collective-permute-start | bytes 1572872 | tf_op jit(solution)/shard_map/ppermute | solution.py:331
  45.7 25.2 %collective-permute-start.1 = (bf16[32,32,256]{2,1,0:T(8,128)(2,1)S(1)}, bf16[32,32,256]{2,1,0:T(8,128)(2,1)S(1)}, u32[]{:S(2)}, u32[]{:S(2)}) collective-permute-start(bf16[32,32,256]{2,1,0:T(8,128)(2,1)S(1)} %broadcast_select_fusion), channel_id=1, source_target_pairs={{0,3},{1,2},{2,1},{3,0},{4,7},{5,6},{6,5},{7,4},{8,11},{9,10},{10,... | collective-permute-start | bytes 1572872 | tf_op jit(solution)/shard_map/ppermute | solution.py:332
  70.9 1.0 copy-start.2
  73.8 9.1 %copy-start.4 = (bf16[256,256]{1,0:T(8,128)(2,1)S(1)}, bf16[256,256]{1,0:T(8,128)(2,1)}, u32[]{:S(2)}) copy-start(bf16[256,256]{1,0:T(8,128)(2,1)} %constant.40.clone.order_ref) | copy-start | bytes 393220
  73.8 48.2 %all-to-all-start.1 = ((bf16[32,3,32,256]{3,2,1,0:T(8,128)(2,1)}), bf16[32,3,32,256]{3,2,1,0:T(8,128)(2,1)}, u32[]{:S(2)}, u32[]{:S(2)}) async-start(bf16[32,3,32,256]{3,2,1,0:T(8,128)(2,1)} %merge_sides.1), calls=%async_computation.1 | async-start | bytes 3145728 | tf_op jit(solution)/shard_map/all_to_all | solution.py:335
  86.0 27.2 %collective-permute-start.2 = (bf16[8,128,512]{2,1,0:T(8,128)(2,1)}, bf16[8,128,512]{2,1,0:T(8,128)(2,1)S(1)}, u32[]{:S(2)}, u32[]{:S(2)}) collective-permute-start(bf16[8,128,512]{2,1,0:T(8,128)(2,1)} %get-tuple-element.27), channel_id=1, source_target_pairs={{0,3},{1,2},{2,1},{3,0},{4,7},{5,6},{6,5},{7,4},{8,11},{9,10},{10,... | collective-permute-start | bytes 3145736 | tf_op jit(solution)/shard_map/ppermute | solution.py:320
  87.2 44.1 %collective-permute-start.6 = (bf16[8,256,512]{2,1,0:T(8,128)(2,1)}, bf16[8,256,512]{2,1,0:T(8,128)(2,1)S(1)}, u32[]{:S(2)}, u32[]{:S(2)}) collective-permute-start(bf16[8,256,512]{2,1,0:T(8,128)(2,1)} %get-tuple-element.32.own0_ref), channel_id=1, source_target_pairs={{0,1},{2,3},{4,5},{6,7},{8,9},{10,11},{12,13},{14,15},{16,17},{18,... | collective-permute-start | bytes 6291464 | tf_op jit(solution)/shard_map/ppermute | solution.py:322
  91.0 37.5 %collective-permute-start.5 = (bf16[8,128,512]{2,1,0:T(8,128)(2,1)}, bf16[8,128,512]{2,1,0:T(8,128)(2,1)}, u32[]{:S(2)}, u32[]{:S(2)}) collective-permute-start(bf16[8,128,512]{2,1,0:T(8,128)(2,1)} %get-tuple-element.35), channel_id=1, source_target_pairs={{1,2},{3,0},{5,6},{7,4},{9,10},{11,8},{13,14},{15,12},{17,18},{19,... | collective-permute-start | bytes 3145736 | tf_op jit(solution)/shard_map/ppermute | solution.py:321
  113.2 18.1 %collective-permute-start.7 = (bf16[8,128,512]{2,1,0:T(8,128)(2,1)S(1)}, bf16[8,128,512]{2,1,0:T(8,128)(2,1)}, u32[]{:S(2)}, u32[]{:S(2)}) collective-permute-start(bf16[8,128,512]{2,1,0:T(8,128)(2,1)S(1)} %collective-permute-done.2.f_ref), channel_id=1, source_target_pairs={{0,1},{1,0},{2,3},{3,2},{4,5},{5,4},{6,7},{7,6},{8,9},{9,8},{10,11... | collective-permute-start | bytes 3145736 | tf_op jit(solution)/shard_map/ppermute | solution.py:326
  125.3 8.0 %collective-permute-start.4 = (bf16[8,256,256]{2,1,0:T(8,128)(2,1)}, bf16[8,256,256]{2,1,0:T(8,128)(2,1)S(1)}, u32[]{:S(2)}, u32[]{:S(2)}) collective-permute-start(bf16[8,256,256]{2,1,0:T(8,128)(2,1)} %get-tuple-element.33.own1_ref), channel_id=1, source_target_pairs={{0,1},{2,3},{4,5},{6,7},{8,9},{10,11},{12,13},{14,15},{16,17},{18,... | collective-permute-start | bytes 3145736 | tf_op jit(solution)/shard_map/ppermute | solution.py:342
  127.3 12.2 %collective-permute-start.3 = (bf16[8,128,256]{2,1,0:T(8,128)(2,1)}, bf16[8,128,256]{2,1,0:T(8,128)(2,1)S(1)}, u32[]{:S(2)}, u32[]{:S(2)}) collective-permute-start(bf16[8,128,256]{2,1,0:T(8,128)(2,1)} %get-tuple-element.29), channel_id=1, source_target_pairs={{1,2},{3,0},{5,6},{7,4},{9,10},{11,8},{13,14},{15,12},{17,18},{19,... | collective-permute-start | bytes 1572872 | tf_op jit(solution)/shard_map/ppermute | solution.py:341
  128.6 4.7 %copy-start = (bf16[8,256,512]{2,1,0:T(8,128)(2,1)S(1)}, bf16[8,256,512]{2,1,0:T(8,128)(2,1)}, u32[]{:S(2)}) copy-start(bf16[8,256,512]{2,1,0:T(8,128)(2,1)} %get-tuple-element.32.own0_ref) | copy-start | bytes 6291460
  128.6 4.7 %copy-start.1 = (bf16[8,256,256]{2,1,0:T(8,128)(2,1)S(1)}, bf16[8,256,256]{2,1,0:T(8,128)(2,1)}, u32[]{:S(2)}) copy-start(bf16[8,256,256]{2,1,0:T(8,128)(2,1)} %get-tuple-element.33.own1_ref) | copy-start | bytes 3145732
  128.6 10.9 %collective-permute-start.8 = (bf16[8,128,256]{2,1,0:T(8,128)(2,1)}, bf16[8,128,256]{2,1,0:T(8,128)(2,1)S(1)}, u32[]{:S(2)}, u32[]{:S(2)}) collective-permute-start(bf16[8,128,256]{2,1,0:T(8,128)(2,1)} %get-tuple-element.38.f_ref), channel_id=1, source_target_pairs={{0,1},{1,0},{2,3},{3,2},{4,5},{5,4},{6,7},{7,6},{8,9},{9,8},{10,11... | collective-permute-start | bytes 1572872 | tf_op jit(solution)/shard_map/ppermute | solution.py:326
  133.3 6.2 %copy-start.3 = (bf16[8,128,256]{2,1,0:T(8,128)(2,1)S(1)}, bf16[8,128,256]{2,1,0:T(8,128)(2,1)}, u32[]{:S(2)}) copy-start(bf16[8,128,256]{2,1,0:T(8,128)(2,1)} %get-tuple-element.38.f_ref) | copy-start | bytes 1572868

commit v8 on v7

--- a/solution.py
+++ b/solution.py
@@ -121,85 +121,117 @@
             pltpu.SemaphoreType.DMA,
             pltpu.SemaphoreType.DMA((2 * blocks,)),
         ],
-        compiler_params=pltpu.CompilerParams(vmem_limit_bytes=40 * 1024 * 1024),
+        compiler_params=pltpu.CompilerParams(vmem_limit_bytes=20 * 1024 * 1024),
         name="filter_section",
     )(place, *(pltpu.with_memory_space_constraint(a, pltpu.HBM) for a in (samples, table, pfb_taps)))
 
 
-def merge_kernel(place_ref, stay_ref, got_ref, far_ref, out_ref, held, sem):
+def merge_kernel(place_ref, stay_ref, got_ref, over_ref, across_ref, out_ref, held, sem):
     side = place_ref[2]
     held[:, side] = stay_ref[...]
     held[:, 1 - side] = got_ref[...]
-    held[:, 2] = far_ref[...]
+
+    @pl.when(side == place_ref[0])
+    def _():
+        held[:, 2] = over_ref[...]
+
+    @pl.when(side != place_ref[0])
+    def _():
+        held[:, 2] = across_ref[...]
+
     copy = pltpu.make_async_copy(held, out_ref, sem)
     copy.start()
     copy.wait()
 
 
-def merge(place, stay, got, far):
+def merge(place, stay, got, over, across):
     shape = (32, 3) + stay.shape[1:]
     return pl.pallas_call(
         merge_kernel,
-        in_specs=[SMALL] + [IN_VMEM] * 3,
+        in_specs=[SMALL] + [IN_VMEM] * 4,
         out_specs=pl.BlockSpec(memory_space=pltpu.HBM),
         out_shape=pltpu.HBM(shape, jnp.bfloat16),
         scratch_shapes=[pltpu.VMEM(shape, jnp.bfloat16), pltpu.SemaphoreType.DMA],
-        compiler_params=pltpu.CompilerParams(vmem_limit_bytes=40 * 1024 * 1024),
+        compiler_params=pltpu.CompilerParams(vmem_limit_bytes=8 * 1024 * 1024),
         name="merge_sides",
-    )(place, stay, got, far)
-
-
-def rows_kernel(place_ref, order_ref, source_ref, first_ref, second_ref, whole_ref, source, held, in_sem, out_sem, whole_sem):
+    )(place, stay, got, over, across)
+
+
+def order_rows(order_ref, source, held):
+    for g in range(4):
+        rows = source[g * 8 : (g + 1) * 8].reshape(256, source.shape[-1])
+        turned = jnp.dot(order_ref[...], rows, preferred_element_type=jnp.float32).astype(jnp.bfloat16)
+        for c in range(8):
+            held[c, g * 32 : (g + 1) * 32, :] = turned[c * 32 : (c + 1) * 32]
+
+
+def early_rows_kernel(place_ref, order_ref, source_ref, cross_ref, rest_ref, whole_ref, source, held, in_sem, out_sem, whole_sem):
     chip = place_ref[0]
-    late = len(source_ref.shape) == 4
-    if late:
-        parts = [source_ref.at[:, chip], source_ref.at[:, 2], source_ref.at[:, 1 - chip]]
-        steps = [(first_ref, chip), (second_ref, None), (None, 1 - chip)]
-    else:
-        parts = [source_ref.at[pl.ds(half * 32, 32)] for half in (1 - chip, chip)]
-        steps = [(first_ref, 1 - chip), (second_ref, chip)]
-    arriving = [pltpu.make_async_copy(part, source.at[k], in_sem.at[k]) for k, part in enumerate(parts)]
+    halves = (1 - chip, chip)
+    arriving = [
+        pltpu.make_async_copy(source_ref.at[pl.ds(half * 32, 32)], source.at[k], in_sem.at[k]) for k, half in enumerate(halves)
+    ]
     for copy in arriving:
         copy.start()
     leaving = []
-    for k, (out_ref, half) in enumerate(steps):
+    for k, (half, out_ref) in enumerate(zip(halves, (cross_ref, rest_ref))):
         arriving[k].wait()
-        for g in range(4):
-            rows = source[k, g * 8 : (g + 1) * 8].reshape(256, source.shape[-1])
-            turned = jnp.dot(order_ref[...], rows, preferred_element_type=jnp.float32).astype(jnp.bfloat16)
-            for c in range(8):
-                held[k, c, g * 32 : (g + 1) * 32, :] = turned[c * 32 : (c + 1) * 32]
-        if out_ref is not None:
-            leaving.append(pltpu.make_async_copy(held.at[k], out_ref, out_sem.at[k]))
-            leaving[-1].start()
-        if half is not None:
-            block_half = whole_ref.at[:, pl.ds(pl.multiple_of(half * 128, 128), 128)]
-            leaving.append(pltpu.make_async_copy(held.at[k], block_half, whole_sem.at[k]))
-            leaving[-1].start()
+        order_rows(order_ref, source.at[k], held.at[k])
+        block_half = whole_ref.at[:, pl.ds(pl.multiple_of(half * 128, 128), 128)]
+        leaving.append(pltpu.make_async_copy(held.at[k], out_ref, out_sem.at[k]))
+        leaving.append(pltpu.make_async_copy(held.at[k], block_half, whole_sem.at[k]))
+        leaving[-2].start()
+        leaving[-1].start()
     for copy in leaving:
         copy.wait()
 
 
-def channel_rows(place, order, source):
+def rows_call(kernel, count, place, order, source, shapes, name):
     lanes = source.shape[-1]
-    count = 3 if source.ndim == 4 else 2
     in_hbm = pl.BlockSpec(memory_space=pltpu.HBM)
-    shapes = [(8, 128, lanes), (8, 128, lanes), (8, BLOCK, lanes)]
-    return pl.pallas_call(
-        rows_kernel,
+    return pl.pallas_call(
+        kernel,
         in_specs=[SMALL, IN_VMEM, pl.BlockSpec(memory_space=pl.ANY)],
-        out_specs=[in_hbm] * 3,
+        out_specs=[in_hbm] * len(shapes),
         out_shape=[pltpu.HBM(shape, jnp.bfloat16) for shape in shapes],
         scratch_shapes=[
             pltpu.VMEM((count, 32, 32, lanes), jnp.bfloat16),
             pltpu.VMEM((count, 8, 128, lanes), jnp.bfloat16),
             pltpu.SemaphoreType.DMA((count,)),
             pltpu.SemaphoreType.DMA((count,)),
-            pltpu.SemaphoreType.DMA((count,)),
-        ],
-        compiler_params=pltpu.CompilerParams(vmem_limit_bytes=40 * 1024 * 1024),
-        name="channel_rows",
+        ] + ([pltpu.SemaphoreType.DMA((count,))] if len(shapes) > count else []),
+        compiler_params=pltpu.CompilerParams(vmem_limit_bytes=12 * 1024 * 1024),
+        name=name,
     )(place, order, source)
+
+
+def early_rows(place, order, source):
+    lanes = source.shape[-1]
+    shapes = [(8, 128, lanes), (8, 128, lanes), (8, BLOCK, lanes)]
+    return rows_call(early_rows_kernel, 2, place, order, source, shapes, "early_rows")
+
+
+def late_rows_kernel(rest, place_ref, order_ref, source_ref, *refs):
+    outs, (source, held, in_sem, out_sem) = refs[:-4], refs[-4:]
+    chip = place_ref[0]
+    slots = (chip,) if rest else (1 - chip, 2)
+    arriving = [pltpu.make_async_copy(source_ref.at[:, slot], source.at[k], in_sem.at[k]) for k, slot in enumerate(slots)]
+    for copy in arriving:
+        copy.start()
+    leaving = []
+    for k, out_ref in enumerate(outs):
+        arriving[k].wait()
+        order_rows(order_ref, source.at[k], held.at[k])
+        leaving.append(pltpu.make_async_copy(held.at[k], out_ref, out_sem.at[k]))
+        leaving[-1].start()
+    for copy in leaving:
+        copy.wait()
+
+
+def late_rows(place, order, source, rest):
+    count = 1 if rest else 2
+    shapes = [(8, 128, source.shape[-1])] * count
+    return rows_call(functools.partial(late_rows_kernel, rest), count, place, order, source, shapes, "late_rows")
 
 
 def stacked(rows):
@@ -213,10 +245,17 @@
     return lax.dot_general(stacked(rows), cols, NT, preferred_element_type=jnp.float32)
 
 
-def self_kernel(own0_ref, own1_ref, self_ref, self_held, sem):
+def put_halves(place_ref, chips_ref, others_ref, out_ref):
+    chip = place_ref[0]
+    out_ref[:, pl.ds(pl.multiple_of(chip * 128, 128), 128), :] = chips_ref[...]
+    out_ref[:, pl.ds(pl.multiple_of((1 - chip) * 128, 128), 128), :] = others_ref[...]
+
+
+def self_kernel(place_ref, own0_ref, crossing1_ref, rest1_ref, self_ref, own1, self_held, sem):
+    put_halves(place_ref, rest1_ref, crossing1_ref, own1)
     copies = []
     for c in range(8):
-        rows = jnp.concatenate([own0_ref[c], own1_ref[c]], axis=1)
+        rows = jnp.concatenate([own0_ref[c], own1[c]], axis=1)
         product = tile_products(rows, rows) * (1.0 / SPECTRA)
         self_held[0, c] = product[:BLOCK]
         self_held[1, c] = product[BLOCK:]
@@ -226,35 +265,32 @@
         copy.wait()
 
 
-def self_tiles(own0, own1):
+def self_tiles(place, *own):
     return pl.pallas_call(
         self_kernel,
-        in_specs=[IN_VMEM] * 2,
+        in_specs=[SMALL] + [IN_VMEM] * 3,
         out_specs=pl.BlockSpec(memory_space=pltpu.HBM),
         out_shape=pltpu.HBM((2, 8, BLOCK, BLOCK), jnp.float32),
-        scratch_shapes=[pltpu.VMEM((2, 8, BLOCK, BLOCK), jnp.float32), pltpu.SemaphoreType.DMA((8,))],
-        compiler_params=pltpu.CompilerParams(vmem_limit_bytes=40 * 1024 * 1024),
+        scratch_shapes=[
+            pltpu.VMEM((8, BLOCK, own[1].shape[-1]), jnp.bfloat16),
+            pltpu.VMEM((2, 8, BLOCK, BLOCK), jnp.float32),
+            pltpu.SemaphoreType.DMA((8,)),
+        ],
+        compiler_params=pltpu.CompilerParams(vmem_limit_bytes=14 * 1024 * 1024),
         name="self_tiles",
-    )(own0, own1)
-
-
-def put_columns(place_ref, f_ref, g_ref, h_ref, s_ref, out_ref):
-    chip = place_ref[0]
-
+    )(place, *own)
+
+
+def early_kernel(place_ref, f_ref, g_ref, h_ref, s_ref, out_ref):
     @pl.when(place_ref[1] == 0)
     def _():
-        out_ref[:, pl.ds(pl.multiple_of(chip * 128, 128), 128), :] = f_ref[...]
-        out_ref[:, pl.ds(pl.multiple_of((1 - chip) * 128, 128), 128), :] = g_ref[...]
+        put_halves(place_ref, f_ref, g_ref, out_ref)
 
     @pl.when(place_ref[1] == 1)
     def _():
         out_ref[:, :BLOCK, :] = h_ref[...]
 
     out_ref[:, BLOCK:, :] = s_ref[...]
-
-
-def early_kernel(place_ref, f_ref, g_ref, h_ref, s_ref, out_ref):
-    put_columns(place_ref, f_ref, g_ref, h_ref, s_ref, out_ref)
 
 
 def early_columns(place, *received):
@@ -263,17 +299,27 @@
         in_specs=[SMALL] + [IN_VMEM] * 4,
         out_specs=IN_VMEM,
         out_shape=jax.ShapeDtypeStruct((8, BLOCK + BLOCK // 2, received[0].shape[-1]), jnp.bfloat16),
-        compiler_params=pltpu.CompilerParams(vmem_limit_bytes=40 * 1024 * 1024),
+        compiler_params=pltpu.CompilerParams(vmem_limit_bytes=8 * 1024 * 1024),
         name="early_columns",
     )(place, *received)
 
 
-def cross_kernel(place_ref, own0_ref, own1_ref, early_ref, f_ref, g_ref, h_ref, s_ref, prior_ref, far_ref,
-                 held, prior_held, far_held, prior_sem, far_sem):
-    put_columns(place_ref, f_ref, g_ref, h_ref, s_ref, held)
+def cross_kernel(place_ref, own0_ref, early_ref, crossing_ref, rest_ref, f_ref, r_ref, h_ref, s_ref, prior_ref, far_ref,
+                 own1, held, prior_held, far_held, prior_sem, far_sem):
+    put_halves(place_ref, rest_ref, crossing_ref, own1)
+
+    @pl.when(place_ref[1] == 0)
+    def _():
+        put_halves(place_ref, f_ref, r_ref, held)
+
+    @pl.when(place_ref[1] == 1)
+    def _():
+        put_halves(place_ref, r_ref, h_ref, held)
+
+    held[:, BLOCK:, :] = s_ref[...]
     copies = []
     for c in range(8):
-        rows = jnp.concatenate([own0_ref[c], own1_ref[c]], axis=1)
+        rows = jnp.concatenate([own0_ref[c], own1[c]], axis=1)
         product = tile_products(rows, jnp.concatenate([early_ref[c], held[c]], axis=1)) * (1.0 / SPECTRA)
         for p in range(2):
             prior_held[p, c] = product[p * BLOCK : (p + 1) * BLOCK, :BLOCK]
@@ -286,29 +332,34 @@
         copy.wait()
 
 
-def cross_tiles(place, own0, own1, early, *late):
+def cross_tiles(place, own0, early, *late):
     in_hbm = pl.BlockSpec(memory_space=pltpu.HBM)
     prior_shape, far_shape = (2, 8, BLOCK, BLOCK), (2, 8, BLOCK, BLOCK // 2)
+    lanes = late[0].shape[-1]
     return pl.pallas_call(
         cross_kernel,
-        in_specs=[SMALL] + [IN_VMEM] * (3 + len(late)),
+        in_specs=[SMALL] + [IN_VMEM] * (2 + len(late)),
         out_specs=[in_hbm, in_hbm],
         out_shape=[pltpu.HBM(prior_shape, jnp.float32), pltpu.HBM(far_shape, jnp.float32)],
         scratch_shapes=[
-            pltpu.VMEM((8, BLOCK + BLOCK // 2, late[0].shape[-1]), jnp.bfloat16),
+            pltpu.VMEM((8, BLOCK, lanes), jnp.bfloat16),
+            pltpu.VMEM((8, BLOCK + BLOCK // 2, lanes), jnp.bfloat16),
             pltpu.VMEM(prior_shape, jnp.float32),
             pltpu.VMEM(far_shape, jnp.float32),
             pltpu.SemaphoreType.DMA((8,)),
             pltpu.SemaphoreType.DMA((8,)),
         ],
-        compiler_params=pltpu.CompilerParams(vmem_limit_bytes=40 * 1024 * 1024),
+        compiler_params=pltpu.CompilerParams(vmem_limit_bytes=20 * 1024 * 1024),
         name="cross_tiles",
-    )(place, own0, own1, early, *late)
+    )(place, own0, early, *late)
 
 
 CROSSED = [(0, 3), (1, 2), (2, 1), (3, 0)]
 ODD_OVER = [(1, 2), (3, 0)]
 EVEN_UP = [(0, 1), (2, 3)]
+NEXT = [(0, 1), (1, 2), (2, 3), (3, 0)]
+OVER = [(4, 7), (5, 6), (2, 1), (3, 0)]
+ACROSS = [(4, 3), (5, 2), (2, 5), (3, 4)]
 SWAPPED = [(0, 1), (1, 0), (2, 3), (3, 2)]
 
 
@@ -328,24 +379,27 @@
     (early,) = filter_section(place, samples, pfb_taps, table, 0, EARLY, False)
     stay, leave = filter_section(place, samples, pfb_taps, table, EARLY * SB, 1, True)
     source0 = lax.all_to_all(early, ("side", "plane"), split_axis=0, concat_axis=0, tiled=True)
+    across = lax.ppermute(leave, ("side", "narrow"), ACROSS)
+    over = lax.ppermute(stay, ("side", "narrow"), OVER)
     got = lax.ppermute(leave, "side", [(0, 1), (1, 0)])
-    far = lax.ppermute(jnp.where(place[2] == 1 - place[0], stay, got), "narrow", CROSSED)
-    late = merge(place, stay, got, far)
+    late = merge(place, stay, got, over, across)
     late, source0 = lax.optimization_barrier((late, source0))
     source1 = lax.all_to_all(late, "plane", split_axis=0, concat_axis=0, tiled=True)
-    crossing0, rest0, own0 = channel_rows(place, order, source0)
+    crossing0, rest0, own0 = early_rows(place, order, pltpu.with_memory_space_constraint(source0, pltpu.HBM))
     f0, g0, h0 = exchange(crossing0, rest0, own0)
     s0 = swap(f0)
     source1, f0 = lax.optimization_barrier((source1, f0))
-    rest1, f1, own1 = channel_rows(place, order, source1)
-    g1 = lax.ppermute(rest1, "narrow", ODD_OVER)
-    h1 = lax.ppermute(own1, "narrow", EVEN_UP)
+    (rest1,) = late_rows(place, order, source1, True)
+    r1 = lax.ppermute(rest1, "narrow", NEXT)
+    source1, rest1 = lax.optimization_barrier((source1, rest1))
+    crossing1, f1 = late_rows(place, order, source1, False)
+    h1 = lax.ppermute(crossing1, "narrow", EVEN_UP)
     s1 = swap(f1)
-    own0, own1, h1 = lax.optimization_barrier((own0, own1, h1))
-    self_vis = self_tiles(own0, own1)
+    own0, crossing1, h1 = lax.optimization_barrier((own0, crossing1, h1))
+    self_vis = self_tiles(place, own0, crossing1, rest1)
     held0 = early_columns(place, f0, g0, h0, s0)
-    g1, self_vis, held0 = lax.optimization_barrier((g1, self_vis, held0))
-    prior_vis, far_vis = cross_tiles(place, own0, own1, held0, f1, g1, h1, s1)
+    r1, self_vis, held0 = lax.optimization_barrier((r1, self_vis, held0))
+    prior_vis, far_vis = cross_tiles(place, own0, held0, crossing1, rest1, f1, r1, h1, s1)
     return (self_vis, prior_vis, far_vis)
 
 

time: 145 us -> 144 us (level)
  waiting for transfers between devices: 75.7 us -> 71.4 us
  Pallas kernels: 30 us -> 32.8 us
    ppermute x3 -> x4, waiting for transfers between devices: 27.7 us -> 21.8 us  [the longest x1 18.4 us: on_device(): over = lax.ppermute(stay, ('side', 'narrow'), OVER)]
    ppermute x1, starting transfers between devices: 1.67 us -> 5.15 us  [on_device(): got = lax.ppermute(leave, 'side', [(0, 1), (1, 0)])]
    ppermute x2, starting transfers between devices: 3.03 us -> 0.53 us  [swap(): return lax.ppermute(f, 'narrow', SWAPPED)]
    pallas_call x5 -> x6, Pallas kernels: 16.4 us -> 18.6 us  [the longest x3 8.05 us: rows_call(): pl.pallas_call(kernel, in_specs=[SMALL, IN_VMEM, pl.BlockSpec(memory_spac...]
    ppermute x3 -> x4, starting transfers between devices: 3.86 us -> 3.4 us  [the longest x1 1.33 us: on_device(): h1 = lax.ppermute(crossing1, 'narrow', EVEN_UP)]
  transfers between devices with their start and end apart: 11 -> 12, of which waited for: 5 -> 5; matrix products, arithmetic and copies ran while one was open for 0% -> 0% of each run, Pallas kernels for 13% -> 15%
where the time goes in v8:
time: 144 us
  waiting for transfers between devices  71.4 us (50%)
  starting transfers between devices  35.9 us (25%)
  Pallas kernels  32.8 us (23%)
  local copies, waits for them, and re-layouts  2.38 us (2%)
    ppermute x1, waiting for transfers between devices, exchange(): f = lax.ppermute(crossing, 'narrow', CROSSED)  22.1 us
    ppermute x1, waiting for transfers between devices, on_device(): got = lax.ppermute(leave, 'side', [(0, 1), (1, 0)])  19.2 us
    ppermute x1, waiting for transfers between devices, on_device(): over = lax.ppermute(stay, ('side', 'narrow'), OVER)  18.4 us
    all_to_all x1, starting transfers between devices, on_device(): lax.all_to_all(early, ('side', 'plane'), split_axis=0, concat_axis=0, til...  12.8 us
    pallas_call x2, Pallas kernels, filter_section(): pl.pallas_call(functools.partial(spectra_kernel, first, split), in_specs=...  11.6 us
    all_to_all x1, starting transfers between devices, on_device(): lax.all_to_all(late, 'plane', split_axis=0, concat_axis=0, tiled=True)  9.13 us
    all_to_all x1, waiting for transfers between devices, on_device(): lax.all_to_all(late, 'plane', split_axis=0, concat_axis=0, tiled=True)  8.3 us
    pallas_call x3, Pallas kernels, rows_call(): pl.pallas_call(kernel, in_specs=[SMALL, IN_VMEM, pl.BlockSpec(memory_spac...  8.05 us
  transfers between devices with their start and end apart: 12, of which 5 were waited for; matrix products, arithmetic and copies ran while one was open for 0% of the time, Pallas kernels for 15%

profile of v8, /device:TPU:24, one launch (start us, length us, event | category | flops | bytes accessed | tf_op | source)
XLA Modules:
  0.0 143.6 jit_solution(9843181038869947332)
XLA Ops:
  0.7 6.6 %filter_section.3 = bf16[64,32,512]{2,1,0:T(8,128)(2,1)} custom-call(s32[3]{0:T(128)S(1)} %pad_add_fusion.place_ref, bf16[4,396288]{1,0:T(4,128)(2,1)} %x_ref.3, bf16[1024,1024]{1,0:T(8,128)(2,1)} %constant.38.clone.table_ref, f32[4,1024]{1,0:T(4,128)} %taps_ref.3), custom_call_target="tpu_custom_call" | custom-call | tf_op jit(solution)/shard_map/filter_section/pallas_call | solution.py:107
  7.4 12.8 %all-to-all-start = ((bf16[64,32,512]{2,1,0:T(8,128)(2,1)}), bf16[64,32,512]{2,1,0:T(8,128)(2,1)S(1)}, u32[]{:S(2)}, u32[]{:S(2)}) async-start(bf16[64,32,512]{2,1,0:T(8,128)(2,1)} %filter_section.3), calls=%async_computation | async-start | bytes 4194304 | tf_op jit(solution)/shard_map/all_to_all | solution.py:381
  20.2 5.0 %filter_section.2 = (bf16[32,32,256]{2,1,0:T(8,128)(2,1)}, bf16[32,32,256]{2,1,0:T(8,128)(2,1)}) custom-call(s32[3]{0:T(128)S(1)} %pad_add_fusion.place_ref, bf16[4,396288]{1,0:T(4,128)(2,1)} %x_ref.3, bf16[1024,1024]{1,0:T(8,128)(2,1)} %constant.38.clone.table_ref, f32[4,1024]{1,0:T(4,128)} %taps_ref.3), custom_call_target="tpu_custom_call" | custom-call | tf_op jit(solution)/shard_map/filter_section/pallas_call | solution.py:107
  25.2 1.3 collective-permute-start.1
  26.5 0.7 collective-permute-start.2
  27.2 5.2 %collective-permute-start = (bf16[32,32,256]{2,1,0:T(8,128)(2,1)}, bf16[32,32,256]{2,1,0:T(8,128)(2,1)S(1)}, u32[]{:S(2)}, u32[]{:S(2)}) collective-permute-start(bf16[32,32,256]{2,1,0:T(8,128)(2,1)} %get-tuple-element.25), channel_id=1, source_target_pairs={{0,128},{128,0},{1,129},{129,1},{2,130},{130,2},{3,131},{131,3},{4... | collective-permute-start | bytes 1572872 | tf_op jit(solution)/shard_map/ppermute | solution.py:384
  32.3 18.4 %collective-permute-done.1.over_ref = bf16[32,32,256]{2,1,0:T(8,128)(2,1)S(1)} collective-permute-done((bf16[32,32,256]{2,1,0:T(8,128)(2,1)}, bf16[32,32,256]{2,1,0:T(8,128)(2,1)S(1)}, u32[]{:S(2)}, u32[]{:S(2)}) %collective-permute-start.1) | collective-permute-done | bytes 524320 | tf_op jit(solution)/shard_map/ppermute | solution.py:383
  50.7 19.2 %collective-permute-done.got_ref = bf16[32,32,256]{2,1,0:T(8,128)(2,1)S(1)} collective-permute-done((bf16[32,32,256]{2,1,0:T(8,128)(2,1)}, bf16[32,32,256]{2,1,0:T(8,128)(2,1)S(1)}, u32[]{:S(2)}, u32[]{:S(2)}) %collective-permute-start) | collective-permute-done | bytes 524320 | tf_op jit(solution)/shard_map/ppermute | solution.py:384
  69.9 1.0 copy-done.5
  70.9 1.8 %merge_sides.1 = bf16[32,3,32,256]{3,2,1,0:T(8,128)(2,1)} custom-call(s32[3]{0:T(128)S(1)} %pad_add_fusion.place_ref, bf16[32,32,256]{2,1,0:T(8,128)(2,1)S(1)} %copy-done.5, bf16[32,32,256]{2,1,0:T(8,128)(2,1)S(1)} %collective-permute-done.got_ref, bf16[32,32,256]{2,1,0:T(8,128)(2,1)S(1)} %collective-permute-done.1.over_ref, ...), custom_call_target="tpu_custom_call" | custom-call | tf_op jit(solution)/shard_map/merge_sides/pallas_call | solution.py:149
  72.8 1.3 copy-done.6
  74.1 9.1 %all-to-all-start.1 = ((bf16[32,3,32,256]{3,2,1,0:T(8,128)(2,1)}), bf16[32,3,32,256]{3,2,1,0:T(8,128)(2,1)S(1)}, u32[]{:S(2)}, u32[]{:S(2)}) async-start(bf16[32,3,32,256]{3,2,1,0:T(8,128)(2,1)} %merge_sides.1), calls=%async_computation.1 | async-start | bytes 3145728 | tf_op jit(solution)/shard_map/all_to_all | solution.py:387
  83.2 4.3 %early_rows.1 = (bf16[8,128,512]{2,1,0:T(8,128)(2,1)}, bf16[8,128,512]{2,1,0:T(8,128)(2,1)}, bf16[8,256,512]{2,1,0:T(8,128)(2,1)}) custom-call(s32[3]{0:T(128)S(1)} %pad_add_fusion.place_ref, bf16[256,256]{1,0:T(8,128)(2,1)S(1)} %copy-done.3, bf16[64,32,512]{2,1,0:T(8,128)(2,1)} %copy-done.6), custom_call_target="tpu_custom_call" | custom-call | tf_op jit(solution)/shard_map/early_rows/pallas_call | solution.py:192
  87.6 3.5 %collective-permute-start.7 = (bf16[8,256,512]{2,1,0:T(8,128)(2,1)}, bf16[8,256,512]{2,1,0:T(8,128)(2,1)}, u32[]{:S(2)}, u32[]{:S(2)}) collective-permute-start(bf16[8,256,512]{2,1,0:T(8,128)(2,1)} %get-tuple-element.33.own0_ref), channel_id=1, source_target_pairs={{0,1},{2,3},{4,5},{6,7},{8,9},{10,11},{12,13},{14,15},{16,17},{18,... | collective-permute-start | bytes 6291464 | tf_op jit(solution)/shard_map/ppermute | solution.py:373
  91.1 1.3 collective-permute-start.6
  92.4 22.1 %collective-permute-done.3.f_ref = bf16[8,128,512]{2,1,0:T(8,128)(2,1)S(1)} collective-permute-done((bf16[8,128,512]{2,1,0:T(8,128)(2,1)}, bf16[8,128,512]{2,1,0:T(8,128)(2,1)S(1)}, u32[]{:S(2)}, u32[]{:S(2)}) %collective-permute-start.3) | collective-permute-done | bytes 1048608 | tf_op jit(solution)/shard_map/ppermute | solution.py:371
  114.5 8.3 %all-to-all-done.1.source_ref = bf16[32,3,32,256]{3,2,1,0:T(8,128)(2,1)S(1)} async-done(((bf16[32,3,32,256]{3,2,1,0:T(8,128)(2,1)}), bf16[32,3,32,256]{3,2,1,0:T(8,128)(2,1)S(1)}, u32[]{:S(2)}, u32[]{:S(2)}) %all-to-all-start.1) | async-done | bytes 1572896 | tf_op jit(solution)/shard_map/all_to_all | solution.py:387
  122.8 1.7 %late_rows.2.rest1_ref.rest_ref = bf16[8,128,256]{2,1,0:T(8,128)(2,1)} custom-call(s32[3]{0:T(128)S(1)} %pad_add_fusion.place_ref, bf16[256,256]{1,0:T(8,128)(2,1)S(1)} %copy-done.3, bf16[32,3,32,256]{3,2,1,0:T(8,128)(2,1)S(1)} %all-to-all-done.1.source_ref), custom_call_target="tpu_custom_call" | custom-call | tf_op jit(solution)/shard_map/late_rows/pallas_call | solution.py:192
  124.5 2.1 %late_rows.3 = (bf16[8,128,256]{2,1,0:T(8,128)(2,1)}, bf16[8,128,256]{2,1,0:T(8,128)(2,1)}) custom-call(s32[3]{0:T(128)S(1)} %pad_add_fusion.place_ref, bf16[256,256]{1,0:T(8,128)(2,1)S(1)} %copy-done.3, bf16[32,3,32,256]{3,2,1,0:T(8,128)(2,1)S(1)} %all-to-all-done.1.source_ref), custom_call_target="tpu_custom_call" | custom-call | tf_op jit(solution)/shard_map/late_rows/pallas_call | solution.py:192
  126.6 1.3 collective-permute-start.5
  128.6 2.7 %early_columns.1.early_ref = bf16[8,384,512]{2,1,0:T(8,128)(2,1)S(1)} custom-call(s32[3]{0:T(128)S(1)} %pad_add_fusion.place_ref, bf16[8,128,512]{2,1,0:T(8,128)(2,1)S(1)} %collective-permute-done.3.f_ref, bf16[8,128,512]{2,1,0:T(8,128)(2,1)} %collective-permute-done.6.g_ref, bf16[8,256,512]{2,1,0:T(8,128)(2,1)} %collective-permute-done.7.h_ref, ...), custom_call_target="tpu_custom_call" | custom-call | tf_op jit(solution)/shard_map/early_columns/pallas_call | solution.py:297
  131.4 3.6 %self_tiles.1 = f32[2,8,256,256]{3,2,1,0:T(8,128)} custom-call(s32[3]{0:T(128)S(1)} %pad_add_fusion.place_ref, bf16[8,256,512]{2,1,0:T(8,128)(2,1)S(1)} %copy-done, bf16[8,128,256]{2,1,0:T(8,128)(2,1)S(1)} %copy-done.2, bf16[8,128,256]{2,1,0:T(8,128)(2,1)S(1)} %copy-done.1), custom_call_target="tpu_custom_call" | custom-call | tf_op jit(solution)/shard_map/self_tiles/pallas_call | solution.py:269
  135.0 3.4 %collective-permute-done.4.r_ref = bf16[8,128,256]{2,1,0:T(8,128)(2,1)S(1)} collective-permute-done((bf16[8,128,256]{2,1,0:T(8,128)(2,1)}, bf16[8,128,256]{2,1,0:T(8,128)(2,1)S(1)}, u32[]{:S(2)}, u32[]{:S(2)}) %collective-permute-start.4) | collective-permute-done | bytes 524320 | tf_op jit(solution)/shard_map/ppermute | solution.py:393
  138.4 5.1 %cross_tiles.1 = (f32[2,8,256,256]{3,2,1,0:T(8,128)}, f32[2,8,256,128]{3,2,1,0:T(8,128)}) custom-call(s32[3]{0:T(128)S(1)} %pad_add_fusion.place_ref, bf16[8,256,512]{2,1,0:T(8,128)(2,1)S(1)} %copy-done, bf16[8,384,512]{2,1,0:T(8,128)(2,1)S(1)} %early_columns.1.early_ref, bf16[8,128,256]{2,1,0:T(8,128)(2,1)S(1)} %copy-done.2, ...), custom_call_target="tpu_custom_call" | custom-call | tf_op jit(solution)/shard_map/cross_tiles/pallas_call | solution.py:339
  (24 shorter events, 0.8 us)
Async XLA Ops:
  7.4 65.4 %all-to-all-start = ((bf16[64,32,512]{2,1,0:T(8,128)(2,1)}), bf16[64,32,512]{2,1,0:T(8,128)(2,1)S(1)}, u32[]{:S(2)}, u32[]{:S(2)}) async-start(bf16[64,32,512]{2,1,0:T(8,128)(2,1)} %filter_section.3), calls=%async_computation | async-start | bytes 4194304 | tf_op jit(solution)/shard_map/all_to_all | solution.py:381
  25.2 25.6 %collective-permute-start.1 = (bf16[32,32,256]{2,1,0:T(8,128)(2,1)}, bf16[32,32,256]{2,1,0:T(8,128)(2,1)S(1)}, u32[]{:S(2)}, u32[]{:S(2)}) collective-permute-start(bf16[32,32,256]{2,1,0:T(8,128)(2,1)} %get-tuple-element.24.stay_ref), channel_id=1, source_target_pairs={{128,131},{129,130},{2,1},{3,0},{132,135},{133,134},{6,5},{7,4},{1... | collective-permute-start | bytes 1572872 | tf_op jit(solution)/shard_map/ppermute | solution.py:383
  26.5 24.3 %collective-permute-start.2 = (bf16[32,32,256]{2,1,0:T(8,128)(2,1)}, bf16[32,32,256]{2,1,0:T(8,128)(2,1)S(1)}, u32[]{:S(2)}, u32[]{:S(2)}) collective-permute-start(bf16[32,32,256]{2,1,0:T(8,128)(2,1)} %get-tuple-element.25), channel_id=1, source_target_pairs={{128,3},{129,2},{2,129},{3,128},{132,7},{133,6},{6,133},{7,132},{1... | collective-permute-start | bytes 1572872 | tf_op jit(solution)/shard_map/ppermute | solution.py:382
  27.2 42.7 %collective-permute-start = (bf16[32,32,256]{2,1,0:T(8,128)(2,1)}, bf16[32,32,256]{2,1,0:T(8,128)(2,1)S(1)}, u32[]{:S(2)}, u32[]{:S(2)}) collective-permute-start(bf16[32,32,256]{2,1,0:T(8,128)(2,1)} %get-tuple-element.25), channel_id=1, source_target_pairs={{0,128},{128,0},{1,129},{129,1},{2,130},{130,2},{3,131},{131,3},{4... | collective-permute-start | bytes 1572872 | tf_op jit(solution)/shard_map/ppermute | solution.py:384
  69.9 1.0 copy-start.5
  72.8 10.5 %copy-start.3 = (bf16[256,256]{1,0:T(8,128)(2,1)S(1)}, bf16[256,256]{1,0:T(8,128)(2,1)}, u32[]{:S(2)}) copy-start(bf16[256,256]{1,0:T(8,128)(2,1)} %constant.39.clone.order_ref) | copy-start | bytes 393220
  72.8 1.3 copy-start.6
  74.1 48.7 %all-to-all-start.1 = ((bf16[32,3,32,256]{3,2,1,0:T(8,128)(2,1)}), bf16[32,3,32,256]{3,2,1,0:T(8,128)(2,1)S(1)}, u32[]{:S(2)}, u32[]{:S(2)}) async-start(bf16[32,3,32,256]{3,2,1,0:T(8,128)(2,1)} %merge_sides.1), calls=%async_computation.1 | async-start | bytes 3145728 | tf_op jit(solution)/shard_map/all_to_all | solution.py:387
  87.5 27.0 %collective-permute-start.3 = (bf16[8,128,512]{2,1,0:T(8,128)(2,1)}, bf16[8,128,512]{2,1,0:T(8,128)(2,1)S(1)}, u32[]{:S(2)}, u32[]{:S(2)}) collective-permute-start(bf16[8,128,512]{2,1,0:T(8,128)(2,1)} %get-tuple-element.28), channel_id=1, source_target_pairs={{0,3},{1,2},{2,1},{3,0},{4,7},{5,6},{6,5},{7,4},{8,11},{9,10},{10,... | collective-permute-start | bytes 3145736 | tf_op jit(solution)/shard_map/ppermute | solution.py:371
  87.6 41.0 %collective-permute-start.7 = (bf16[8,256,512]{2,1,0:T(8,128)(2,1)}, bf16[8,256,512]{2,1,0:T(8,128)(2,1)}, u32[]{:S(2)}, u32[]{:S(2)}) collective-permute-start(bf16[8,256,512]{2,1,0:T(8,128)(2,1)} %get-tuple-element.33.own0_ref), channel_id=1, source_target_pairs={{0,1},{2,3},{4,5},{6,7},{8,9},{10,11},{12,13},{14,15},{16,17},{18,... | collective-permute-start | bytes 6291464 | tf_op jit(solution)/shard_map/ppermute | solution.py:373
  91.1 36.9 %collective-permute-start.6 = (bf16[8,128,512]{2,1,0:T(8,128)(2,1)}, bf16[8,128,512]{2,1,0:T(8,128)(2,1)}, u32[]{:S(2)}, u32[]{:S(2)}) collective-permute-start(bf16[8,128,512]{2,1,0:T(8,128)(2,1)} %get-tuple-element.37), channel_id=1, source_target_pairs={{1,2},{3,0},{5,6},{7,4},{9,10},{11,8},{13,14},{15,12},{17,18},{19,... | collective-permute-start | bytes 3145736 | tf_op jit(solution)/shard_map/ppermute | solution.py:372
  114.5 14.1 %collective-permute-start.8 = (bf16[8,128,512]{2,1,0:T(8,128)(2,1)S(1)}, bf16[8,128,512]{2,1,0:T(8,128)(2,1)}, u32[]{:S(2)}, u32[]{:S(2)}) collective-permute-start(bf16[8,128,512]{2,1,0:T(8,128)(2,1)S(1)} %collective-permute-done.3.f_ref), channel_id=1, source_target_pairs={{0,1},{1,0},{2,3},{3,2},{4,5},{5,4},{6,7},{7,6},{8,9},{9,8},{10,11... | collective-permute-start | bytes 3145736 | tf_op jit(solution)/shard_map/ppermute | solution.py:377
  126.6 4.7 %collective-permute-start.5 = (bf16[8,128,256]{2,1,0:T(8,128)(2,1)}, bf16[8,128,256]{2,1,0:T(8,128)(2,1)S(1)}, u32[]{:S(2)}, u32[]{:S(2)}) collective-permute-start(bf16[8,128,256]{2,1,0:T(8,128)(2,1)} %get-tuple-element.34.crossing1_ref.crossing_ref), channel_id=1, source_target_pairs={{0,1},{2,3},{4,5},{6,7},{8,9},{10,11},{12,13},{14,15},{16,17},{18,... | collective-permute-start | bytes 1572872 | tf_op jit(solution)/shard_map/ppermute | solution.py:396
  128.0 10.4 %collective-permute-start.4 = (bf16[8,128,256]{2,1,0:T(8,128)(2,1)}, bf16[8,128,256]{2,1,0:T(8,128)(2,1)S(1)}, u32[]{:S(2)}, u32[]{:S(2)}) collective-permute-start(bf16[8,128,256]{2,1,0:T(8,128)(2,1)} %late_rows.2.rest1_ref.rest_ref), channel_id=1, source_target_pairs={{0,1},{1,2},{2,3},{3,0},{4,5},{5,6},{6,7},{7,4},{8,9},{9,10},{10,1... | collective-permute-start | bytes 1572872 | tf_op jit(solution)/shard_map/ppermute | solution.py:393
  128.1 3.3 %copy-start = (bf16[8,256,512]{2,1,0:T(8,128)(2,1)S(1)}, bf16[8,256,512]{2,1,0:T(8,128)(2,1)}, u32[]{:S(2)}) copy-start(bf16[8,256,512]{2,1,0:T(8,128)(2,1)} %get-tuple-element.33.own0_ref) | copy-start | bytes 6291460
  128.1 3.3 %copy-start.1 = (bf16[8,128,256]{2,1,0:T(8,128)(2,1)S(1)}, bf16[8,128,256]{2,1,0:T(8,128)(2,1)}, u32[]{:S(2)}) copy-start(bf16[8,128,256]{2,1,0:T(8,128)(2,1)} %late_rows.2.rest1_ref.rest_ref) | copy-start | bytes 1572868
  128.1 3.3 %copy-start.2 = (bf16[8,128,256]{2,1,0:T(8,128)(2,1)S(1)}, bf16[8,128,256]{2,1,0:T(8,128)(2,1)}, u32[]{:S(2)}) copy-start(bf16[8,128,256]{2,1,0:T(8,128)(2,1)} %get-tuple-element.34.crossing1_ref.crossing_ref) | copy-start | bytes 1572868
  128.1 10.3 %collective-permute-start.9 = (bf16[8,128,256]{2,1,0:T(8,128)(2,1)}, bf16[8,128,256]{2,1,0:T(8,128)(2,1)S(1)}, u32[]{:S(2)}, u32[]{:S(2)}) collective-permute-start(bf16[8,128,256]{2,1,0:T(8,128)(2,1)} %get-tuple-element.40.f_ref), channel_id=1, source_target_pairs={{0,1},{1,0},{2,3},{3,2},{4,5},{5,4},{6,7},{7,6},{8,9},{9,8},{10,11... | collective-permute-start | bytes 1572872 | tf_op jit(solution)/shard_map/ppermute | solution.py:377
  131.3 7.0 %copy-start.4 = (bf16[8,128,256]{2,1,0:T(8,128)(2,1)S(1)}, bf16[8,128,256]{2,1,0:T(8,128)(2,1)}, u32[]{:S(2)}) copy-start(bf16[8,128,256]{2,1,0:T(8,128)(2,1)} %get-tuple-element.40.f_ref) | copy-start | bytes 1572868

commit v9 on v5

--- a/solution.py
+++ b/solution.py
@@ -121,7 +121,7 @@
             pltpu.SemaphoreType.DMA,
             pltpu.SemaphoreType.DMA((2 * blocks,)),
         ],
-        compiler_params=pltpu.CompilerParams(vmem_limit_bytes=40 * 1024 * 1024),
+        compiler_params=pltpu.CompilerParams(vmem_limit_bytes=20 * 1024 * 1024),
         name="filter_section",
     )(place, *(pltpu.with_memory_space_constraint(a, pltpu.HBM) for a in (samples, table, pfb_taps)))
 
@@ -143,36 +143,41 @@
         out_specs=pl.BlockSpec(memory_space=pltpu.HBM),
         out_shape=pltpu.HBM(shape, jnp.bfloat16),
         scratch_shapes=[pltpu.VMEM(shape, jnp.bfloat16), pltpu.SemaphoreType.DMA],
-        compiler_params=pltpu.CompilerParams(vmem_limit_bytes=40 * 1024 * 1024),
+        compiler_params=pltpu.CompilerParams(vmem_limit_bytes=8 * 1024 * 1024),
         name="merge_sides",
     )(place, stay, got)
 
 
-def rows_kernel(place_ref, order_ref, source_ref, cross_ref, rest_ref, whole_ref):
-    chip = place_ref[0]
-    order = order_ref[...]
-    for out_ref, half in ((cross_ref, 1 - chip), (rest_ref, chip)):
-        for g in range(4):
-            if len(source_ref.shape) == 3:
-                rows = source_ref[pl.ds(half * 32 + g * 8, 8)]
-            else:
-                rows = source_ref[g * 8 : (g + 1) * 8, half]
-            turned = jnp.dot(order, rows.reshape(256, rows.shape[-1]), preferred_element_type=jnp.float32).astype(jnp.bfloat16)
-            for c in range(8):
-                part = turned[c * 32 : (c + 1) * 32]
-                out_ref[c, g * 32 : (g + 1) * 32, :] = part
-                whole_ref[c, pl.ds(pl.multiple_of(half * 128 + g * 32, 32), 32), :] = part
-
-
-def channel_rows(place, order, source):
+def rows_kernel(crossing, place_ref, order_ref, source_ref, out_ref, source, held, in_sem, out_sem):
+    half = 1 - place_ref[0] if crossing else place_ref[0]
+    part = source_ref.at[pl.ds(half * 32, 32)] if len(source_ref.shape) == 3 else source_ref.at[:, half]
+    arriving = pltpu.make_async_copy(part, source, in_sem)
+    arriving.start()
+    arriving.wait()
+    for g in range(4):
+        rows = source[g * 8 : (g + 1) * 8].reshape(256, source.shape[-1])
+        turned = jnp.dot(order_ref[...], rows, preferred_element_type=jnp.float32).astype(jnp.bfloat16)
+        for c in range(8):
+            held[c, g * 32 : (g + 1) * 32, :] = turned[c * 32 : (c + 1) * 32]
+    leaving = pltpu.make_async_copy(held, out_ref, out_sem)
+    leaving.start()
+    leaving.wait()
+
+
+def channel_rows(place, order, source, crossing):
     lanes = source.shape[-1]
-    shapes = [(8, 128, lanes), (8, 128, lanes), (8, BLOCK, lanes)]
-    return pl.pallas_call(
-        rows_kernel,
-        in_specs=[SMALL, IN_VMEM, IN_VMEM],
-        out_specs=[IN_VMEM] * 3,
-        out_shape=[jax.ShapeDtypeStruct(shape, jnp.bfloat16) for shape in shapes],
-        compiler_params=pltpu.CompilerParams(vmem_limit_bytes=40 * 1024 * 1024),
+    return pl.pallas_call(
+        functools.partial(rows_kernel, crossing),
+        in_specs=[SMALL, IN_VMEM, pl.BlockSpec(memory_space=pl.ANY)],
+        out_specs=pl.BlockSpec(memory_space=pltpu.HBM),
+        out_shape=pltpu.HBM((8, 128, lanes), jnp.bfloat16),
+        scratch_shapes=[
+            pltpu.VMEM((32, 32, lanes), jnp.bfloat16),
+            pltpu.VMEM((8, 128, lanes), jnp.bfloat16),
+            pltpu.SemaphoreType.DMA,
+            pltpu.SemaphoreType.DMA,
+        ],
+        compiler_params=pltpu.CompilerParams(vmem_limit_bytes=12 * 1024 * 1024),
         name="channel_rows",
     )(place, order, source)
 
@@ -185,14 +190,22 @@
 
 
 def tile_products(rows, cols):
-    return lax.dot_general(stacked(rows), cols, NT, preferred_element_type=jnp.float32) * (1.0 / SPECTRA)
-
-
-def self_kernel(own0_ref, own1_ref, self_ref, self_held, sem):
+    return lax.dot_general(stacked(rows), cols, NT, preferred_element_type=jnp.float32)
+
+
+def put_halves(place_ref, chips_ref, others_ref, out_ref, lane=0):
+    chip = place_ref[0]
+    lanes = slice(lane, lane + chips_ref.shape[-1])
+    out_ref[:, pl.ds(pl.multiple_of(chip * 128, 128), 128), lanes] = chips_ref[...]
+    out_ref[:, pl.ds(pl.multiple_of((1 - chip) * 128, 128), 128), lanes] = others_ref[...]
+
+
+def self_kernel(place_ref, crossing0_ref, rest0_ref, crossing1_ref, rest1_ref, self_ref, own, self_held, sem):
+    put_halves(place_ref, rest0_ref, crossing0_ref, own)
+    put_halves(place_ref, rest1_ref, crossing1_ref, own, rest0_ref.shape[-1])
     copies = []
     for c in range(8):
-        rows = jnp.concatenate([own0_ref[c], own1_ref[c]], axis=1)
-        product = tile_products(rows, rows)
+        product = tile_products(own[c], own[c]) * (1.0 / SPECTRA)
         self_held[0, c] = product[:BLOCK]
         self_held[1, c] = product[BLOCK:]
         copies.append(pltpu.make_async_copy(self_held.at[:, c], self_ref.at[:, c], sem.at[c]))
@@ -201,55 +214,61 @@
         copy.wait()
 
 
-def self_tiles(own0, own1):
+def self_tiles(place, *own):
     return pl.pallas_call(
         self_kernel,
-        in_specs=[IN_VMEM] * 2,
+        in_specs=[SMALL] + [IN_VMEM] * 4,
         out_specs=pl.BlockSpec(memory_space=pltpu.HBM),
         out_shape=pltpu.HBM((2, 8, BLOCK, BLOCK), jnp.float32),
-        scratch_shapes=[pltpu.VMEM((2, 8, BLOCK, BLOCK), jnp.float32), pltpu.SemaphoreType.DMA((8,))],
-        compiler_params=pltpu.CompilerParams(vmem_limit_bytes=40 * 1024 * 1024),
+        scratch_shapes=[
+            pltpu.VMEM((8, BLOCK, own[0].shape[-1] + own[2].shape[-1]), jnp.bfloat16),
+            pltpu.VMEM((2, 8, BLOCK, BLOCK), jnp.float32),
+            pltpu.SemaphoreType.DMA((8,)),
+        ],
+        compiler_params=pltpu.CompilerParams(vmem_limit_bytes=14 * 1024 * 1024),
         name="self_tiles",
-    )(own0, own1)
-
-
-def put_columns(place_ref, f_ref, g_ref, h_ref, s_ref, out_ref):
-    chip = place_ref[0]
-
+    )(place, *own)
+
+
+def put_columns(place_ref, f_ref, r_ref, h_ref, s_ref, out_ref):
     @pl.when(place_ref[1] == 0)
     def _():
-        out_ref[:, pl.ds(pl.multiple_of(chip * 128, 128), 128), :] = f_ref[...]
-        out_ref[:, pl.ds(pl.multiple_of((1 - chip) * 128, 128), 128), :] = g_ref[...]
+        put_halves(place_ref, f_ref, r_ref, out_ref)
 
     @pl.when(place_ref[1] == 1)
     def _():
-        out_ref[:, :BLOCK, :] = h_ref[...]
+        put_halves(place_ref, r_ref, h_ref, out_ref)
 
     out_ref[:, BLOCK:, :] = s_ref[...]
 
 
-def early_kernel(place_ref, f_ref, g_ref, h_ref, s_ref, out_ref):
-    put_columns(place_ref, f_ref, g_ref, h_ref, s_ref, out_ref)
-
-
-def early_columns(place, *received):
+def early_kernel(place_ref, crossing_ref, rest_ref, f_ref, r_ref, h_ref, s_ref, out_ref, own, held):
+    put_halves(place_ref, rest_ref, crossing_ref, own)
+    put_columns(place_ref, f_ref, r_ref, h_ref, s_ref, held)
+    for c in range(8):
+        out_ref[c] = tile_products(own[c], held[c])
+
+
+def early_products(place, *chunk):
+    columns, lanes = BLOCK + BLOCK // 2, chunk[0].shape[-1]
     return pl.pallas_call(
         early_kernel,
-        in_specs=[SMALL] + [IN_VMEM] * 4,
+        in_specs=[SMALL] + [IN_VMEM] * 6,
         out_specs=IN_VMEM,
-        out_shape=jax.ShapeDtypeStruct((8, BLOCK + BLOCK // 2, received[0].shape[-1]), jnp.bfloat16),
-        compiler_params=pltpu.CompilerParams(vmem_limit_bytes=40 * 1024 * 1024),
-        name="early_columns",
-    )(place, *received)
-
-
-def cross_kernel(place_ref, own0_ref, own1_ref, early_ref, f_ref, g_ref, h_ref, s_ref, prior_ref, far_ref,
-                 held, prior_held, far_held, prior_sem, far_sem):
-    put_columns(place_ref, f_ref, g_ref, h_ref, s_ref, held)
+        out_shape=jax.ShapeDtypeStruct((8, 2 * BLOCK, columns), jnp.float32),
+        scratch_shapes=[pltpu.VMEM((8, BLOCK, lanes), jnp.bfloat16), pltpu.VMEM((8, columns, lanes), jnp.bfloat16)],
+        compiler_params=pltpu.CompilerParams(vmem_limit_bytes=14 * 1024 * 1024),
+        name="early_products",
+    )(place, *chunk)
+
+
+def cross_kernel(place_ref, early_ref, crossing_ref, rest_ref, f_ref, r_ref, h_ref, s_ref, prior_ref, far_ref,
+                 own, held, prior_held, far_held, prior_sem, far_sem):
+    put_halves(place_ref, rest_ref, crossing_ref, own)
+    put_columns(place_ref, f_ref, r_ref, h_ref, s_ref, held)
     copies = []
     for c in range(8):
-        rows = jnp.concatenate([own0_ref[c], own1_ref[c]], axis=1)
-        product = tile_products(rows, jnp.concatenate([early_ref[c], held[c]], axis=1))
+        product = (tile_products(own[c], held[c]) + early_ref[c]) * (1.0 / SPECTRA)
         for p in range(2):
             prior_held[p, c] = product[p * BLOCK : (p + 1) * BLOCK, :BLOCK]
             far_held[p, c] = product[p * BLOCK : (p + 1) * BLOCK, BLOCK:]
@@ -261,28 +280,30 @@
         copy.wait()
 
 
-def cross_tiles(place, own0, own1, early, *late):
+def cross_tiles(place, early, *chunk):
     in_hbm = pl.BlockSpec(memory_space=pltpu.HBM)
     prior_shape, far_shape = (2, 8, BLOCK, BLOCK), (2, 8, BLOCK, BLOCK // 2)
+    lanes = chunk[0].shape[-1]
     return pl.pallas_call(
         cross_kernel,
-        in_specs=[SMALL] + [IN_VMEM] * (3 + len(late)),
+        in_specs=[SMALL] + [IN_VMEM] * 7,
         out_specs=[in_hbm, in_hbm],
         out_shape=[pltpu.HBM(prior_shape, jnp.float32), pltpu.HBM(far_shape, jnp.float32)],
         scratch_shapes=[
-            pltpu.VMEM((8, BLOCK + BLOCK // 2, late[0].shape[-1]), jnp.bfloat16),
+            pltpu.VMEM((8, BLOCK, lanes), jnp.bfloat16),
+            pltpu.VMEM((8, BLOCK + BLOCK // 2, lanes), jnp.bfloat16),
             pltpu.VMEM(prior_shape, jnp.float32),
             pltpu.VMEM(far_shape, jnp.float32),
             pltpu.SemaphoreType.DMA((8,)),
             pltpu.SemaphoreType.DMA((8,)),
         ],
-        compiler_params=pltpu.CompilerParams(vmem_limit_bytes=40 * 1024 * 1024),
+        compiler_params=pltpu.CompilerParams(vmem_limit_bytes=20 * 1024 * 1024),
         name="cross_tiles",
-    )(place, own0, own1, early, *late)
+    )(place, early, *chunk)
 
 
 CROSSED = [(0, 3), (1, 2), (2, 1), (3, 0)]
-ODD_OVER = [(1, 2), (3, 0)]
+NEXT = [(0, 1), (1, 2), (2, 3), (3, 0)]
 EVEN_UP = [(0, 1), (2, 3)]
 SWAPPED = [(0, 1), (1, 0), (2, 3), (3, 2)]
 
@@ -290,12 +311,6 @@
 def on_device(table, order, samples, pfb_taps):
     position = lax.axis_index("narrow")
     place = jnp.stack([position // 2, position % 2, lax.axis_index("side")]).astype(jnp.int32)
-
-    def exchange(crossing, rest, whole):
-        f = lax.ppermute(crossing, "narrow", CROSSED)
-        g = lax.ppermute(rest, "narrow", ODD_OVER)
-        h = lax.ppermute(whole, "narrow", EVEN_UP)
-        return f, g, h
 
     def swap(f):
         return lax.ppermute(f, "narrow", SWAPPED)
@@ -306,16 +321,24 @@
     late = merge(place, stay, lax.ppermute(leave, "side", [(0, 1), (1, 0)]))
     late, source0 = lax.optimization_barrier((late, source0))
     source1 = lax.all_to_all(late, "plane", split_axis=0, concat_axis=0, tiled=True)
-    crossing0, rest0, own0 = channel_rows(place, order, source0)
-    f, g, h = exchange(crossing0, rest0, own0)
-    held0 = early_columns(place, f, g, h, swap(f))
-    source1, held0 = lax.optimization_barrier((source1, held0))
-    crossing1, rest1, own1 = channel_rows(place, order, source1)
-    f, g, h = exchange(crossing1, rest1, own1)
-    own1, h = lax.optimization_barrier((own1, h))
-    self_vis = self_tiles(own0, own1)
-    f, self_vis = lax.optimization_barrier((f, self_vis))
-    prior_vis, far_vis = cross_tiles(place, own0, own1, held0, f, g, h, swap(f))
+    crossing0 = channel_rows(place, order, source0, True)
+    f0 = lax.ppermute(crossing0, "narrow", CROSSED)
+    rest0 = channel_rows(place, order, source0, False)
+    r0 = lax.ppermute(rest0, "narrow", NEXT)
+    h0 = lax.ppermute(crossing0, "narrow", EVEN_UP)
+    f0, rest0 = lax.optimization_barrier((f0, rest0))
+    s0 = swap(f0)
+    source1, f0, h0, s0 = lax.optimization_barrier((source1, f0, h0, s0))
+    crossing1 = channel_rows(place, order, source1, True)
+    f1 = lax.ppermute(crossing1, "narrow", CROSSED)
+    rest1 = channel_rows(place, order, source1, False)
+    r1 = lax.ppermute(rest1, "narrow", NEXT)
+    h1 = lax.ppermute(crossing1, "narrow", EVEN_UP)
+    crossing1, r0, h1 = lax.optimization_barrier((crossing1, r0, h1))
+    early = early_products(place, crossing0, rest0, f0, r0, h0, s0)
+    self_vis = self_tiles(place, crossing0, rest0, crossing1, rest1)
+    f1, self_vis, early = lax.optimization_barrier((f1, self_vis, early))
+    prior_vis, far_vis = cross_tiles(place, early, crossing1, rest1, f1, r1, h1, swap(f1))
     return (self_vis, prior_vis, far_vis)
 
 

time: 147 us -> 139 us (0.946)
  waiting for transfers between devices: 79.8 us -> 72.3 us
  Pallas kernels: 26.7 us -> 32.9 us
  local copies, waits for them, and re-layouts: 8.7 us -> 4.12 us
  starting transfers between devices: 30.1 us -> 28 us
    ppermute x6, waiting for transfers between devices: 37.7 us -> 23 us  [the longest x1 15.3 us: on_device(): f0 = lax.ppermute(crossing0, 'narrow', CROSSED)]
    all_to_all x1, waiting for transfers between devices: 0.01 us -> 7.16 us  [on_device(): lax.all_to_all(late, 'plane', split_axis=0, concat_axis=0, tiled=True)]
    pallas_call x5 -> x7, Pallas kernels: 13.5 us -> 19.7 us  [the longest x4 7.52 us: channel_rows(): pl.pallas_call(functools.partial(rows_kernel, crossing), in_specs=[SMALL,...]
    unnamed x20 -> x22, local copies, waits for them, and re-layouts: 8.7 us -> 4.12 us
    ppermute x6, starting transfers between devices: 10.3 us -> 6.78 us  [the longest x1 2.79 us: on_device(): h0 = lax.ppermute(crossing0, 'narrow', EVEN_UP)]
  transfers between devices with their start and end apart: 11 -> 11, of which waited for: 7 -> 7; matrix products, arithmetic and copies ran while one was open for 0% -> 0% of each run, Pallas kernels for 8% -> 15%
where the time goes in v9:
time: 139 us; the launch traced here: 138 us
  waiting for transfers between devices  72.3 us (52%)
  Pallas kernels  32.9 us (24%)
  starting transfers between devices  28 us (20%)
  local copies, waits for them, and re-layouts  4.12 us (3%)
    all_to_all x1, waiting for transfers between devices, on_device(): lax.all_to_all(early, ('side', 'plane'), split_axis=0, concat_axis=0, til...  23.3 us
    ppermute x1, waiting for transfers between devices, on_device(): late = merge(place, stay, lax.ppermute(leave, 'side', [(0, 1), (1, 0)]))  18.7 us
    ppermute x1, waiting for transfers between devices, on_device(): f0 = lax.ppermute(crossing0, 'narrow', CROSSED)  15.3 us
    all_to_all x1, starting transfers between devices, on_device(): lax.all_to_all(early, ('side', 'plane'), split_axis=0, concat_axis=0, til...  12.8 us
    pallas_call x2, Pallas kernels, filter_section(): pl.pallas_call(functools.partial(spectra_kernel, first, split), in_specs=...  11.6 us
    pallas_call x4, Pallas kernels, channel_rows(): pl.pallas_call(functools.partial(rows_kernel, crossing), in_specs=[SMALL,...  7.52 us
    all_to_all x1, waiting for transfers between devices, on_device(): lax.all_to_all(late, 'plane', split_axis=0, concat_axis=0, tiled=True)  7.16 us
    all_to_all x1, starting transfers between devices, on_device(): lax.all_to_all(late, 'plane', split_axis=0, concat_axis=0, tiled=True)  6.71 us
  transfers between devices with their start and end apart: 11, of which 7 were waited for; matrix products, arithmetic and copies ran while one was open for 0% of the time, Pallas kernels for 15%

profile of v9, /device:TPU:24, one launch (start us, length us, event | category | flops | bytes accessed | tf_op | source)
XLA Modules:
  0.0 138.3 jit_solution(17714336017290102132)
XLA Ops:
  0.7 6.6 %filter_section.3 = bf16[64,32,512]{2,1,0:T(8,128)(2,1)} custom-call(s32[3]{0:T(128)S(1)} %pad_add_fusion.place_ref, bf16[4,396288]{1,0:T(4,128)(2,1)} %x_ref.3, bf16[1024,1024]{1,0:T(8,128)(2,1)} %constant.38.clone.table_ref, f32[4,1024]{1,0:T(4,128)} %taps_ref.3), custom_call_target="tpu_custom_call" | custom-call | tf_op jit(solution)/shard_map/filter_section/pallas_call | solution.py:107
  7.4 12.8 %all-to-all-start = ((bf16[64,32,512]{2,1,0:T(8,128)(2,1)}), bf16[64,32,512]{2,1,0:T(8,128)(2,1)S(1)}, u32[]{:S(2)}, u32[]{:S(2)}) async-start(bf16[64,32,512]{2,1,0:T(8,128)(2,1)} %filter_section.3), calls=%async_computation | async-start | bytes 4194304 | tf_op jit(solution)/shard_map/all_to_all | solution.py:320
  20.2 5.0 %filter_section.2 = (bf16[32,32,256]{2,1,0:T(8,128)(2,1)}, bf16[32,32,256]{2,1,0:T(8,128)(2,1)}) custom-call(s32[3]{0:T(128)S(1)} %pad_add_fusion.place_ref, bf16[4,396288]{1,0:T(4,128)(2,1)} %x_ref.3, bf16[1024,1024]{1,0:T(8,128)(2,1)} %constant.38.clone.table_ref, f32[4,1024]{1,0:T(4,128)} %taps_ref.3), custom_call_target="tpu_custom_call" | custom-call | tf_op jit(solution)/shard_map/filter_section/pallas_call | solution.py:107
  25.2 1.7 %collective-permute-start = (bf16[32,32,256]{2,1,0:T(8,128)(2,1)}, bf16[32,32,256]{2,1,0:T(8,128)(2,1)S(1)}, u32[]{:S(2)}, u32[]{:S(2)}) collective-permute-start(bf16[32,32,256]{2,1,0:T(8,128)(2,1)} %get-tuple-element.22), channel_id=1, source_target_pairs={{0,128},{128,0},{1,129},{129,1},{2,130},{130,2},{3,131},{131,3},{4... | collective-permute-start | bytes 1572872 | tf_op jit(solution)/shard_map/ppermute | solution.py:321
  26.8 18.7 %collective-permute-done.got_ref = bf16[32,32,256]{2,1,0:T(8,128)(2,1)S(1)} collective-permute-done((bf16[32,32,256]{2,1,0:T(8,128)(2,1)}, bf16[32,32,256]{2,1,0:T(8,128)(2,1)S(1)}, u32[]{:S(2)}, u32[]{:S(2)}) %collective-permute-start) | collective-permute-done | bytes 524320 | tf_op jit(solution)/shard_map/ppermute | solution.py:321
  45.6 1.0 copy-done.10
  46.6 1.6 %merge_sides.1 = bf16[32,2,32,256]{3,2,1,0:T(8,128)(2,1)} custom-call(s32[3]{0:T(128)S(1)} %pad_add_fusion.place_ref, bf16[32,32,256]{2,1,0:T(8,128)(2,1)S(1)} %copy-done.10, bf16[32,32,256]{2,1,0:T(8,128)(2,1)S(1)} %collective-permute-done.got_ref), custom_call_target="tpu_custom_call" | custom-call | tf_op jit(solution)/shard_map/merge_sides/pallas_call | solution.py:140
  48.2 23.3 %all-to-all-done.source_ref = bf16[64,32,512]{2,1,0:T(8,128)(2,1)S(1)} async-done(((bf16[64,32,512]{2,1,0:T(8,128)(2,1)}), bf16[64,32,512]{2,1,0:T(8,128)(2,1)S(1)}, u32[]{:S(2)}, u32[]{:S(2)}) %all-to-all-start) | async-done | bytes 2097184 | tf_op jit(solution)/shard_map/all_to_all | solution.py:320
  71.6 2.0 %channel_rows.4.crossing0_ref.crossing_ref = bf16[8,128,512]{2,1,0:T(8,128)(2,1)} custom-call(s32[3]{0:T(128)S(1)} %pad_add_fusion.place_ref, bf16[256,256]{1,0:T(8,128)(2,1)S(1)} %copy-done.7, bf16[64,32,512]{2,1,0:T(8,128)(2,1)S(1)} %all-to-all-done.source_ref), custom_call_target="tpu_custom_call" | custom-call | tf_op jit(solution)/shard_map/channel_rows/pallas_call | solution.py:169
  73.9 6.7 %all-to-all-start.1 = ((bf16[32,2,32,256]{3,2,1,0:T(8,128)(2,1)}), bf16[32,2,32,256]{3,2,1,0:T(8,128)(2,1)S(1)}, u32[]{:S(2)}, u32[]{:S(2)}) async-start(bf16[32,2,32,256]{3,2,1,0:T(8,128)(2,1)} %merge_sides.1), calls=%async_computation.1 | async-start | bytes 2097152 | tf_op jit(solution)/shard_map/all_to_all | solution.py:323
  80.6 2.0 %channel_rows.5.rest0_ref.rest_ref = bf16[8,128,512]{2,1,0:T(8,128)(2,1)} custom-call(s32[3]{0:T(128)S(1)} %pad_add_fusion.place_ref, bf16[256,256]{1,0:T(8,128)(2,1)S(1)} %copy-done.7, bf16[64,32,512]{2,1,0:T(8,128)(2,1)S(1)} %all-to-all-done.source_ref), custom_call_target="tpu_custom_call" | custom-call | tf_op jit(solution)/shard_map/channel_rows/pallas_call | solution.py:169
  82.7 2.8 %collective-permute-start.2 = (bf16[8,128,512]{2,1,0:T(8,128)(2,1)S(1)}, bf16[8,128,512]{2,1,0:T(8,128)(2,1)S(1)}, u32[]{:S(2)}, u32[]{:S(2)}) collective-permute-start(bf16[8,128,512]{2,1,0:T(8,128)(2,1)S(1)} %copy-done), channel_id=1, source_target_pairs={{0,1},{2,3},{4,5},{6,7},{8,9},{10,11},{12,13},{14,15},{16,17},{18,... | collective-permute-start | bytes 3145736 | tf_op jit(solution)/shard_map/ppermute | solution.py:328
  85.5 15.3 %collective-permute-done.1.f_ref = bf16[8,128,512]{2,1,0:T(8,128)(2,1)} collective-permute-done((bf16[8,128,512]{2,1,0:T(8,128)(2,1)}, bf16[8,128,512]{2,1,0:T(8,128)(2,1)}, u32[]{:S(2)}, u32[]{:S(2)}) %collective-permute-start.1) | collective-permute-done | bytes 1048608 | tf_op jit(solution)/shard_map/ppermute | solution.py:325
  102.2 7.2 %all-to-all-done.1.source_ref = bf16[32,2,32,256]{3,2,1,0:T(8,128)(2,1)S(1)} async-done(((bf16[32,2,32,256]{3,2,1,0:T(8,128)(2,1)}), bf16[32,2,32,256]{3,2,1,0:T(8,128)(2,1)S(1)}, u32[]{:S(2)}, u32[]{:S(2)}) %all-to-all-start.1) | async-done | bytes 1048608 | tf_op jit(solution)/shard_map/all_to_all | solution.py:323
  109.4 1.7 %channel_rows.6.crossing1_ref.crossing_ref = bf16[8,128,256]{2,1,0:T(8,128)(2,1)} custom-call(s32[3]{0:T(128)S(1)} %pad_add_fusion.place_ref, bf16[256,256]{1,0:T(8,128)(2,1)S(1)} %copy-done.7, bf16[32,2,32,256]{3,2,1,0:T(8,128)(2,1)S(1)} %all-to-all-done.1.source_ref), custom_call_target="tpu_custom_call" | custom-call | tf_op jit(solution)/shard_map/channel_rows/pallas_call | solution.py:169
  111.1 2.1 %collective-permute-start.6 = (bf16[8,128,256]{2,1,0:T(8,128)(2,1)}, bf16[8,128,256]{2,1,0:T(8,128)(2,1)S(1)}, u32[]{:S(2)}, u32[]{:S(2)}) collective-permute-start(bf16[8,128,256]{2,1,0:T(8,128)(2,1)} %channel_rows.6.crossing1_ref.crossing_ref), channel_id=1, source_target_pairs={{0,1},{2,3},{4,5},{6,7},{8,9},{10,11},{12,13},{14,15},{16,17},{18,... | collective-permute-start | bytes 1572872 | tf_op jit(solution)/shard_map/ppermute | solution.py:336
  113.3 1.7 %channel_rows.7.rest1_ref.rest_ref = bf16[8,128,256]{2,1,0:T(8,128)(2,1)} custom-call(s32[3]{0:T(128)S(1)} %pad_add_fusion.place_ref, bf16[256,256]{1,0:T(8,128)(2,1)S(1)} %copy-done.7, bf16[32,2,32,256]{3,2,1,0:T(8,128)(2,1)S(1)} %all-to-all-done.1.source_ref), custom_call_target="tpu_custom_call" | custom-call | tf_op jit(solution)/shard_map/channel_rows/pallas_call | solution.py:169
  115.0 1.1 collective-permute-start.7
  117.9 1.0 copy-done.5
  118.9 3.8 %self_tiles.1 = f32[2,8,256,256]{3,2,1,0:T(8,128)} custom-call(s32[3]{0:T(128)S(1)} %pad_add_fusion.place_ref, bf16[8,128,512]{2,1,0:T(8,128)(2,1)S(1)} %copy-done.1, bf16[8,128,512]{2,1,0:T(8,128)(2,1)S(1)} %copy-done.2, bf16[8,128,256]{2,1,0:T(8,128)(2,1)S(1)} %copy-done.3, bf16[8,128,256]{2,1,0:T(8,128)(2,1)S(1)} %copy-done.5), custom_call_target="tpu_custom_call" | custom-call | tf_op jit(solution)/shard_map/self_tiles/pallas_call | solution.py:218
  122.7 4.6 %early_products.1.early_ref = f32[8,512,384]{2,1,0:T(8,128)S(1)} custom-call(s32[3]{0:T(128)S(1)} %pad_add_fusion.place_ref, bf16[8,128,512]{2,1,0:T(8,128)(2,1)S(1)} %copy-done.1, bf16[8,128,512]{2,1,0:T(8,128)(2,1)S(1)} %copy-done.2, bf16[8,128,512]{2,1,0:T(8,128)(2,1)} %collective-permute-done.1.f_ref, bf16[8,128,512]{2,1,0:T(8,128)(2,1)} %collective-permute-done.5.r_ref, ...), custom_call_target="tpu_custom_call" | custom-call | tf_op jit(solution)/shard_map/early_products/pallas_call | solution.py:254
  127.3 1.4 %collective-permute-done.4.f_ref = bf16[8,128,256]{2,1,0:T(8,128)(2,1)S(1)} collective-permute-done((bf16[8,128,256]{2,1,0:T(8,128)(2,1)}, bf16[8,128,256]{2,1,0:T(8,128)(2,1)S(1)}, u32[]{:S(2)}, u32[]{:S(2)}) %collective-permute-start.4) | collective-permute-done | bytes 524320 | tf_op jit(solution)/shard_map/ppermute | solution.py:333
  128.8 5.6 %collective-permute-done.7.r_ref = bf16[8,128,256]{2,1,0:T(8,128)(2,1)S(1)} collective-permute-done((bf16[8,128,256]{2,1,0:T(8,128)(2,1)}, bf16[8,128,256]{2,1,0:T(8,128)(2,1)S(1)}, u32[]{:S(2)}, u32[]{:S(2)}) %collective-permute-start.7) | collective-permute-done | bytes 524320 | tf_op jit(solution)/shard_map/ppermute | solution.py:335
  134.4 3.8 %cross_tiles.1 = (f32[2,8,256,256]{3,2,1,0:T(8,128)}, f32[2,8,256,128]{3,2,1,0:T(8,128)}) custom-call(s32[3]{0:T(128)S(1)} %pad_add_fusion.place_ref, f32[8,512,384]{2,1,0:T(8,128)S(1)} %early_products.1.early_ref, bf16[8,128,256]{2,1,0:T(8,128)(2,1)S(1)} %copy-done.4, bf16[8,128,256]{2,1,0:T(8,128)(2,1)S(1)} %copy-done.6, ...), custom_call_target="tpu_custom_call" | custom-call | tf_op jit(solution)/shard_map/cross_tiles/pallas_call | solution.py:287
  (31 shorter events, 3.7 us)
Async XLA Ops:
  7.4 64.2 %all-to-all-start = ((bf16[64,32,512]{2,1,0:T(8,128)(2,1)}), bf16[64,32,512]{2,1,0:T(8,128)(2,1)S(1)}, u32[]{:S(2)}, u32[]{:S(2)}) async-start(bf16[64,32,512]{2,1,0:T(8,128)(2,1)} %filter_section.3), calls=%async_computation | async-start | bytes 4194304 | tf_op jit(solution)/shard_map/all_to_all | solution.py:320
  20.2 51.4 %copy-start.7 = (bf16[256,256]{1,0:T(8,128)(2,1)S(1)}, bf16[256,256]{1,0:T(8,128)(2,1)}, u32[]{:S(2)}) copy-start(bf16[256,256]{1,0:T(8,128)(2,1)} %constant.39.clone.order_ref) | copy-start | bytes 393220
  25.2 20.4 %collective-permute-start = (bf16[32,32,256]{2,1,0:T(8,128)(2,1)}, bf16[32,32,256]{2,1,0:T(8,128)(2,1)S(1)}, u32[]{:S(2)}, u32[]{:S(2)}) collective-permute-start(bf16[32,32,256]{2,1,0:T(8,128)(2,1)} %get-tuple-element.22), channel_id=1, source_target_pairs={{0,128},{128,0},{1,129},{129,1},{2,130},{130,2},{3,131},{131,3},{4... | collective-permute-start | bytes 1572872 | tf_op jit(solution)/shard_map/ppermute | solution.py:321
  45.6 1.0 copy-start.10
  73.6 27.1 %collective-permute-start.1 = (bf16[8,128,512]{2,1,0:T(8,128)(2,1)}, bf16[8,128,512]{2,1,0:T(8,128)(2,1)}, u32[]{:S(2)}, u32[]{:S(2)}) collective-permute-start(bf16[8,128,512]{2,1,0:T(8,128)(2,1)} %channel_rows.4.crossing0_ref.crossing_ref), channel_id=1, source_target_pairs={{0,3},{1,2},{2,1},{3,0},{4,7},{5,6},{6,5},{7,4},{8,11},{9,10},{10,... | collective-permute-start | bytes 3145736 | tf_op jit(solution)/shard_map/ppermute | solution.py:325
  73.9 35.5 %all-to-all-start.1 = ((bf16[32,2,32,256]{3,2,1,0:T(8,128)(2,1)}), bf16[32,2,32,256]{3,2,1,0:T(8,128)(2,1)S(1)}, u32[]{:S(2)}, u32[]{:S(2)}) async-start(bf16[32,2,32,256]{3,2,1,0:T(8,128)(2,1)} %merge_sides.1), calls=%async_computation.1 | async-start | bytes 2097152 | tf_op jit(solution)/shard_map/all_to_all | solution.py:323
  80.6 2.1 %copy-start = (bf16[8,128,512]{2,1,0:T(8,128)(2,1)S(1)}, bf16[8,128,512]{2,1,0:T(8,128)(2,1)}, u32[]{:S(2)}) copy-start(bf16[8,128,512]{2,1,0:T(8,128)(2,1)} %channel_rows.4.crossing0_ref.crossing_ref) | copy-start | bytes 3145732
  82.7 34.2 %copy-start.1 = (bf16[8,128,512]{2,1,0:T(8,128)(2,1)S(1)}, bf16[8,128,512]{2,1,0:T(8,128)(2,1)}, u32[]{:S(2)}) copy-start(bf16[8,128,512]{2,1,0:T(8,128)(2,1)} %channel_rows.4.crossing0_ref.crossing_ref) | copy-start | bytes 3145732
  82.7 34.2 %copy-start.2 = (bf16[8,128,512]{2,1,0:T(8,128)(2,1)S(1)}, bf16[8,128,512]{2,1,0:T(8,128)(2,1)}, u32[]{:S(2)}) copy-start(bf16[8,128,512]{2,1,0:T(8,128)(2,1)} %channel_rows.5.rest0_ref.rest_ref) | copy-start | bytes 3145732
  82.7 18.6 %collective-permute-start.2 = (bf16[8,128,512]{2,1,0:T(8,128)(2,1)S(1)}, bf16[8,128,512]{2,1,0:T(8,128)(2,1)S(1)}, u32[]{:S(2)}, u32[]{:S(2)}) collective-permute-start(bf16[8,128,512]{2,1,0:T(8,128)(2,1)S(1)} %copy-done), channel_id=1, source_target_pairs={{0,1},{2,3},{4,5},{6,7},{8,9},{10,11},{12,13},{14,15},{16,17},{18,... | collective-permute-start | bytes 3145736 | tf_op jit(solution)/shard_map/ppermute | solution.py:328
  100.8 8.6 %collective-permute-start.3 = (bf16[8,128,512]{2,1,0:T(8,128)(2,1)}, bf16[8,128,512]{2,1,0:T(8,128)(2,1)}, u32[]{:S(2)}, u32[]{:S(2)}) collective-permute-start(bf16[8,128,512]{2,1,0:T(8,128)(2,1)} %collective-permute-done.1.f_ref), channel_id=1, source_target_pairs={{0,1},{1,0},{2,3},{3,2},{4,5},{5,4},{6,7},{7,6},{8,9},{9,8},{10,11... | collective-permute-start | bytes 3145736 | tf_op jit(solution)/shard_map/ppermute | solution.py:316
  100.8 16.0 %collective-permute-start.5 = (bf16[8,128,512]{2,1,0:T(8,128)(2,1)}, bf16[8,128,512]{2,1,0:T(8,128)(2,1)}, u32[]{:S(2)}, u32[]{:S(2)}) collective-permute-start(bf16[8,128,512]{2,1,0:T(8,128)(2,1)} %channel_rows.5.rest0_ref.rest_ref), channel_id=1, source_target_pairs={{0,1},{1,2},{2,3},{3,0},{4,5},{5,6},{6,7},{7,4},{8,9},{9,10},{10,1... | collective-permute-start | bytes 3145736 | tf_op jit(solution)/shard_map/ppermute | solution.py:327
  101.3 1.0 copy-start.8
  111.1 5.7 %collective-permute-start.6 = (bf16[8,128,256]{2,1,0:T(8,128)(2,1)}, bf16[8,128,256]{2,1,0:T(8,128)(2,1)S(1)}, u32[]{:S(2)}, u32[]{:S(2)}) collective-permute-start(bf16[8,128,256]{2,1,0:T(8,128)(2,1)} %channel_rows.6.crossing1_ref.crossing_ref), channel_id=1, source_target_pairs={{0,1},{2,3},{4,5},{6,7},{8,9},{10,11},{12,13},{14,15},{16,17},{18,... | collective-permute-start | bytes 1572872 | tf_op jit(solution)/shard_map/ppermute | solution.py:336
  113.2 15.6 %collective-permute-start.4 = (bf16[8,128,256]{2,1,0:T(8,128)(2,1)}, bf16[8,128,256]{2,1,0:T(8,128)(2,1)S(1)}, u32[]{:S(2)}, u32[]{:S(2)}) collective-permute-start(bf16[8,128,256]{2,1,0:T(8,128)(2,1)} %channel_rows.6.crossing1_ref.crossing_ref), channel_id=1, source_target_pairs={{0,3},{1,2},{2,1},{3,0},{4,7},{5,6},{6,5},{7,4},{8,11},{9,10},{10,... | collective-permute-start | bytes 1572872 | tf_op jit(solution)/shard_map/ppermute | solution.py:333
  113.3 9.4 %copy-start.9 = (bf16[8,128,512]{2,1,0:T(8,128)(2,1)S(1)}, bf16[8,128,512]{2,1,0:T(8,128)(2,1)}, u32[]{:S(2)}) copy-start(bf16[8,128,512]{2,1,0:T(8,128)(2,1)} %copy-done.8) | copy-start | bytes 3145732
  115.0 19.3 %collective-permute-start.7 = (bf16[8,128,256]{2,1,0:T(8,128)(2,1)}, bf16[8,128,256]{2,1,0:T(8,128)(2,1)S(1)}, u32[]{:S(2)}, u32[]{:S(2)}) collective-permute-start(bf16[8,128,256]{2,1,0:T(8,128)(2,1)} %channel_rows.7.rest1_ref.rest_ref), channel_id=1, source_target_pairs={{0,1},{1,2},{2,3},{3,0},{4,5},{5,6},{6,7},{7,4},{8,9},{9,10},{10,1... | collective-permute-start | bytes 1572872 | tf_op jit(solution)/shard_map/ppermute | solution.py:335
  116.8 1.0 copy-start.3
  117.9 1.0 copy-start.5
  122.7 11.7 %copy-start.4 = (bf16[8,128,256]{2,1,0:T(8,128)(2,1)S(1)}, bf16[8,128,256]{2,1,0:T(8,128)(2,1)}, u32[]{:S(2)}) copy-start(bf16[8,128,256]{2,1,0:T(8,128)(2,1)} %channel_rows.6.crossing1_ref.crossing_ref) | copy-start | bytes 1572868
  122.7 11.6 %copy-start.6 = (bf16[8,128,256]{2,1,0:T(8,128)(2,1)S(1)}, bf16[8,128,256]{2,1,0:T(8,128)(2,1)}, u32[]{:S(2)}) copy-start(bf16[8,128,256]{2,1,0:T(8,128)(2,1)} %channel_rows.7.rest1_ref.rest_ref) | copy-start | bytes 1572868
  128.8 5.6 %collective-permute-start.8 = (bf16[8,128,256]{2,1,0:T(8,128)(2,1)S(1)}, bf16[8,128,256]{2,1,0:T(8,128)(2,1)S(1)}, u32[]{:S(2)}, u32[]{:S(2)}) collective-permute-start(bf16[8,128,256]{2,1,0:T(8,128)(2,1)S(1)} %collective-permute-done.4.f_ref), channel_id=1, source_target_pairs={{0,1},{1,0},{2,3},{3,2},{4,5},{5,4},{6,7},{7,6},{8,9},{9,8},{10,11... | collective-permute-start | bytes 1572872 | tf_op jit(solution)/shard_map/ppermute | solution.py:316

commit v10 on v9

--- a/solution.py
+++ b/solution.py
@@ -334,7 +334,7 @@
     rest1 = channel_rows(place, order, source1, False)
     r1 = lax.ppermute(rest1, "narrow", NEXT)
     h1 = lax.ppermute(crossing1, "narrow", EVEN_UP)
-    crossing1, r0, h1 = lax.optimization_barrier((crossing1, r0, h1))
+    crossing1, r0 = lax.optimization_barrier((crossing1, r0))
     early = early_products(place, crossing0, rest0, f0, r0, h0, s0)
     self_vis = self_tiles(place, crossing0, rest0, crossing1, rest1)
     f1, self_vis, early = lax.optimization_barrier((f1, self_vis, early))

time: 139 us -> 138 us (level)
  waiting for transfers between devices: 72.3 us -> 70.2 us
    ppermute x1, waiting for transfers between devices: 5.61 us -> 4.04 us  [on_device(): r1 = lax.ppermute(rest1, 'narrow', NEXT)]
    ppermute x2, starting transfers between devices: 0.01 us -> 1.57 us  [swap(): return lax.ppermute(f, 'narrow', SWAPPED)]
where the time goes in v10:
time: 138 us; the launch traced here: 137 us
  waiting for transfers between devices  70.2 us (51%)
  Pallas kernels  32.8 us (24%)
  starting transfers between devices  29.2 us (21%)
  local copies, waits for them, and re-layouts  4.12 us (3%)
    all_to_all x1, waiting for transfers between devices, on_device(): lax.all_to_all(early, ('side', 'plane'), split_axis=0, concat_axis=0, til...  23.3 us
    ppermute x1, waiting for transfers between devices, on_device(): late = merge(place, stay, lax.ppermute(leave, 'side', [(0, 1), (1, 0)]))  18.7 us
    ppermute x1, waiting for transfers between devices, on_device(): f0 = lax.ppermute(crossing0, 'narrow', CROSSED)  15.3 us
    all_to_all x1, starting transfers between devices, on_device(): lax.all_to_all(early, ('side', 'plane'), split_axis=0, concat_axis=0, til...  12.8 us
    pallas_call x2, Pallas kernels, filter_section(): pl.pallas_call(functools.partial(spectra_kernel, first, split), in_specs=...  11.6 us
    pallas_call x4, Pallas kernels, channel_rows(): pl.pallas_call(functools.partial(rows_kernel, crossing), in_specs=[SMALL,...  7.52 us
    all_to_all x1, waiting for transfers between devices, on_device(): lax.all_to_all(late, 'plane', split_axis=0, concat_axis=0, tiled=True)  7.16 us
    all_to_all x1, starting transfers between devices, on_device(): lax.all_to_all(late, 'plane', split_axis=0, concat_axis=0, tiled=True)  6.71 us
  transfers between devices with their start and end apart: 11, of which 7 were waited for; matrix products, arithmetic and copies ran while one was open for 0% of the time, Pallas kernels for 15%

profile of v10, /device:TPU:24, one launch (start us, length us, event | category | flops | bytes accessed | tf_op | source)
XLA Modules:
  0.0 137.5 jit_solution(11212310479149975546)
XLA Ops:
  0.7 6.6 %filter_section.3 = bf16[64,32,512]{2,1,0:T(8,128)(2,1)} custom-call(s32[3]{0:T(128)S(1)} %pad_add_fusion.place_ref, bf16[4,396288]{1,0:T(4,128)(2,1)} %x_ref.3, bf16[1024,1024]{1,0:T(8,128)(2,1)} %constant.38.clone.table_ref, f32[4,1024]{1,0:T(4,128)} %taps_ref.3), custom_call_target="tpu_custom_call" | custom-call | tf_op jit(solution)/shard_map/filter_section/pallas_call | solution.py:107
  7.4 12.8 %all-to-all-start = ((bf16[64,32,512]{2,1,0:T(8,128)(2,1)}), bf16[64,32,512]{2,1,0:T(8,128)(2,1)S(1)}, u32[]{:S(2)}, u32[]{:S(2)}) async-start(bf16[64,32,512]{2,1,0:T(8,128)(2,1)} %filter_section.3), calls=%async_computation | async-start | bytes 4194304 | tf_op jit(solution)/shard_map/all_to_all | solution.py:320
  20.2 5.0 %filter_section.2 = (bf16[32,32,256]{2,1,0:T(8,128)(2,1)}, bf16[32,32,256]{2,1,0:T(8,128)(2,1)}) custom-call(s32[3]{0:T(128)S(1)} %pad_add_fusion.place_ref, bf16[4,396288]{1,0:T(4,128)(2,1)} %x_ref.3, bf16[1024,1024]{1,0:T(8,128)(2,1)} %constant.38.clone.table_ref, f32[4,1024]{1,0:T(4,128)} %taps_ref.3), custom_call_target="tpu_custom_call" | custom-call | tf_op jit(solution)/shard_map/filter_section/pallas_call | solution.py:107
  25.2 1.7 %collective-permute-start = (bf16[32,32,256]{2,1,0:T(8,128)(2,1)}, bf16[32,32,256]{2,1,0:T(8,128)(2,1)S(1)}, u32[]{:S(2)}, u32[]{:S(2)}) collective-permute-start(bf16[32,32,256]{2,1,0:T(8,128)(2,1)} %get-tuple-element.21), channel_id=1, source_target_pairs={{0,128},{128,0},{1,129},{129,1},{2,130},{130,2},{3,131},{131,3},{4... | collective-permute-start | bytes 1572872 | tf_op jit(solution)/shard_map/ppermute | solution.py:321
  26.8 18.7 %collective-permute-done.got_ref = bf16[32,32,256]{2,1,0:T(8,128)(2,1)S(1)} collective-permute-done((bf16[32,32,256]{2,1,0:T(8,128)(2,1)}, bf16[32,32,256]{2,1,0:T(8,128)(2,1)S(1)}, u32[]{:S(2)}, u32[]{:S(2)}) %collective-permute-start) | collective-permute-done | bytes 524320 | tf_op jit(solution)/shard_map/ppermute | solution.py:321
  45.6 1.0 copy-done.10
  46.6 1.6 %merge_sides.1 = bf16[32,2,32,256]{3,2,1,0:T(8,128)(2,1)} custom-call(s32[3]{0:T(128)S(1)} %pad_add_fusion.place_ref, bf16[32,32,256]{2,1,0:T(8,128)(2,1)S(1)} %copy-done.10, bf16[32,32,256]{2,1,0:T(8,128)(2,1)S(1)} %collective-permute-done.got_ref), custom_call_target="tpu_custom_call" | custom-call | tf_op jit(solution)/shard_map/merge_sides/pallas_call | solution.py:140
  48.2 23.3 %all-to-all-done.source_ref = bf16[64,32,512]{2,1,0:T(8,128)(2,1)S(1)} async-done(((bf16[64,32,512]{2,1,0:T(8,128)(2,1)}), bf16[64,32,512]{2,1,0:T(8,128)(2,1)S(1)}, u32[]{:S(2)}, u32[]{:S(2)}) %all-to-all-start) | async-done | bytes 2097184 | tf_op jit(solution)/shard_map/all_to_all | solution.py:320
  71.6 2.0 %channel_rows.4.crossing0_ref.crossing_ref = bf16[8,128,512]{2,1,0:T(8,128)(2,1)} custom-call(s32[3]{0:T(128)S(1)} %pad_add_fusion.place_ref, bf16[256,256]{1,0:T(8,128)(2,1)S(1)} %copy-done.7, bf16[64,32,512]{2,1,0:T(8,128)(2,1)S(1)} %all-to-all-done.source_ref), custom_call_target="tpu_custom_call" | custom-call | tf_op jit(solution)/shard_map/channel_rows/pallas_call | solution.py:169
  73.9 6.7 %all-to-all-start.1 = ((bf16[32,2,32,256]{3,2,1,0:T(8,128)(2,1)}), bf16[32,2,32,256]{3,2,1,0:T(8,128)(2,1)S(1)}, u32[]{:S(2)}, u32[]{:S(2)}) async-start(bf16[32,2,32,256]{3,2,1,0:T(8,128)(2,1)} %merge_sides.1), calls=%async_computation.1 | async-start | bytes 2097152 | tf_op jit(solution)/shard_map/all_to_all | solution.py:323
  80.6 2.0 %channel_rows.5.rest0_ref.rest_ref = bf16[8,128,512]{2,1,0:T(8,128)(2,1)} custom-call(s32[3]{0:T(128)S(1)} %pad_add_fusion.place_ref, bf16[256,256]{1,0:T(8,128)(2,1)S(1)} %copy-done.7, bf16[64,32,512]{2,1,0:T(8,128)(2,1)S(1)} %all-to-all-done.source_ref), custom_call_target="tpu_custom_call" | custom-call | tf_op jit(solution)/shard_map/channel_rows/pallas_call | solution.py:169
  82.7 2.8 %collective-permute-start.2 = (bf16[8,128,512]{2,1,0:T(8,128)(2,1)S(1)}, bf16[8,128,512]{2,1,0:T(8,128)(2,1)S(1)}, u32[]{:S(2)}, u32[]{:S(2)}) collective-permute-start(bf16[8,128,512]{2,1,0:T(8,128)(2,1)S(1)} %copy-done), channel_id=1, source_target_pairs={{0,1},{2,3},{4,5},{6,7},{8,9},{10,11},{12,13},{14,15},{16,17},{18,... | collective-permute-start | bytes 3145736 | tf_op jit(solution)/shard_map/ppermute | solution.py:328
  85.5 15.3 %collective-permute-done.1.f_ref = bf16[8,128,512]{2,1,0:T(8,128)(2,1)} collective-permute-done((bf16[8,128,512]{2,1,0:T(8,128)(2,1)}, bf16[8,128,512]{2,1,0:T(8,128)(2,1)}, u32[]{:S(2)}, u32[]{:S(2)}) %collective-permute-start.1) | collective-permute-done | bytes 1048608 | tf_op jit(solution)/shard_map/ppermute | solution.py:325
  102.2 7.2 %all-to-all-done.1.source_ref = bf16[32,2,32,256]{3,2,1,0:T(8,128)(2,1)S(1)} async-done(((bf16[32,2,32,256]{3,2,1,0:T(8,128)(2,1)}), bf16[32,2,32,256]{3,2,1,0:T(8,128)(2,1)S(1)}, u32[]{:S(2)}, u32[]{:S(2)}) %all-to-all-start.1) | async-done | bytes 1048608 | tf_op jit(solution)/shard_map/all_to_all | solution.py:323
  109.4 1.7 %channel_rows.6.crossing1_ref.crossing_ref = bf16[8,128,256]{2,1,0:T(8,128)(2,1)} custom-call(s32[3]{0:T(128)S(1)} %pad_add_fusion.place_ref, bf16[256,256]{1,0:T(8,128)(2,1)S(1)} %copy-done.7, bf16[32,2,32,256]{3,2,1,0:T(8,128)(2,1)S(1)} %all-to-all-done.1.source_ref), custom_call_target="tpu_custom_call" | custom-call | tf_op jit(solution)/shard_map/channel_rows/pallas_call | solution.py:169
  111.7 1.7 %channel_rows.7.rest1_ref.rest_ref = bf16[8,128,256]{2,1,0:T(8,128)(2,1)} custom-call(s32[3]{0:T(128)S(1)} %pad_add_fusion.place_ref, bf16[256,256]{1,0:T(8,128)(2,1)S(1)} %copy-done.7, bf16[32,2,32,256]{3,2,1,0:T(8,128)(2,1)S(1)} %all-to-all-done.1.source_ref), custom_call_target="tpu_custom_call" | custom-call | tf_op jit(solution)/shard_map/channel_rows/pallas_call | solution.py:169
  113.4 2.4 %collective-permute-start.7 = (bf16[8,128,256]{2,1,0:T(8,128)(2,1)}, bf16[8,128,256]{2,1,0:T(8,128)(2,1)S(1)}, u32[]{:S(2)}, u32[]{:S(2)}) collective-permute-start(bf16[8,128,256]{2,1,0:T(8,128)(2,1)} %channel_rows.6.crossing1_ref.crossing_ref), channel_id=1, source_target_pairs={{0,1},{2,3},{4,5},{6,7},{8,9},{10,11},{12,13},{14,15},{16,17},{18,... | collective-permute-start | bytes 1572872 | tf_op jit(solution)/shard_map/ppermute | solution.py:336
  115.8 1.4 %collective-permute-done.5.r_ref = bf16[8,128,512]{2,1,0:T(8,128)(2,1)} collective-permute-done((bf16[8,128,512]{2,1,0:T(8,128)(2,1)}, bf16[8,128,512]{2,1,0:T(8,128)(2,1)}, u32[]{:S(2)}, u32[]{:S(2)}) %collective-permute-start.5) | collective-permute-done | bytes 1048608 | tf_op jit(solution)/shard_map/ppermute | solution.py:327
  118.3 1.0 copy-done.5
  119.3 3.8 %self_tiles.1 = f32[2,8,256,256]{3,2,1,0:T(8,128)} custom-call(s32[3]{0:T(128)S(1)} %pad_add_fusion.place_ref, bf16[8,128,512]{2,1,0:T(8,128)(2,1)S(1)} %copy-done.1, bf16[8,128,512]{2,1,0:T(8,128)(2,1)S(1)} %copy-done.2, bf16[8,128,256]{2,1,0:T(8,128)(2,1)S(1)} %copy-done.3, bf16[8,128,256]{2,1,0:T(8,128)(2,1)S(1)} %copy-done.5), custom_call_target="tpu_custom_call" | custom-call | tf_op jit(solution)/shard_map/self_tiles/pallas_call | solution.py:218
  123.2 4.6 %early_products.1.early_ref = f32[8,512,384]{2,1,0:T(8,128)S(1)} custom-call(s32[3]{0:T(128)S(1)} %pad_add_fusion.place_ref, bf16[8,128,512]{2,1,0:T(8,128)(2,1)S(1)} %copy-done.1, bf16[8,128,512]{2,1,0:T(8,128)(2,1)S(1)} %copy-done.2, bf16[8,128,512]{2,1,0:T(8,128)(2,1)} %collective-permute-done.1.f_ref, bf16[8,128,512]{2,1,0:T(8,128)(2,1)} %collective-permute-done.5.r_ref, ...), custom_call_target="tpu_custom_call" | custom-call | tf_op jit(solution)/shard_map/early_products/pallas_call | solution.py:254
  127.9 1.6 %collective-permute-start.8 = (bf16[8,128,256]{2,1,0:T(8,128)(2,1)S(1)}, bf16[8,128,256]{2,1,0:T(8,128)(2,1)S(1)}, u32[]{:S(2)}, u32[]{:S(2)}) collective-permute-start(bf16[8,128,256]{2,1,0:T(8,128)(2,1)S(1)} %collective-permute-done.4.f_ref), channel_id=1, source_target_pairs={{0,1},{1,0},{2,3},{3,2},{4,5},{5,4},{6,7},{7,6},{8,9},{9,8},{10,11... | collective-permute-start | bytes 1572872 | tf_op jit(solution)/shard_map/ppermute | solution.py:316
  129.5 4.0 %collective-permute-done.6.r_ref = bf16[8,128,256]{2,1,0:T(8,128)(2,1)S(1)} collective-permute-done((bf16[8,128,256]{2,1,0:T(8,128)(2,1)}, bf16[8,128,256]{2,1,0:T(8,128)(2,1)S(1)}, u32[]{:S(2)}, u32[]{:S(2)}) %collective-permute-start.6) | collective-permute-done | bytes 524320 | tf_op jit(solution)/shard_map/ppermute | solution.py:335
  133.6 3.8 %cross_tiles.1 = (f32[2,8,256,256]{3,2,1,0:T(8,128)}, f32[2,8,256,128]{3,2,1,0:T(8,128)}) custom-call(s32[3]{0:T(128)S(1)} %pad_add_fusion.place_ref, f32[8,512,384]{2,1,0:T(8,128)S(1)} %early_products.1.early_ref, bf16[8,128,256]{2,1,0:T(8,128)(2,1)S(1)} %copy-done.4, bf16[8,128,256]{2,1,0:T(8,128)(2,1)S(1)} %copy-done.6, ...), custom_call_target="tpu_custom_call" | custom-call | tf_op jit(solution)/shard_map/cross_tiles/pallas_call | solution.py:287
  (31 shorter events, 3.6 us)
Async XLA Ops:
  7.4 64.2 %all-to-all-start = ((bf16[64,32,512]{2,1,0:T(8,128)(2,1)}), bf16[64,32,512]{2,1,0:T(8,128)(2,1)S(1)}, u32[]{:S(2)}, u32[]{:S(2)}) async-start(bf16[64,32,512]{2,1,0:T(8,128)(2,1)} %filter_section.3), calls=%async_computation | async-start | bytes 4194304 | tf_op jit(solution)/shard_map/all_to_all | solution.py:320
  20.2 51.4 %copy-start.7 = (bf16[256,256]{1,0:T(8,128)(2,1)S(1)}, bf16[256,256]{1,0:T(8,128)(2,1)}, u32[]{:S(2)}) copy-start(bf16[256,256]{1,0:T(8,128)(2,1)} %constant.39.clone.order_ref) | copy-start | bytes 393220
  25.2 20.4 %collective-permute-start = (bf16[32,32,256]{2,1,0:T(8,128)(2,1)}, bf16[32,32,256]{2,1,0:T(8,128)(2,1)S(1)}, u32[]{:S(2)}, u32[]{:S(2)}) collective-permute-start(bf16[32,32,256]{2,1,0:T(8,128)(2,1)} %get-tuple-element.21), channel_id=1, source_target_pairs={{0,128},{128,0},{1,129},{129,1},{2,130},{130,2},{3,131},{131,3},{4... | collective-permute-start | bytes 1572872 | tf_op jit(solution)/shard_map/ppermute | solution.py:321
  45.6 1.0 copy-start.10
  73.6 27.1 %collective-permute-start.1 = (bf16[8,128,512]{2,1,0:T(8,128)(2,1)}, bf16[8,128,512]{2,1,0:T(8,128)(2,1)}, u32[]{:S(2)}, u32[]{:S(2)}) collective-permute-start(bf16[8,128,512]{2,1,0:T(8,128)(2,1)} %channel_rows.4.crossing0_ref.crossing_ref), channel_id=1, source_target_pairs={{0,3},{1,2},{2,1},{3,0},{4,7},{5,6},{6,5},{7,4},{8,11},{9,10},{10,... | collective-permute-start | bytes 3145736 | tf_op jit(solution)/shard_map/ppermute | solution.py:325
  73.9 35.5 %all-to-all-start.1 = ((bf16[32,2,32,256]{3,2,1,0:T(8,128)(2,1)}), bf16[32,2,32,256]{3,2,1,0:T(8,128)(2,1)S(1)}, u32[]{:S(2)}, u32[]{:S(2)}) async-start(bf16[32,2,32,256]{3,2,1,0:T(8,128)(2,1)} %merge_sides.1), calls=%async_computation.1 | async-start | bytes 2097152 | tf_op jit(solution)/shard_map/all_to_all | solution.py:323
  80.6 2.1 %copy-start = (bf16[8,128,512]{2,1,0:T(8,128)(2,1)S(1)}, bf16[8,128,512]{2,1,0:T(8,128)(2,1)}, u32[]{:S(2)}) copy-start(bf16[8,128,512]{2,1,0:T(8,128)(2,1)} %channel_rows.4.crossing0_ref.crossing_ref) | copy-start | bytes 3145732
  82.7 34.6 %copy-start.1 = (bf16[8,128,512]{2,1,0:T(8,128)(2,1)S(1)}, bf16[8,128,512]{2,1,0:T(8,128)(2,1)}, u32[]{:S(2)}) copy-start(bf16[8,128,512]{2,1,0:T(8,128)(2,1)} %channel_rows.4.crossing0_ref.crossing_ref) | copy-start | bytes 3145732
  82.7 34.6 %copy-start.2 = (bf16[8,128,512]{2,1,0:T(8,128)(2,1)S(1)}, bf16[8,128,512]{2,1,0:T(8,128)(2,1)}, u32[]{:S(2)}) copy-start(bf16[8,128,512]{2,1,0:T(8,128)(2,1)} %channel_rows.5.rest0_ref.rest_ref) | copy-start | bytes 3145732
  82.7 18.6 %collective-permute-start.2 = (bf16[8,128,512]{2,1,0:T(8,128)(2,1)S(1)}, bf16[8,128,512]{2,1,0:T(8,128)(2,1)S(1)}, u32[]{:S(2)}, u32[]{:S(2)}) collective-permute-start(bf16[8,128,512]{2,1,0:T(8,128)(2,1)S(1)} %copy-done), channel_id=1, source_target_pairs={{0,1},{2,3},{4,5},{6,7},{8,9},{10,11},{12,13},{14,15},{16,17},{18,... | collective-permute-start | bytes 3145736 | tf_op jit(solution)/shard_map/ppermute | solution.py:328
  100.8 8.6 %collective-permute-start.3 = (bf16[8,128,512]{2,1,0:T(8,128)(2,1)}, bf16[8,128,512]{2,1,0:T(8,128)(2,1)}, u32[]{:S(2)}, u32[]{:S(2)}) collective-permute-start(bf16[8,128,512]{2,1,0:T(8,128)(2,1)} %collective-permute-done.1.f_ref), channel_id=1, source_target_pairs={{0,1},{1,0},{2,3},{3,2},{4,5},{5,4},{6,7},{7,6},{8,9},{9,8},{10,11... | collective-permute-start | bytes 3145736 | tf_op jit(solution)/shard_map/ppermute | solution.py:316
  100.8 16.5 %collective-permute-start.5 = (bf16[8,128,512]{2,1,0:T(8,128)(2,1)}, bf16[8,128,512]{2,1,0:T(8,128)(2,1)}, u32[]{:S(2)}, u32[]{:S(2)}) collective-permute-start(bf16[8,128,512]{2,1,0:T(8,128)(2,1)} %channel_rows.5.rest0_ref.rest_ref), channel_id=1, source_target_pairs={{0,1},{1,2},{2,3},{3,0},{4,5},{5,6},{6,7},{7,4},{8,9},{9,10},{10,1... | collective-permute-start | bytes 3145736 | tf_op jit(solution)/shard_map/ppermute | solution.py:327
  101.3 1.0 copy-start.8
  111.1 16.8 %collective-permute-start.4 = (bf16[8,128,256]{2,1,0:T(8,128)(2,1)}, bf16[8,128,256]{2,1,0:T(8,128)(2,1)S(1)}, u32[]{:S(2)}, u32[]{:S(2)}) collective-permute-start(bf16[8,128,256]{2,1,0:T(8,128)(2,1)} %channel_rows.6.crossing1_ref.crossing_ref), channel_id=1, source_target_pairs={{0,3},{1,2},{2,1},{3,0},{4,7},{5,6},{6,5},{7,4},{8,11},{9,10},{10,... | collective-permute-start | bytes 1572872 | tf_op jit(solution)/shard_map/ppermute | solution.py:333
  111.7 11.4 %copy-start.9 = (bf16[8,128,512]{2,1,0:T(8,128)(2,1)S(1)}, bf16[8,128,512]{2,1,0:T(8,128)(2,1)}, u32[]{:S(2)}) copy-start(bf16[8,128,512]{2,1,0:T(8,128)(2,1)} %copy-done.8) | copy-start | bytes 3145732
  113.4 16.1 %collective-permute-start.7 = (bf16[8,128,256]{2,1,0:T(8,128)(2,1)}, bf16[8,128,256]{2,1,0:T(8,128)(2,1)S(1)}, u32[]{:S(2)}, u32[]{:S(2)}) collective-permute-start(bf16[8,128,256]{2,1,0:T(8,128)(2,1)} %channel_rows.6.crossing1_ref.crossing_ref), channel_id=1, source_target_pairs={{0,1},{2,3},{4,5},{6,7},{8,9},{10,11},{12,13},{14,15},{16,17},{18,... | collective-permute-start | bytes 1572872 | tf_op jit(solution)/shard_map/ppermute | solution.py:336
  117.2 16.3 %collective-permute-start.6 = (bf16[8,128,256]{2,1,0:T(8,128)(2,1)}, bf16[8,128,256]{2,1,0:T(8,128)(2,1)S(1)}, u32[]{:S(2)}, u32[]{:S(2)}) collective-permute-start(bf16[8,128,256]{2,1,0:T(8,128)(2,1)} %channel_rows.7.rest1_ref.rest_ref), channel_id=1, source_target_pairs={{0,1},{1,2},{2,3},{3,0},{4,5},{5,6},{6,7},{7,4},{8,9},{9,10},{10,1... | collective-permute-start | bytes 1572872 | tf_op jit(solution)/shard_map/ppermute | solution.py:335
  117.3 1.0 copy-start.3
  118.3 1.0 copy-start.5
  123.1 10.4 %copy-start.4 = (bf16[8,128,256]{2,1,0:T(8,128)(2,1)S(1)}, bf16[8,128,256]{2,1,0:T(8,128)(2,1)}, u32[]{:S(2)}) copy-start(bf16[8,128,256]{2,1,0:T(8,128)(2,1)} %channel_rows.6.crossing1_ref.crossing_ref) | copy-start | bytes 1572868
  123.2 10.4 %copy-start.6 = (bf16[8,128,256]{2,1,0:T(8,128)(2,1)S(1)}, bf16[8,128,256]{2,1,0:T(8,128)(2,1)}, u32[]{:S(2)}) copy-start(bf16[8,128,256]{2,1,0:T(8,128)(2,1)} %channel_rows.7.rest1_ref.rest_ref) | copy-start | bytes 1572868
  127.9 5.6 %collective-permute-start.8 = (bf16[8,128,256]{2,1,0:T(8,128)(2,1)S(1)}, bf16[8,128,256]{2,1,0:T(8,128)(2,1)S(1)}, u32[]{:S(2)}, u32[]{:S(2)}) collective-permute-start(bf16[8,128,256]{2,1,0:T(8,128)(2,1)S(1)} %collective-permute-done.4.f_ref), channel_id=1, source_target_pairs={{0,1},{1,0},{2,3},{3,2},{4,5},{5,4},{6,7},{7,6},{8,9},{9,8},{10,11... | collective-permute-start | bytes 1572872 | tf_op jit(solution)/shard_map/ppermute | solution.py:316
